TPU v7x, 32 devices: a whole 2x2x4 slice. The times are simulated.
32 devices in a mesh: section: 2 (over core), tensor: 4 (over z), dp: 4 (over y, x).
Axes of the slice: x: 2, y: 2, z: 4, core: 2. Of those that a mesh axis runs over, the one named last changes fastest.
Arguments:
- block_input: bfloat16 [2, 1024, 1024], P(None, ('dp', 'tensor')), may hold values from -6 to 6
- output_grad: bfloat16 [2, 1024, 1024], P(None, ('dp', 'tensor')), may hold values from -6 to 6
- valid_len: int32 [2], replicated, may hold values from 769 to 1024
- first_gain: bfloat16 [2, 1024], P('section'), may hold values from 0.5 to 1.5
- first_bias: bfloat16 [2, 1024], P('section'), may hold values from -1.1953125 to 1.1953125
- triple_weight: bfloat16 [2, 1024, 3, 1024], P('section', None, None, 'tensor'), may hold values from -0.1875 to 0.1875
- triple_bias: bfloat16 [2, 3, 1024], P('section', None, 'tensor'), may hold values from -1.1953125 to 1.1953125
- mixer_weight: bfloat16 [2, 1024, 1024], P('section', 'tensor'), may hold values from -1.5 to 1.5
- mixer_bias: bfloat16 [2, 1024], P('section'), may hold values from -1.1953125 to 1.1953125
- second_gain: bfloat16 [2, 1024], P('section'), may hold values from 0.5 to 1.5
- second_bias: bfloat16 [2, 1024], P('section'), may hold values from -1.1953125 to 1.1953125
- expand_weight: bfloat16 [2, 1024, 4096], P('section', None, 'tensor'), may hold values from -0.1875 to 0.1875
- expand_bias: bfloat16 [2, 4096], P('section', 'tensor'), may hold values from -3 to 3
- reduce_weight: bfloat16 [2, 4096, 1024], P('section', 'tensor'), may hold values from -0.09375 to 0.09375
- reduce_bias: bfloat16 [2, 1024], P('section'), may hold values from -1.1953125 to 1.1953125
- prefix_table: bfloat16 [10, 1024], replicated, may hold values from -6 to 6
- inner_weight: bfloat16 [1024, 512], replicated, may hold values from -0.1875 to 0.1875
- inner_bias: bfloat16 [512], replicated, may hold values from -3 to 3
- outer_weight: bfloat16 [512, 2, 2, 1024], P(None, 'section', None, 'tensor'), may hold values from -0.25 to 0.25
- outer_bias: bfloat16 [2, 2, 1024], P('section', None, 'tensor'), may hold values from -3 to 3
Outputs:
- layer_outputs: bfloat16 [2, 2, 1024, 1024], P('section', None, ('dp', 'tensor'))
- input_grads: bfloat16 [2, 2, 1024, 1024], P('section', None, ('dp', 'tensor'))
- prefix_states: bfloat16 [2, 2, 10, 1024], P('section', None, None, 'tensor')
- table_grad: float32 [10, 1024], replicated
- inner_weight_grad: float32 [1024, 512], replicated
- inner_bias_grad: float32 [512], replicated
- outer_weight_grad: float32 [512, 2, 2, 1024], P(None, 'section', None, 'tensor')
- outer_bias_grad: float32 [2, 2, 1024], P('section', None, 'tensor')
Inputs may be any that keep to these rules, and one draw needn't show every extreme that they name: Positions at or after valid_len of a micro-batch are padding and are never attended to as keys.
All inputs are finite; a program needn't handle non-finite values.
Results may differ from a plain program's by a relative error of at most 0.015.
Values may be sent and summed in bfloat16 or wider, within the bound.
A program may use at most 128 MiB of HBM per device.

v0:
```python
from functools import partial

import jax
import jax.numpy as jnp
from jax import lax
from jax.sharding import PartitionSpec as P

HD = 64


epsilon = 1e-05
masked_score = -1e30
highest = lax.Precision.HIGHEST


def passed_along(block, axis, distance):
    devices = range(lax.axis_size(axis))
    route = [(i - distance, i) for i in devices if i - distance in devices]
    return lax.ppermute(block, axis, route)


def layer_norm(values, norm_gain, norm_bias):
    center = values - jnp.mean(values, axis=-1, keepdims=True)
    variance = jnp.mean(center * center, axis=-1, keepdims=True)
    inverse = lax.rsqrt(variance + epsilon)
    normed = center * inverse
    return (normed * norm_gain + norm_bias, normed, inverse)


def norm_back(grad_out, normed, inverse, norm_gain):
    scaled = grad_out * norm_gain
    mean_grad = jnp.mean(scaled, axis=-1, keepdims=True)
    mean_cross = jnp.mean(scaled * normed, axis=-1, keepdims=True)
    return inverse * (scaled - mean_grad - normed * mean_cross)


def attention_scores(queries, seq_keys, pre_keys, valid, query_start):
    score_scale = HD ** (-0.5)
    seq_scores = (
        jnp.einsum("qhd,khd->hqk", queries, seq_keys, preferred_element_type=jnp.float32)
        * score_scale
    )
    pre_scores = (
        jnp.einsum("qhd,khd->hqk", queries, pre_keys, preferred_element_type=jnp.float32)
        * score_scale
    )
    query_pos = query_start + lax.broadcasted_iota(jnp.int32, (queries.shape[0], 1), 0)
    key_pos = lax.broadcasted_iota(jnp.int32, (1, seq_keys.shape[0]), 1)
    visible = (key_pos <= query_pos) & (key_pos < valid)
    seq_scores = jnp.where(visible[None], seq_scores, masked_score)
    return (seq_scores, pre_scores)


def split_prefix(prefix_full, local_width):
    local_heads = local_width // HD
    pre_keys = prefix_full[:, :local_width].reshape(-1, local_heads, HD)
    pre_values = prefix_full[:, local_width:].reshape(-1, local_heads, HD)
    return (pre_keys, pre_values)


def layer_forward(inputs, weights, prefix_full, valid, query_start):
    (
        gain_one,
        bias_one,
        triple_weight,
        triple_bias,
        mixer_weight,
        mixer_bias,
        gain_two,
        bias_two,
        expand_weight,
        expand_bias,
        reduce_weight,
        reduce_bias,
    ) = weights
    local_width = triple_weight.shape[1] // 3
    local_heads = local_width // HD
    normed_one, unit_one, inverse_one = layer_norm(inputs, gain_one, bias_one)
    mixed_rows = (
        jnp.dot(
            lax.all_gather(normed_one.astype(jnp.bfloat16), "tensor", axis=0, tiled=True),
            triple_weight,
            preferred_element_type=jnp.float32,
        )
        + triple_bias
    ).astype(jnp.bfloat16)
    tokens = mixed_rows.shape[0]
    queries = mixed_rows[:, :local_width].reshape(tokens, local_heads, HD)
    seq_keys, seq_values = (
        lax.all_gather(mixed_rows[:, local_width : 2 * local_width], "dp", axis=0, tiled=True),
        lax.all_gather(mixed_rows[:, 2 * local_width :], "dp", axis=0, tiled=True),
    )
    seq_keys = seq_keys.reshape(-1, local_heads, HD)
    seq_values = seq_values.reshape(-1, local_heads, HD)
    pre_keys, pre_values = split_prefix(prefix_full, local_width)
    seq_scores, pre_scores = attention_scores(queries, seq_keys, pre_keys, valid, query_start)
    row_max = jnp.maximum(
        jnp.max(seq_scores, axis=2, keepdims=True), jnp.max(pre_scores, axis=2, keepdims=True)
    )
    seq_exp = jnp.exp(seq_scores - row_max)
    pre_exp = jnp.exp(pre_scores - row_max)
    row_total = jnp.sum(seq_exp, axis=2, keepdims=True) + jnp.sum(pre_exp, axis=2, keepdims=True)
    log_total = row_max + jnp.log(row_total)
    seq_low = (seq_exp / row_total).astype(jnp.bfloat16)
    pre_low = (pre_exp / row_total).astype(jnp.bfloat16)
    attended = jnp.einsum("hqk,khd->qhd", seq_low, seq_values, preferred_element_type=jnp.float32)
    attended = attended + jnp.einsum(
        "hqk,khd->qhd", pre_low, pre_values, preferred_element_type=jnp.float32
    )
    attended = attended.astype(jnp.bfloat16).reshape(tokens, local_width)
    mixer_out = lax.psum_scatter(
        jnp.dot(attended, mixer_weight, preferred_element_type=jnp.float32),
        "tensor",
        scatter_dimension=0,
        tiled=True,
    )
    residual = inputs + mixer_out + mixer_bias
    normed_two, unit_two, inverse_two = layer_norm(residual, gain_two, bias_two)
    hidden_pre = (
        jnp.dot(
            lax.all_gather(normed_two.astype(jnp.bfloat16), "tensor", axis=0, tiled=True),
            expand_weight,
            preferred_element_type=jnp.float32,
        )
        + expand_bias
    )
    active = jax.nn.gelu(hidden_pre, approximate=True).astype(jnp.bfloat16)
    result = (
        residual
        + lax.psum_scatter(
            jnp.dot(active, reduce_weight, preferred_element_type=jnp.float32),
            "tensor",
            scatter_dimension=0,
            tiled=True,
        )
        + reduce_bias
    )
    saved_state = (
        unit_one,
        inverse_one,
        queries,
        seq_keys,
        seq_values,
        log_total,
        unit_two,
        inverse_two,
        hidden_pre,
    )
    return (result, saved_state)


def layer_backward(grad_out, saved_state, weights, prefix_full, valid, query_start):
    (
        gain_one,
        bias_one,
        triple_weight,
        triple_bias,
        mixer_weight,
        mixer_bias,
        gain_two,
        bias_two,
        expand_weight,
        expand_bias,
        reduce_weight,
        reduce_bias,
    ) = weights
    (
        unit_one,
        inverse_one,
        queries,
        seq_keys,
        seq_values,
        log_total,
        unit_two,
        inverse_two,
        hidden_pre,
    ) = saved_state
    tokens = queries.shape[0]
    local_heads = queries.shape[1]
    local_width = local_heads * HD
    score_scale = HD ** (-0.5)
    grad_active = jnp.dot(
        lax.all_gather(grad_out.astype(jnp.bfloat16), "tensor", axis=0, tiled=True),
        reduce_weight.T,
        preferred_element_type=jnp.float32,
    )
    gelu_pull = jax.vjp(partial(jax.nn.gelu, approximate=True), hidden_pre)[1]
    grad_pre = gelu_pull(grad_active)[0].astype(jnp.bfloat16)
    grad_two = lax.psum_scatter(
        jnp.dot(grad_pre, expand_weight.T, preferred_element_type=jnp.float32),
        "tensor",
        scatter_dimension=0,
        tiled=True,
    )
    grad_residual = grad_out + norm_back(grad_two, unit_two, inverse_two, gain_two)
    grad_heads = jnp.dot(
        lax.all_gather(grad_residual.astype(jnp.bfloat16), "tensor", axis=0, tiled=True),
        mixer_weight.T,
        preferred_element_type=jnp.float32,
    ).astype(jnp.bfloat16)
    grad_heads = grad_heads.reshape(tokens, local_heads, HD)
    pre_keys, pre_values = split_prefix(prefix_full, local_width)
    seq_scores, pre_scores = attention_scores(queries, seq_keys, pre_keys, valid, query_start)
    seq_prob = jnp.exp(seq_scores - log_total)
    pre_prob = jnp.exp(pre_scores - log_total)
    seq_dprob = jnp.einsum(
        "qhd,khd->hqk", grad_heads, seq_values, preferred_element_type=jnp.float32
    )
    pre_dprob = jnp.einsum(
        "qhd,khd->hqk", grad_heads, pre_values, preferred_element_type=jnp.float32
    )
    delta_row = jnp.sum(seq_prob * seq_dprob, axis=2, keepdims=True) + jnp.sum(
        pre_prob * pre_dprob, axis=2, keepdims=True
    )
    seq_dscore = (seq_prob * (seq_dprob - delta_row)).astype(jnp.bfloat16)
    pre_dscore = (pre_prob * (pre_dprob - delta_row)).astype(jnp.bfloat16)
    seq_low = seq_prob.astype(jnp.bfloat16)
    pre_low = pre_prob.astype(jnp.bfloat16)
    grad_queries = jnp.einsum(
        "hqk,khd->qhd", seq_dscore, seq_keys, preferred_element_type=jnp.float32
    )
    grad_queries = (
        grad_queries
        + jnp.einsum("hqk,khd->qhd", pre_dscore, pre_keys, preferred_element_type=jnp.float32)
    ) * score_scale
    key_term = (
        jnp.einsum("hqk,qhd->khd", seq_dscore, queries, preferred_element_type=jnp.float32)
        * score_scale
    )
    value_term = jnp.einsum("hqk,qhd->khd", seq_low, grad_heads, preferred_element_type=jnp.float32)
    grad_keys, grad_values = (
        lax.psum_scatter(key_term.reshape(-1, local_width), "dp", scatter_dimension=0, tiled=True),
        lax.psum_scatter(
            value_term.reshape(-1, local_width), "dp", scatter_dimension=0, tiled=True
        ),
    )
    pre_key_grad = (
        jnp.einsum("hqk,qhd->khd", pre_dscore, queries, preferred_element_type=jnp.float32)
        * score_scale
    )
    pre_value_grad = jnp.einsum(
        "hqk,qhd->khd", pre_low, grad_heads, preferred_element_type=jnp.float32
    )
    prefix_term = jnp.concatenate(
        [pre_key_grad.reshape(-1, local_width), pre_value_grad.reshape(-1, local_width)], axis=1
    )
    grad_mixed = jnp.concatenate(
        [grad_queries.reshape(tokens, local_width), grad_keys, grad_values], axis=1
    ).astype(jnp.bfloat16)
    grad_one = lax.psum_scatter(
        jnp.dot(grad_mixed, triple_weight.T, preferred_element_type=jnp.float32),
        "tensor",
        scatter_dimension=0,
        tiled=True,
    )
    grad_input = grad_residual + norm_back(grad_one, unit_one, inverse_one, gain_one)
    return (grad_input, prefix_term)


def shards(
    block_input,
    output_grad,
    valid_len,
    first_gain,
    first_bias,
    triple_weight,
    triple_bias,
    mixer_weight,
    mixer_bias,
    second_gain,
    second_bias,
    expand_weight,
    expand_bias,
    reduce_weight,
    reduce_bias,
    prefix_table,
    inner_weight,
    inner_bias,
    outer_weight,
    outer_bias,
):
    section_index = lax.axis_index("section")
    micro_count = block_input.shape[0]
    share_rows = block_input.shape[1]
    model_width = block_input.shape[2]
    local_width = triple_weight.shape[3]
    query_start = lax.axis_index("dp") * (share_rows * lax.axis_size("tensor"))
    weights = (
        first_gain[0],
        first_bias[0],
        triple_weight[0].reshape(-1, 3 * local_width),
        triple_bias[0].reshape(3 * local_width),
        mixer_weight[0],
        mixer_bias[0],
        second_gain[0],
        second_bias[0],
        expand_weight[0],
        expand_bias[0],
        reduce_weight[0],
        reduce_bias[0],
    )
    inner_pre = jnp.dot(prefix_table, inner_weight, preferred_element_type=jnp.float32) + inner_bias
    inner_act = jnp.tanh(inner_pre)
    inner_low = inner_act.astype(jnp.bfloat16)
    outer_local = outer_weight[:, 0].reshape(outer_weight.shape[0], 2 * local_width)
    prefix_full = (
        jnp.dot(inner_low, outer_local, preferred_element_type=jnp.float32)
        + outer_bias[0].reshape(2 * local_width)
    ).astype(jnp.bfloat16)
    moments = micro_count + 1
    carried = jnp.zeros((share_rows, model_width), jnp.bfloat16)
    results = []
    stored_states = []
    for moment in range(moments):
        micro_index = jnp.clip(moment - section_index, 0, micro_count - 1)
        inputs = jnp.where(
            section_index == 0, block_input[min(moment, micro_count - 1)], carried
        ).astype(jnp.float32)
        result, saved_state = layer_forward(
            inputs, weights, prefix_full, valid_len[micro_index], query_start
        )
        result_low = result.astype(jnp.bfloat16)
        results.append(result_low)
        stored_states.append(inputs)
        if moment + 1 < moments:
            carried = passed_along(result_low, "section", 1)
    grad_carried = jnp.zeros((share_rows, model_width), jnp.bfloat16)
    grad_list = []
    prefix_grad = jnp.zeros((prefix_full.shape[0], 2 * local_width), jnp.float32)
    for moment in range(moments):
        micro_index = moment - 1 + section_index
        valid_tick = (micro_index >= 0) & (micro_index < micro_count)
        clipped = jnp.clip(micro_index, 0, micro_count - 1)
        grad_in = jnp.where(
            section_index == 1, output_grad[min(moment, micro_count - 1)], grad_carried
        ).astype(jnp.float32)
        early_state = stored_states[max(moment - 1, 0)]
        late_state = stored_states[min(moment + 1, moments - 1)]
        picked = jnp.where(section_index == 0, early_state, late_state)
        picked_state = layer_forward(picked, weights, prefix_full, valid_len[clipped], query_start)[
            1
        ]
        grad_input, prefix_term = layer_backward(
            grad_in, picked_state, weights, prefix_full, valid_len[clipped], query_start
        )
        prefix_grad = prefix_grad + jnp.where(valid_tick, prefix_term, 0.0)
        grad_low = grad_input.astype(jnp.bfloat16)
        grad_list.append(grad_low)
        if moment + 1 < moments:
            grad_carried = passed_along(grad_low, "section", -1)
    layer_outputs = jnp.stack(
        [
            jnp.where(section_index == 0, results[number], results[number + 1])
            for number in range(micro_count)
        ]
    )[None]
    input_grads = jnp.stack(
        [
            jnp.where(section_index == 0, grad_list[number + 1], grad_list[number])
            for number in range(micro_count)
        ]
    )[None]
    prefix_total = lax.psum(prefix_grad, "dp")
    inner_float = inner_low.astype(jnp.float32)
    outer_float = outer_local.astype(jnp.float32)
    outer_weight_grad = jnp.dot(inner_float.T, prefix_total, precision=highest).reshape(
        -1, 1, 2, local_width
    )
    outer_bias_grad = jnp.sum(prefix_total, axis=0).reshape(1, 2, local_width)
    hidden_grad = lax.psum(
        jnp.dot(prefix_total, outer_float.T, precision=highest), ("section", "tensor")
    )
    inner_grad = hidden_grad * (1.0 - inner_act * inner_act)
    inner_weight_grad = jnp.dot(prefix_table.astype(jnp.float32).T, inner_grad, precision=highest)
    inner_bias_grad = jnp.sum(inner_grad, axis=0)
    table_grad = jnp.dot(inner_grad, inner_weight.astype(jnp.float32).T, precision=highest)
    prefix_states = prefix_full.reshape(-1, 2, local_width).transpose(1, 0, 2)[None]
    return (
        layer_outputs,
        input_grads,
        prefix_states,
        table_grad,
        inner_weight_grad,
        inner_bias_grad,
        outer_weight_grad,
        outer_bias_grad,
    )


def solution(mesh):
    return jax.shard_map(
        shards,
        mesh=mesh,
        in_specs=(
            P(None, ("dp", "tensor"), None),
            P(None, ("dp", "tensor"), None),
            P(),
            P("section", None),
            P("section", None),
            P("section", None, None, "tensor"),
            P("section", None, "tensor"),
            P("section", "tensor", None),
            P("section", None),
            P("section", None),
            P("section", None),
            P("section", None, "tensor"),
            P("section", "tensor"),
            P("section", "tensor", None),
            P("section", None),
            P(),
            P(),
            P(),
            P(None, "section", None, "tensor"),
            P("section", None, "tensor"),
        ),
        out_specs=(
            P("section", None, ("dp", "tensor"), None),
            P("section", None, ("dp", "tensor"), None),
            P("section", None, None, "tensor"),
            P(),
            P(),
            P(),
            P(None, "section", None, "tensor"),
            P("section", None, "tensor"),
        ),
        check_vma=False,
    )
```

profile of v0, /device:TPU:1, one launch (start us, length us, event | category | flops | bytes accessed | tf_op | source)
XLA Modules:
  0.0 1152.9 jit_solution(14280715155612601728)
XLA Ops:
  12.0 15.3 %all_gather.90 = bf16[256,1024]{1,0:T(8,128)(2,1)S(1)} all-gather(bf16[64,1024]{1,0:T(8,128)(2,1)S(1)} %fusion.266), channel_id=1, replica_groups=mesh['section'=2,'tensor'=4,'dp'=4] {'tensor'}, dimensions={0}, use_global_device_ids=true | all-gather | bytes 655360 | tf_op jit(solution)/shard_map/all_gather | solution.py:81
  32.6 8.9 all_gather.91
  70.9 33.0 %reduce-scatter.22.cloned.1.call-done = f32[64,1024]{1,0:T(8,128)} async-done(((f32[256,1024]{1,0:T(8,128)}), f32[64,1024]{1,0:T(8,128)}) %reduce-scatter.22.cloned.1.call-update) | async-done | bytes 262160 | tf_op jit(solution)/shard_map/reduce_scatter | solution.py:111
  107.2 12.8 %all_gather.93 = bf16[256,1024]{1,0:T(8,128)(2,1)} all-gather(bf16[64,1024]{1,0:T(8,128)(2,1)S(1)} %add_convert_fusion.14), channel_id=1, replica_groups=mesh['section'=2,'tensor'=4,'dp'=4] {'tensor'}, dimensions={0}, use_global_device_ids=true | all-gather | bytes 655360 | tf_op jit(solution)/shard_map/all_gather | solution.py:121
  124.5 29.5 %reduce-scatter.24.cloned.1.call-done = f32[64,1024]{1,0:T(8,128)} async-done(((f32[256,1024]{1,0:T(8,128)}), f32[64,1024]{1,0:T(8,128)}) %reduce-scatter.24.cloned.1.call-update) | async-done | bytes 262160 | tf_op jit(solution)/shard_map/reduce_scatter | solution.py:130
  158.8 13.1 %all_gather.94 = bf16[256,1024]{1,0:T(8,128)(2,1)S(1)} all-gather(bf16[64,1024]{1,0:T(8,128)(2,1)S(1)} %fusion.262), channel_id=1, replica_groups=mesh['section'=2,'tensor'=4,'dp'=4] {'tensor'}, dimensions={0}, use_global_device_ids=true | all-gather | bytes 655360 | tf_op jit(solution)/shard_map/all_gather | solution.py:81
  174.6 9.3 all_gather.95
  187.0 9.2 all_gather.96
  204.8 30.9 %reduce-scatter.26.cloned.1.call-done = f32[64,1024]{1,0:T(8,128)} async-done(((f32[256,1024]{1,0:T(8,128)}), f32[64,1024]{1,0:T(8,128)}) %reduce-scatter.26.cloned.1.call-update) | async-done | bytes 262160 | tf_op jit(solution)/shard_map/reduce_scatter | solution.py:111
  239.0 12.8 %all_gather.97 = bf16[256,1024]{1,0:T(8,128)(2,1)} all-gather(bf16[64,1024]{1,0:T(8,128)(2,1)S(1)} %add_convert_fusion.12), channel_id=1, replica_groups=mesh['section'=2,'tensor'=4,'dp'=4] {'tensor'}, dimensions={0}, use_global_device_ids=true | all-gather | bytes 655360 | tf_op jit(solution)/shard_map/all_gather | solution.py:121
  256.2 29.2 %reduce-scatter.28.cloned.1.call-done = f32[64,1024]{1,0:T(8,128)} async-done(((f32[256,1024]{1,0:T(8,128)}), f32[64,1024]{1,0:T(8,128)}) %reduce-scatter.28.cloned.1.call-update) | async-done | bytes 262160 | tf_op jit(solution)/shard_map/reduce_scatter | solution.py:130
  292.2 12.9 %all_gather.102 = bf16[256,1024]{1,0:T(8,128)(2,1)S(1)} all-gather(bf16[64,1024]{1,0:T(8,128)(2,1)S(1)} %get-tuple-element.100), channel_id=1, replica_groups=mesh['section'=2,'tensor'=4,'dp'=4] {'tensor'}, dimensions={0}, use_global_device_ids=true | all-gather | bytes 655360 | tf_op jit(solution)/shard_map/all_gather | solution.py:81
  307.8 9.3 all_gather.103
  320.3 8.9 all_gather.104
  338.4 11.9 %all_gather.98 = bf16[256,1024]{1,0:T(8,128)(2,1)S(1)} all-gather(bf16[64,1024]{1,0:T(8,128)(2,1)S(1)} %copy-done.60), channel_id=1, replica_groups=mesh['section'=2,'tensor'=4,'dp'=4] {'tensor'}, dimensions={0}, use_global_device_ids=true | all-gather | bytes 655360 | tf_op jit(solution)/shard_map/all_gather | solution.py:81
  353.0 8.6 all_gather.99
  364.7 9.0 all_gather.100
  384.2 12.7 %all-gather = bf16[1,256,1024]{2,1,0:T(8,128)(2,1)} all-gather(bf16[1,64,1024]{2,1,0:T(8,128)(2,1)S(1)} %slice_select_fusion), channel_id=2, replica_groups=mesh['section'=2,'tensor'=4,'dp'=4] {'tensor'}, dimensions={1}, use_global_device_ids=true | all-gather | bytes 655360 | tf_op jit(solution)/shard_map/all_gather | solution.py:183
  396.8 30.3 %reduce-scatter.30.cloned.1.call-done = f32[64,1024]{1,0:T(8,128)} async-done(((f32[256,1024]{1,0:T(8,128)}), f32[64,1024]{1,0:T(8,128)}) %reduce-scatter.30.cloned.1.call-update) | async-done | bytes 262160 | tf_op jit(solution)/shard_map/reduce_scatter | solution.py:111
  429.2 13.4 %all_gather.106 = bf16[256,1024]{1,0:T(8,128)(2,1)S(1)} all-gather(bf16[64,1024]{1,0:T(8,128)(2,1)S(1)} %add_convert_fusion.7), channel_id=1, replica_groups=mesh['section'=2,'tensor'=4,'dp'=4] {'tensor'}, dimensions={0}, use_global_device_ids=true | all-gather | bytes 655360 | tf_op jit(solution)/shard_map/all_gather | solution.py:121
  449.1 28.6 %reduce-scatter.36.cloned.1.call-done = f32[64,1024]{1,0:T(8,128)} async-done(((f32[256,1024]{1,0:T(8,128)}), f32[64,1024]{1,0:T(8,128)}) %reduce-scatter.36.cloned.1.call-update) | async-done | bytes 262160 | tf_op jit(solution)/shard_map/reduce_scatter | solution.py:189
  480.9 12.2 %all_gather.107 = bf16[256,1024]{1,0:T(8,128)(2,1)S(1)} all-gather(bf16[64,1024]{1,0:T(8,128)(2,1)S(1)} %get-tuple-element.61), channel_id=1, replica_groups=mesh['section'=2,'tensor'=4,'dp'=4] {'tensor'}, dimensions={0}, use_global_device_ids=true | all-gather | bytes 655360 | tf_op jit(solution)/shard_map/all_gather | solution.py:197
  510.8 17.0 %reduce-scatter.40.cloned.1.call-done = f32[256,256]{0,1:T(8,128)} async-done(((f32[1024,256]{0,1:T(8,128)}), f32[256,256]{0,1:T(8,128)}) %reduce-scatter.40.cloned.1.call-update) | async-done | bytes 262160 | tf_op jit(solution)/shard_map/reduce_scatter | solution.py:233
  529.4 29.0 %reduce-scatter.38.cloned.1.call-done = f32[256,256]{0,1:T(8,128)} async-done(((f32[1024,256]{0,1:T(8,128)}), f32[256,256]{0,1:T(8,128)}) %reduce-scatter.38.cloned.1.call-update) | async-done | bytes 262160 | tf_op jit(solution)/shard_map/reduce_scatter | solution.py:232
  566.4 23.3 %reduce-scatter.42.cloned.1.call-done = f32[64,1024]{1,0:T(8,128)} async-done(((f32[256,1024]{1,0:T(8,128)}), f32[64,1024]{1,0:T(8,128)}) %reduce-scatter.42.cloned.1.call-update) | async-done | bytes 262160 | tf_op jit(solution)/shard_map/reduce_scatter | solution.py:250
  593.6 12.1 %all_gather.114 = bf16[256,1024]{1,0:T(8,128)(2,1)S(1)} all-gather(bf16[64,1024]{1,0:T(8,128)(2,1)S(1)} %get-tuple-element.89), channel_id=1, replica_groups=mesh['section'=2,'tensor'=4,'dp'=4] {'tensor'}, dimensions={0}, use_global_device_ids=true | all-gather | bytes 655360 | tf_op jit(solution)/shard_map/all_gather | solution.py:81
  608.5 8.8 all_gather.115
  637.9 12.0 %all_gather.108 = bf16[256,1024]{1,0:T(8,128)(2,1)S(1)} all-gather(bf16[64,1024]{1,0:T(8,128)(2,1)S(1)} %copy-done.56), channel_id=1, replica_groups=mesh['section'=2,'tensor'=4,'dp'=4] {'tensor'}, dimensions={0}, use_global_device_ids=true | all-gather | bytes 655360 | tf_op jit(solution)/shard_map/all_gather | solution.py:81
  652.7 9.1 all_gather.109
  664.9 9.5 all_gather.110
  683.5 19.0 %collective-permute-start.2 = (bf16[64,1024]{1,0:T(8,128)(2,1)S(1)}, bf16[64,1024]{1,0:T(8,128)(2,1)S(1)}, u32[]{:S(2)}, u32[]{:S(2)}) collective-permute-start(bf16[64,1024]{1,0:T(8,128)(2,1)S(1)} %copy-done.63), channel_id=1, source_target_pairs={{16,0},{17,1},{18,2},{19,3},{20,4},{21,5},{22,6},{23,7},{24,8},{25... | collective-permute-start | bytes 393224 | tf_op jit(solution)/shard_map/ppermute | solution.py:19
  704.7 21.9 %all_gather.111 = bf16[256,1024]{1,0:T(8,128)(2,1)} all-gather(bf16[64,1024]{1,0:T(8,128)(2,1)S(1)} %bitcast_select_fusion.1), channel_id=1, replica_groups=mesh['section'=2,'tensor'=4,'dp'=4] {'tensor'}, dimensions={0}, use_global_device_ids=true | all-gather | bytes 655360 | tf_op jit(solution)/shard_map/all_gather | solution.py:183
  726.5 8.8 reduce-scatter.44.cloned.1.call-done
  739.6 12.5 %all_gather.112 = bf16[256,1024]{1,0:T(8,128)(2,1)S(1)} all-gather(bf16[64,1024]{1,0:T(8,128)(2,1)S(1)} %get-tuple-element.98), channel_id=1, replica_groups=mesh['section'=2,'tensor'=4,'dp'=4] {'tensor'}, dimensions={0}, use_global_device_ids=true | all-gather | bytes 655360 | tf_op jit(solution)/shard_map/all_gather | solution.py:121
  759.3 29.7 %reduce-scatter.46.cloned.1.call-done = f32[64,1024]{1,0:T(8,128)} async-done(((f32[256,1024]{1,0:T(8,128)}), f32[64,1024]{1,0:T(8,128)}) %reduce-scatter.46.cloned.1.call-update) | async-done | bytes 262160 | tf_op jit(solution)/shard_map/reduce_scatter | solution.py:189
  792.2 12.1 %all_gather.113 = bf16[256,1024]{1,0:T(8,128)(2,1)S(1)} all-gather(bf16[64,1024]{1,0:T(8,128)(2,1)S(1)} %get-tuple-element.53), channel_id=1, replica_groups=mesh['section'=2,'tensor'=4,'dp'=4] {'tensor'}, dimensions={0}, use_global_device_ids=true | all-gather | bytes 655360 | tf_op jit(solution)/shard_map/all_gather | solution.py:197
  823.6 16.1 %reduce-scatter.50.cloned.1.call-done = f32[256,256]{0,1:T(8,128)} async-done(((f32[1024,256]{0,1:T(8,128)}), f32[256,256]{0,1:T(8,128)}) %reduce-scatter.50.cloned.1.call-update) | async-done | bytes 262160 | tf_op jit(solution)/shard_map/reduce_scatter | solution.py:233
  841.3 28.9 %reduce-scatter.48.cloned.1.call-done = f32[256,256]{0,1:T(8,128)} async-done(((f32[1024,256]{0,1:T(8,128)}), f32[256,256]{0,1:T(8,128)}) %reduce-scatter.48.cloned.1.call-update) | async-done | bytes 262160 | tf_op jit(solution)/shard_map/reduce_scatter | solution.py:232
  874.4 19.4 %all_gather.118 = bf16[256,1024]{1,0:T(8,128)(2,1)} all-gather(bf16[64,1024]{1,0:T(8,128)(2,1)} %get-tuple-element.97), channel_id=1, replica_groups=mesh['section'=2,'tensor'=4,'dp'=4] {'tensor'}, dimensions={0}, use_global_device_ids=true | all-gather | bytes 655360 | tf_op jit(solution)/shard_map/all_gather | solution.py:121
  893.8 13.3 %reduce-scatter.52.cloned.1.call-done = f32[64,1024]{1,0:T(8,128)} async-done(((f32[256,1024]{1,0:T(8,128)}), f32[64,1024]{1,0:T(8,128)}) %reduce-scatter.52.cloned.1.call-update) | async-done | bytes 262160 | tf_op jit(solution)/shard_map/reduce_scatter | solution.py:250
  915.3 14.7 %all_gather.117 = bf16[256,1024]{1,0:T(8,128)(2,1)} all-gather(bf16[64,1024]{1,0:T(8,128)(2,1)S(1)} %bitcast_select_fusion), channel_id=1, replica_groups=mesh['section'=2,'tensor'=4,'dp'=4] {'tensor'}, dimensions={0}, use_global_device_ids=true | all-gather | bytes 655360 | tf_op jit(solution)/shard_map/all_gather | solution.py:183
  934.9 27.0 %reduce-scatter.56.cloned.1.call-done = f32[64,1024]{1,0:T(8,128)} async-done(((f32[256,1024]{1,0:T(8,128)}), f32[64,1024]{1,0:T(8,128)}) %reduce-scatter.56.cloned.1.call-update) | async-done | bytes 262160 | tf_op jit(solution)/shard_map/reduce_scatter | solution.py:189
  964.9 12.2 %all_gather.119 = bf16[256,1024]{1,0:T(8,128)(2,1)S(1)} all-gather(bf16[64,1024]{1,0:T(8,128)(2,1)S(1)} %get-tuple-element.47), channel_id=1, replica_groups=mesh['section'=2,'tensor'=4,'dp'=4] {'tensor'}, dimensions={0}, use_global_device_ids=true | all-gather | bytes 655360 | tf_op jit(solution)/shard_map/all_gather | solution.py:197
  993.6 18.2 %reduce-scatter.60.cloned.1.call-done = f32[256,256]{0,1:T(8,128)} async-done(((f32[1024,256]{0,1:T(8,128)}), f32[256,256]{0,1:T(8,128)}) %reduce-scatter.60.cloned.1.call-update) | async-done | bytes 262160 | tf_op jit(solution)/shard_map/reduce_scatter | solution.py:233
  1012.8 29.7 %reduce-scatter.58.cloned.1.call-done = f32[256,256]{0,1:T(8,128)} async-done(((f32[1024,256]{0,1:T(8,128)}), f32[256,256]{0,1:T(8,128)}) %reduce-scatter.58.cloned.1.call-update) | async-done | bytes 262160 | tf_op jit(solution)/shard_map/reduce_scatter | solution.py:232
  1049.6 20.8 %all_gather.101 = bf16[256,1024]{1,0:T(8,128)(2,1)} all-gather(bf16[64,1024]{1,0:T(8,128)(2,1)S(1)} %copy-done.55), channel_id=1, replica_groups=mesh['section'=2,'tensor'=4,'dp'=4] {'tensor'}, dimensions={0}, use_global_device_ids=true | all-gather | bytes 655360 | tf_op jit(solution)/shard_map/all_gather | solution.py:121
  1078.2 12.1 %psum.14 = f32[10,512]{1,0:T(8,128)S(1)} all-reduce(f32[10,512]{1,0:T(8,128)S(1)} %fusion.290), channel_id=1, replica_groups=mesh['section'=2,'tensor'=4,'dp'=4] {'dp'}, use_global_device_ids=true, to_apply=%region_87.88 | all-reduce | flops 5120 | bytes 40960 | tf_op jit(solution)/shard_map/psum | solution.py:363
  1090.7 34.9 %psum.15 = f32[10,512]{1,0:T(8,128)S(1)} all-reduce(f32[10,512]{1,0:T(8,128)S(1)} %fusion.400), channel_id=1, replica_groups=mesh['section'=2,'tensor'=4,'dp'=4] {'section','tensor'}, use_global_device_ids=true, to_apply=%region_88.89 | all-reduce | flops 5120 | bytes 40960 | tf_op jit(solution)/shard_map/psum | solution.py:370
  (550 shorter events, 302.2 us)
Async XLA Ops:
  7.2 112.9 %copy-start = (bf16[1,1024,1024]{2,1,0:T(8,128)(2,1)S(1)}, bf16[1,1024,1024]{2,1,0:T(8,128)(2,1)}, u32[]{:S(2)}) copy-start(bf16[1,1024,1024]{2,1,0:T(8,128)(2,1)} %param.31) | copy-start | bytes 6291460
  7.2 96.7 %reduce-scatter.22.cloned.1.call-start = ((), (), s32[]{:S(2)}) async-start(), calls=%async_computation.21 | async-start | bytes 1310720 | tf_op jit(solution)/shard_map/reduce_scatter | solution.py:111
  65.7 315.9 %copy-start.31 = (bf16[10,4,64]{2,1,0:T(4,128)(2,1)}, bf16[10,4,64]{2,1,0:T(4,128)(2,1)S(1)}, u32[]{:S(2)}) copy-start(bf16[10,4,64]{2,1,0:T(4,128)(2,1)S(1)} %reshape.749) | copy-start | bytes 15364
  65.8 38.1 %copy-start.8 = (bf16[2,64,1024]{2,1,0:T(8,128)(2,1)S(1)}, bf16[2,64,1024]{2,1,0:T(8,128)(2,1)}, u32[]{:S(2)}) copy-start(bf16[2,64,1024]{2,1,0:T(8,128)(2,1)} %param.20) | copy-start | bytes 786436
  70.7 83.3 %reduce-scatter.24.cloned.1.call-start = ((), (), s32[]{:S(2)}) async-start(), calls=%async_computation.22 | async-start | bytes 1310720 | tf_op jit(solution)/shard_map/reduce_scatter | solution.py:130
  70.8 358.4 %copy-start.81 = (f32[1,1024]{1,0:T(1,128)}, f32[1,1024]{1,0:T(1,128)S(1)}, u32[]{:S(2)}) copy-start(f32[1,1024]{1,0:T(1,128)S(1)} %add.783) | copy-start | bytes 12292
  70.8 408.2 %copy-start.53 = (f32[1,1024]{1,0:T(1,128)}, f32[1,1024]{1,0:T(1,128)S(1)}, u32[]{:S(2)}) copy-start(f32[1,1024]{1,0:T(1,128)S(1)} %mul.822) | copy-start | bytes 12292
  70.8 371.8 %copy-start.110 = (f32[1,1024]{1,0:T(1,128)}, f32[1,1024]{1,0:T(1,128)S(1)}, u32[]{:S(2)}) copy-start(f32[1,1024]{1,0:T(1,128)S(1)} %add.784) | copy-start | bytes 12292
  120.1 33.9 %copy-start.19 = (f32[64,1024]{1,0:T(8,128)S(1)}, f32[64,1024]{1,0:T(8,128)}, u32[]{:S(2)}) copy-start(f32[64,1024]{1,0:T(8,128)} %reduce-scatter.22.cloned.1.call-done) | copy-start | bytes 786436
  120.1 38.6 %copy-start.69 = (f32[1,1024]{1,0:T(1,128)S(1)}, f32[1,1024]{1,0:T(1,128)}, u32[]{:S(2)}) copy-start(f32[1,1024]{1,0:T(1,128)} %copy-done.68) | copy-start | bytes 12292
  120.1 38.6 %copy-start.84 = (f32[1,1024]{1,0:T(1,128)S(1)}, f32[1,1024]{1,0:T(1,128)}, u32[]{:S(2)}) copy-start(f32[1,1024]{1,0:T(1,128)} %copy-done.83) | copy-start | bytes 12292
  120.1 51.8 %copy-start.103 = (f32[768]{0:T(1024)S(1)}, f32[768]{0:T(1024)}, u32[]{:S(2)}) copy-start(f32[768]{0:T(1024)} %copy-done.102) | copy-start | bytes 9220
  124.4 111.3 %reduce-scatter.26.cloned.1.call-start = ((), (), s32[]{:S(2)}) async-start(), calls=%async_computation.23 | async-start | bytes 1310720 | tf_op jit(solution)/shard_map/reduce_scatter | solution.py:111
  124.5 160.9 %copy-start.85 = (f32[1,1024]{1,0:T(1,128)}, f32[1,1024]{1,0:T(1,128)S(1)}, u32[]{:S(2)}) copy-start(f32[1,1024]{1,0:T(1,128)S(1)} %add.785) | copy-start | bytes 12292
  155.0 3.2 collective-permute-start
  158.8 39.6 %copy-start.36 = (pred[256,1024]{1,0:T(8,128)(4,1)S(1)}, pred[256,1024]{1,0:T(8,128)(4,1)}, u32[]{:S(2)}) copy-start(pred[256,1024]{1,0:T(8,128)(4,1)} %get-tuple-element.106) | copy-start | bytes 786436
  204.7 80.7 %reduce-scatter.28.cloned.1.call-start = ((), (), s32[]{:S(2)}) async-start(), calls=%async_computation.24 | async-start | bytes 1310720 | tf_op jit(solution)/shard_map/reduce_scatter | solution.py:130
  251.8 33.6 %copy-start.20 = (f32[64,1024]{1,0:T(8,128)S(1)}, f32[64,1024]{1,0:T(8,128)}, u32[]{:S(2)}) copy-start(f32[64,1024]{1,0:T(8,128)} %reduce-scatter.26.cloned.1.call-done) | copy-start | bytes 786436
  256.1 140.7 %reduce-scatter.34.cloned.1.call-start = ((), (), s32[]{:S(2)}) async-start(), calls=%async_computation.27 | async-start | bytes 1310720 | tf_op jit(solution)/shard_map/reduce_scatter | solution.py:111
  287.1 3.2 collective-permute-start.1
  291.2 40.0 %copy-start.91 = (f32[64]{0:T(128)}, f32[64]{0:T(128)S(1)}, u32[]{:S(2)}) copy-start(f32[64]{0:T(128)S(1)} %broadcast_multiply_fusion.17) | copy-start | bytes 772
  291.4 39.8 %copy-start.95 = (f32[64]{0:T(128)}, f32[64]{0:T(128)S(1)}, u32[]{:S(2)}) copy-start(f32[64]{0:T(128)S(1)} %add_rsqrt_fusion.5) | copy-start | bytes 772
  338.3 88.8 %reduce-scatter.30.cloned.1.call-start = ((), (), s32[]{:S(2)}) async-start(), calls=%async_computation.25 | async-start | bytes 1310720 | tf_op jit(solution)/shard_map/reduce_scatter | solution.py:111
  383.2 94.6 %reduce-scatter.36.cloned.1.call-start = ((), (), s32[]{:S(2)}) async-start(), calls=%async_computation.28 | async-start | bytes 1310720 | tf_op jit(solution)/shard_map/reduce_scatter | solution.py:189
  449.1 78.7 %reduce-scatter.40.cloned.1.call-start = ((), (), s32[]{:S(2)}) async-start(), calls=%async_computation.30 | async-start | bytes 1310720 | tf_op jit(solution)/shard_map/reduce_scatter | solution.py:233
  497.5 61.0 %reduce-scatter.38.cloned.1.call-start = ((), (), s32[]{:S(2)}) async-start(), calls=%async_computation.29 | async-start | bytes 1310720 | tf_op jit(solution)/shard_map/reduce_scatter | solution.py:232
  505.8 83.9 %copy-start.17 = (f32[64,1024]{1,0:T(8,128)S(1)}, f32[64,1024]{1,0:T(8,128)}, u32[]{:S(2)}) copy-start(f32[64,1024]{1,0:T(8,128)} %reduce-scatter.30.cloned.1.call-done) | copy-start | bytes 786436
  505.8 83.9 %reduce-scatter.42.cloned.1.call-start = ((), (), s32[]{:S(2)}) async-start(), calls=%async_computation.31 | async-start | bytes 1310720 | tf_op jit(solution)/shard_map/reduce_scatter | solution.py:250
  562.6 163.9 %reduce-scatter.54.cloned.1.call-start = ((), (), s32[]{:S(2)}) async-start(), calls=%async_computation.37 | async-start | bytes 1310720 | tf_op jit(solution)/shard_map/reduce_scatter | solution.py:111
  637.8 97.5 %reduce-scatter.44.cloned.1.call-start = ((), (), s32[]{:S(2)}) async-start(), calls=%async_computation.32 | async-start | bytes 1310720 | tf_op jit(solution)/shard_map/reduce_scatter | solution.py:111
  683.5 105.5 %reduce-scatter.46.cloned.1.call-start = ((), (), s32[]{:S(2)}) async-start(), calls=%async_computation.33 | async-start | bytes 1310720 | tf_op jit(solution)/shard_map/reduce_scatter | solution.py:189
  683.5 20.2 %collective-permute-start.2 = (bf16[64,1024]{1,0:T(8,128)(2,1)S(1)}, bf16[64,1024]{1,0:T(8,128)(2,1)S(1)}, u32[]{:S(2)}, u32[]{:S(2)}) collective-permute-start(bf16[64,1024]{1,0:T(8,128)(2,1)S(1)} %copy-done.63), channel_id=1, source_target_pairs={{16,0},{17,1},{18,2},{19,3},{20,4},{21,5},{22,6},{23,7},{24,8},{25... | collective-permute-start | bytes 393224 | tf_op jit(solution)/shard_map/ppermute | solution.py:19
  759.3 80.4 %reduce-scatter.50.cloned.1.call-start = ((), (), s32[]{:S(2)}) async-start(), calls=%async_computation.35 | async-start | bytes 1310720 | tf_op jit(solution)/shard_map/reduce_scatter | solution.py:233
  809.3 60.8 %reduce-scatter.48.cloned.1.call-start = ((), (), s32[]{:S(2)}) async-start(), calls=%async_computation.34 | async-start | bytes 1310720 | tf_op jit(solution)/shard_map/reduce_scatter | solution.py:232
  818.6 88.5 %reduce-scatter.52.cloned.1.call-start = ((), (), s32[]{:S(2)}) async-start(), calls=%async_computation.36 | async-start | bytes 1310720 | tf_op jit(solution)/shard_map/reduce_scatter | solution.py:250
  874.3 87.5 %reduce-scatter.56.cloned.1.call-start = ((), (), s32[]{:S(2)}) async-start(), calls=%async_computation.38 | async-start | bytes 1310720 | tf_op jit(solution)/shard_map/reduce_scatter | solution.py:189
  910.3 5.0 collective-permute-start.3
  934.8 77.0 %reduce-scatter.60.cloned.1.call-start = ((), (), s32[]{:S(2)}) async-start(), calls=%async_computation.40 | async-start | bytes 1310720 | tf_op jit(solution)/shard_map/reduce_scatter | solution.py:233
  981.5 61.0 %reduce-scatter.58.cloned.1.call-start = ((), (), s32[]{:S(2)}) async-start(), calls=%async_computation.39 | async-start | bytes 1310720 | tf_op jit(solution)/shard_map/reduce_scatter | solution.py:232
  989.4 150.3 %reduce-scatter.62.cloned.1.call-start = ((), (), s32[]{:S(2)}) async-start(), calls=%async_computation.41 | async-start | bytes 1310720 | tf_op jit(solution)/shard_map/reduce_scatter | solution.py:250
  989.5 58.5 %copy-start.39 = (f32[4,256,10]{1,2,0:T(8,128)S(1)}, f32[4,256,10]{1,2,0:T(8,128)}, u32[]{:S(2)}) copy-start(f32[4,256,10]{1,2,0:T(8,128)} %copy-done.37) | copy-start | bytes 122884
  990.1 57.8 %copy-start.76 = (f32[4,256]{1,0:T(4,128)S(1)}, f32[4,256]{1,0:T(4,128)}, u32[]{:S(2)}) copy-start(f32[4,256]{1,0:T(4,128)} %get-tuple-element.59) | copy-start | bytes 12292
  990.4 58.4 %copy-start.25 = (bf16[256,256]{0,1:T(8,128)(2,1)S(1)}, bf16[256,256]{0,1:T(8,128)(2,1)}, u32[]{:S(2)}) copy-start(bf16[256,256]{0,1:T(8,128)(2,1)} %copy-done.23) | copy-start | bytes 393220
  990.4 58.4 %copy-start.72 = (bf16[4,256,10]{1,2,0:T(8,128)(2,1)S(1)}, bf16[4,256,10]{1,2,0:T(8,128)(2,1)}, u32[]{:S(2)}) copy-start(bf16[4,256,10]{1,2,0:T(8,128)(2,1)} %copy-done.71) | copy-start | bytes 61444
  990.4 80.0 %copy-start.111 = (f32[1,1024]{1,0:T(1,128)S(1)}, f32[1,1024]{1,0:T(1,128)}, u32[]{:S(2)}) copy-start(f32[1,1024]{1,0:T(1,128)} %copy-done.110) | copy-start | bytes 12292
  993.6 56.1 %copy-start.55 = (bf16[64,1024]{1,0:T(8,128)(2,1)S(1)}, bf16[64,1024]{1,0:T(8,128)(2,1)}, u32[]{:S(2)}) copy-start(bf16[64,1024]{1,0:T(8,128)(2,1)} %get-tuple-element.90) | copy-start | bytes 393220
  1046.5 95.4 %reduce-scatter.32.cloned.1.call-start = ((), (), s32[]{:S(2)}) async-start(), calls=%async_computation.26 | async-start | bytes 1310720 | tf_op jit(solution)/shard_map/reduce_scatter | solution.py:130
  1075.0 56.8 %copy-start.49 = (f32[10,512]{1,0:T(8,128)S(1)}, f32[10,512]{1,0:T(8,128)}, u32[]{:S(2)}) copy-start(f32[10,512]{1,0:T(8,128)} %copy-done.48) | copy-start | bytes 61444
  (93 other events, 790.6 us)
Sparse Core Ops, SparseCore 0:
  70.8 33.0 reduce-scatter.21
  124.5 29.4 reduce-scatter.23
  204.8 30.7 reduce-scatter.25
  256.3 29.0 reduce-scatter.27
  338.4 33.3 reduce-scatter.33
  383.3 43.7 reduce-scatter.29
  449.2 28.5 reduce-scatter.35
  497.6 30.1 reduce-scatter.39
  530.7 27.7 reduce-scatter.37
  562.7 26.9 reduce-scatter.41
  638.0 35.7 reduce-scatter.53
  683.6 51.7 reduce-scatter.43
  759.4 29.5 reduce-scatter.45
  809.5 30.2 reduce-scatter.49
  842.5 27.6 reduce-scatter.47
  874.4 32.6 reduce-scatter.51
  934.9 26.8 reduce-scatter.55
  981.6 30.1 reduce-scatter.59
  1014.7 27.7 reduce-scatter.57
  1046.7 33.5 reduce-scatter.61
  1082.6 27.6 reduce-scatter.31
where the time goes:
time: 1160 us; the launch traced here: 1150 us
  waiting for transfers between devices  427 us (37%)
  blocking collectives  408 us (35%)
  matrix products  142 us (12%)
  other arithmetic  80.8 us (7%)
  local copies, waits for them, and re-layouts  53.3 us (5%)
  starting transfers between devices  25.2 us (2%)
  between operations  16.7 us (1%)
    reduce_scatter x6, waiting for transfers between devices, layer_forward(): lax.psum_scatter(jnp.dot(attended, mixer_weight, preferred_element_type=j...  103 us
    all_gather x6, blocking collectives, layer_forward(): lax.all_gather(normed_two.astype(jnp.bfloat16), 'tensor', axis=0, tiled=T...  91.7 us
    reduce_scatter x3, waiting for transfers between devices, layer_backward(): lax.psum_scatter(key_term.reshape(-1, local_width), 'dp', scatter_dimensi...  87.6 us
    reduce_scatter x3, waiting for transfers between devices, layer_backward(): lax.psum_scatter(jnp.dot(grad_pre, expand_weight.T, preferred_element_typ...  85.3 us
    all_gather x6, blocking collectives, layer_forward(): lax.all_gather(normed_one.astype(jnp.bfloat16), 'tensor', axis=0, tiled=T...  77.3 us
    reduce_scatter x3, waiting for transfers between devices, layer_forward(): lax.psum_scatter(jnp.dot(active, reduce_weight, preferred_element_type=jn...  58.7 us
    all_gather x6, blocking collectives, layer_forward(): lax.all_gather(mixed_rows[:, 2 * local_width:], 'dp', axis=0, tiled=True)  54.1 us
    all_gather x6, blocking collectives, layer_forward(): lax.all_gather(mixed_rows[:, local_width:2 * local_width], 'dp', axis=0,...  52.2 us
  transfers between devices with their start and end apart: 25, of which 19 were waited for; matrix products, arithmetic and copies ran while one was open for 9% of the time, Pallas kernels for 0%

commit v1 on v0

--- a/solution.py
+++ b/solution.py
@@ -3,6 +3,8 @@
 import jax
 import jax.numpy as jnp
 from jax import lax
+from jax.experimental import pallas as pl
+from jax.experimental.pallas import tpu as pltpu
 from jax.sharding import PartitionSpec as P
 
 HD = 64
@@ -11,6 +13,9 @@
 epsilon = 1e-05
 masked_score = -1e30
 highest = lax.Precision.HIGHEST
+MESH = pl.DeviceIdType.MESH
+f32 = jnp.float32
+bf16 = jnp.bfloat16
 
 
 def passed_along(block, axis, distance):
@@ -361,8 +366,810 @@
         ]
     )[None]
     prefix_total = lax.psum(prefix_grad, "dp")
-    inner_float = inner_low.astype(jnp.float32)
-    outer_float = outer_local.astype(jnp.float32)
+    return (layer_outputs, input_grads) + prefix_back(
+        prefix_total,
+        prefix_full,
+        inner_act,
+        inner_low,
+        outer_local,
+        prefix_table,
+        inner_weight,
+        local_width,
+    )
+
+
+def dot_nn(left, right):
+    return lax.dot_general(left, right, (((1,), (0,)), ((), ())), preferred_element_type=f32)
+
+
+def dot_nt(left, right):
+    return lax.dot_general(left, right, (((1,), (1,)), ((), ())), preferred_element_type=f32)
+
+
+class Sizes:
+    def __init__(self, planes, blocks, rows, width, local_width, hidden, prefix_rows):
+        self.planes = planes
+        self.blocks = blocks
+        self.rows = rows
+        self.block_rows = rows * planes
+        self.width = width
+        self.local_width = local_width
+        self.hidden = hidden
+        self.prefix_rows = prefix_rows
+        self.cells = planes * blocks
+        self.tile = 256
+
+
+def both_layers(
+    z,
+    valid_ref,
+    x_in,
+    gy_in,
+    vec_in,
+    tbias_in,
+    triple_in,
+    mixer_in,
+    expand_in,
+    reduce_in,
+    prefix_in,
+    lo_out,
+    ig_out,
+    pg_out,
+    vec,
+    tbias,
+    triple_own,
+    wq,
+    wm,
+    we,
+    wr,
+    pre,
+    xs,
+    gys,
+    qkv_send,
+    qkv,
+    ot_send,
+    att,
+    y_send,
+    y_recv,
+    gh_send,
+    gh,
+    dm_send,
+    dm,
+    gi_send,
+    gi_recv,
+    z_one,
+    inv_one,
+    z_two,
+    inv_two,
+    gelu_grad,
+    probs,
+    probs_pre,
+    out_t,
+    keys_n,
+    normed,
+    wide,
+    total,
+    grad_res,
+    resid,
+    dkeys,
+    dvalues,
+    y_last,
+    gi_own,
+    pg,
+    pg_recv,
+    pg_sum,
+    pg_all,
+    send_sem,
+    recv_sem,
+    local_sem,
+):
+    s = lax.axis_index("section")
+    t = lax.axis_index("tensor")
+    d = lax.axis_index("dp")
+    nt, nb, rows, brows, tile = z.planes, z.blocks, z.rows, z.block_rows, z.tile
+    cells = z.cells
+    me = t * nb + d
+    sib = (1 - s, t, d)
+    counts = dict(send=0, recv=0, local=0)
+    pending = []
+
+    def claim(kind, number):
+        first = counts[kind]
+        counts[kind] += number
+        return first
+
+    def rcopy(src, dst, ss, rs, device):
+        return pltpu.make_async_remote_copy(
+            src_ref=src,
+            dst_ref=dst,
+            send_sem=send_sem.at[ss],
+            recv_sem=recv_sem.at[rs],
+            device_id=device,
+            device_id_type=MESH,
+        )
+
+    def push(src, dst, rs, device, when=None):
+        copy = rcopy(src, dst, claim("send", 1), rs, device)
+        if when is None:
+            copy.start()
+            pending.append((copy, None))
+        else:
+            pl.when(when)(copy.start)
+            pending.append((copy, when))
+
+    def arrived(dst, rs, when=None):
+        copy = rcopy(dst, dst, 0, rs, sib)
+        if when is None:
+            copy.wait_recv()
+        else:
+            pl.when(when)(copy.wait_recv)
+
+    def lcopy(src, dst):
+        copy = pltpu.make_async_copy(src, dst, local_sem.at[claim("local", 1)])
+        copy.start()
+        return copy
+
+    def plane(k):
+        return lax.rem(t + k, nt)
+
+    def block(k):
+        return lax.rem(d + k, nb)
+
+    barrier = pltpu.get_barrier_semaphore()
+    for k in range(1, cells):
+        pl.semaphore_signal(
+            barrier, inc=1, device_id=(s, plane(k // nb), block(k % nb)), device_id_type=MESH
+        )
+    pl.semaphore_signal(barrier, inc=1, device_id=sib, device_id_type=MESH)
+
+    load_x = lcopy(x_in.at[s], xs.at[0, t])
+    load_triple = lcopy(triple_in, triple_own)
+    load_vec = lcopy(vec_in, vec.at[s])
+    load_tbias = lcopy(tbias_in, tbias.at[s])
+    load_pre = lcopy(prefix_in, pre.at[s])
+    load_mixer = lcopy(mixer_in, wm.at[s, pl.ds(pl.multiple_of(t * z.local_width, 256), z.local_width)])
+    load_expand = lcopy(expand_in, we.at[s])
+    load_reduce = lcopy(reduce_in, wr.at[s])
+    load_gy = lcopy(gy_in.at[s], gys.at[1, t])
+
+    pl.semaphore_wait(barrier, cells)
+
+    def spread(src, buf, layer):
+        first = claim("recv", nt)
+        for k in range(1, nt):
+            push(src, buf.at[layer, t], first + k, (s, plane(k), d))
+        return first
+
+    def spread_wait(buf, layer, first, k):
+        arrived(buf.at[layer, plane(nt - k)], first + k)
+
+    x_first = [None, None]
+    gy_first = [None, None]
+    x_first[0] = spread(x_in.at[s], xs, 0)
+
+    small = claim("recv", 3)
+    push(vec_in, vec.at[s], small, sib)
+    push(tbias_in, tbias.at[s], small + 1, sib)
+    push(prefix_in, pre.at[s], small + 2, sib)
+
+    mix_first = [claim("recv", nt), claim("recv", nt)]
+    mix_second = [claim("recv", nt * nb), claim("recv", nt * nb)]
+    mix_third = [claim("recv", 1), claim("recv", 1)]
+
+    def piece(layer, p, q):
+        return wm.at[layer, pl.ds(pl.multiple_of((p * nb + q) * (z.local_width // nb), 64), z.local_width // nb)]
+
+    def mix_one(layer):
+        part = z.local_width // nb
+        for k in range(1, nt):
+            push(
+                mixer_in.at[pl.ds(pl.multiple_of(d * part, 64), part)],
+                piece(layer, t, d),
+                mix_first[layer] + k,
+                (s, plane(k), d),
+                s == layer,
+            )
+
+    def mix_two(layer):
+        for k in range(1, nt):
+            source = plane(nt - k)
+            arrived(piece(layer, source, d), mix_first[layer] + k, s == layer)
+            for q in range(1, nb):
+                push(
+                    piece(layer, source, d),
+                    piece(layer, source, d),
+                    mix_second[layer] + k * nb + q,
+                    (s, t, block(q)),
+                    s == layer,
+                )
+
+    def mix_three(layer):
+        for k in range(1, nt):
+            for q in range(1, nb):
+                arrived(
+                    piece(layer, plane(nt - k), block(nb - q)),
+                    mix_second[layer] + k * nb + q,
+                    s == layer,
+                )
+        push(wm.at[layer], wm.at[layer], mix_third[layer], sib, s == layer)
+
+    mix_one(0)
+
+    load_triple.wait()
+    for c in range(3):
+        for n in range(z.width // tile):
+            turned = triple_own[c, n * tile : (n + 1) * tile, :].T
+            for j in range(nb):
+                wq[s, j, c * HD : (c + 1) * HD, n * tile : (n + 1) * tile] = turned[j * HD : (j + 1) * HD]
+    wq_first = claim("recv", 1)
+    push(wq.at[s], wq.at[s], wq_first, sib)
+    load_vec.wait()
+    load_tbias.wait()
+    load_pre.wait()
+    arrived(vec.at[1 - s], small)
+    arrived(tbias.at[1 - s], small + 1)
+    arrived(pre.at[1 - s], small + 2)
+
+    def row(layer, index):
+        return vec[layer, index : index + 1, :]
+
+    step = 32
+
+    def norm_one(layer, p):
+        def some(i, _):
+            at = pl.multiple_of(i * step, step)
+            x = xs[layer, p, pl.ds(at, step), :].astype(f32)
+            center = x - jnp.mean(x, axis=1, keepdims=True)
+            inverse = lax.rsqrt(jnp.mean(center * center, axis=1, keepdims=True) + epsilon)
+            unit = center * inverse
+            where = pl.multiple_of(p * rows + at, step)
+            z_one[layer, pl.ds(where, step), :] = unit
+            inv_one[layer, pl.ds(where, step), :] = inverse
+            normed[pl.ds(where, step), :] = (unit * row(layer, 0) + row(layer, 1)).astype(bf16)
+            return 0
+
+        lax.fori_loop(0, rows // step, some, 0)
+
+    def norm_two(layer):
+        def some(i, _):
+            at = pl.multiple_of(i * step, step)
+            x = resid[pl.ds(at, step), :]
+            center = x - jnp.mean(x, axis=1, keepdims=True)
+            inverse = lax.rsqrt(jnp.mean(center * center, axis=1, keepdims=True) + epsilon)
+            unit = center * inverse
+            z_two[layer, pl.ds(at, step), :] = unit
+            inv_two[layer, pl.ds(at, step), :] = inverse
+            normed[pl.ds(at, step), :] = (unit * row(layer, 3) + row(layer, 4)).astype(bf16)
+            return 0
+
+        lax.fori_loop(0, brows // step, some, 0)
+
+    def norm_pull(i, units, inverses, gain):
+        at = pl.multiple_of(i * step, step)
+        unit = units[pl.ds(at, step), :]
+        scaled = total[pl.ds(at, step), :] * gain
+        mean_grad = jnp.mean(scaled, axis=1, keepdims=True)
+        mean_cross = jnp.mean(scaled * unit, axis=1, keepdims=True)
+        return at, inverses[pl.ds(at, step), :] * (scaled - mean_grad - unit * mean_cross)
+
+    def tiles(count, body):
+        def some(i, _):
+            body(pl.multiple_of(i * tile, tile))
+            return 0
+
+        lax.fori_loop(0, count // tile, some, 0)
+
+    def project(layer):
+        first = claim("recv", nb)
+        for k in range(1, nb + 1):
+            head = block(k)
+            part = dot_nt(wq[layer, head], normed[...])
+            shift = tbias[layer, head].astype(f32)
+            part = (part + jnp.concatenate([shift, shift], axis=1)).astype(bf16)
+            if k < nb:
+                qkv_send[layer, k] = part
+                push(qkv_send.at[layer, k], qkv.at[layer, d], first + k, (s, t, head))
+            else:
+                qkv[layer, d] = part
+        return first
+
+    def attend(layer, first):
+        out_first = claim("recv", cells)
+        pre_keys = pre[layer, 0, d]
+        pre_values = pre[layer, 1, d].T
+        prefix_row = lax.broadcasted_iota(jnp.int32, (z.prefix_pad, brows), 0)
+        key_at = lax.broadcasted_iota(jnp.int32, (brows, brows), 0)
+        query_at = lax.broadcasted_iota(jnp.int32, (brows, brows), 1)
+        valid = valid_ref[s]
+        number = 0
+        for b in range(nb):
+            arrived(qkv.at[layer, b], first + lax.rem(d + nb - b, nb), d != b)
+            keys_n[layer, b] = qkv[layer, b, HD : 2 * HD, :].T
+            queries = (qkv[layer, b, 0:HD, :].astype(f32) * HD ** (-0.5)).astype(bf16)
+            scores = dot_nn(pre_keys, queries)
+            scores = jnp.where(prefix_row < z.prefix_rows, scores, masked_score)
+            probs_pre[layer, b] = scores
+            peak = jnp.max(scores, axis=0, keepdims=True)
+            for kb in range(b + 1):
+                scores = dot_nn(keys_n[layer, kb], queries)
+                if kb == b:
+                    seen = key_at <= query_at
+                    if b == nb - 1:
+                        seen = seen & (key_at + b * brows < valid)
+                    scores = jnp.where(seen, scores, masked_score)
+                probs[layer, number + kb] = scores
+                peak = jnp.maximum(peak, jnp.max(scores, axis=0, keepdims=True))
+            expons = jnp.exp(probs_pre[layer, b] - peak)
+            probs_pre[layer, b] = expons
+            denominator = jnp.sum(expons, axis=0, keepdims=True)
+            for kb in range(b + 1):
+                expons = jnp.exp(probs[layer, number + kb] - peak)
+                probs[layer, number + kb] = expons
+                denominator = denominator + jnp.sum(expons, axis=0, keepdims=True)
+            scale = 1.0 / denominator
+            prob = probs_pre[layer, b] * scale
+            probs_pre[layer, b] = prob
+            result = dot_nn(pre_values, prob.astype(bf16))
+            for kb in range(b + 1):
+                prob = probs[layer, number + kb] * scale
+                probs[layer, number + kb] = prob
+                result = result + dot_nn(qkv[layer, kb, 2 * HD : 3 * HD, :], prob.astype(bf16))
+            number += b + 1
+            out_t[layer, b] = result
+            low = result.astype(bf16)
+            ot_send[layer, b] = low
+            for k in range(nt):
+                if k == 0:
+                    push(ot_send.at[layer, b], att.at[layer, me], out_first + me, (s, t, b), d != b)
+
+                    @pl.when(d == b)
+                    def _():
+                        att[layer, me] = low
+                else:
+                    push(ot_send.at[layer, b], att.at[layer, me], out_first + me, (s, plane(k), b))
+        return out_first
+
+    def cells_wait(buf, layer, first):
+        for cell in range(cells):
+            arrived(buf.at[layer, cell], first + cell, me != cell)
+
+    def mixer_rows(layer, first):
+        cells_wait(att, layer, first)
+        for p in range(nt):
+            joined = att[layer, p * nb : (p + 1) * nb].reshape(nb * HD, brows)
+            wide[:, p * nb * HD : (p + 1) * nb * HD] = joined.T
+
+        def some(at):
+            x = xs[layer, :, :, pl.ds(at, tile)].reshape(brows, tile).astype(f32)
+            shift = vec[layer, 2:3, pl.ds(at, tile)]
+            resid[:, pl.ds(at, tile)] = dot_nn(wide[...], wm[layer, :, pl.ds(at, tile)]) + x + shift
+
+        tiles(z.width, some)
+
+    def feed_first(layer):
+        def some(at):
+            v = dot_nn(normed[...], we[layer, :, pl.ds(at, tile)]) + vec[layer, 6:7, pl.ds(at, tile)]
+            root = 0.7978845608028654
+            square = v * v
+            th = jnp.tanh(root * v * (1.0 + 0.044715 * square))
+            half = 0.5 * (1.0 + th)
+            wide[:, pl.ds(at, tile)] = (v * half).astype(bf16)
+            gelu_grad[layer, :, pl.ds(at, tile)] = half + (0.5 * root) * v * (1.0 - th * th) * (
+                1.0 + 3.0 * 0.044715 * square
+            )
+
+        tiles(z.hidden, some)
+
+    def feed_second(layer):
+        def some(at):
+            part = dot_nn(wide[...], wr[layer, :, pl.ds(at, tile)])
+            total[:, pl.ds(at, tile)] = part
+            y_send[layer, :, :, pl.ds(at, tile)] = part.astype(bf16).reshape(nt, rows, tile)
+
+        tiles(z.width, some)
+        first = claim("recv", nt)
+        for k in range(1, nt):
+            push(y_send.at[layer, plane(k)], y_recv.at[layer, k], first + k, (s, plane(k), d))
+        return first
+
+    def own_rows(ref):
+        return ref[pl.ds(pl.multiple_of(t * rows, rows), rows), :]
+
+    def output_sum(layer, first, base):
+        result = base
+        for k in range(1, nt):
+            arrived(y_recv.at[layer, k], first + k)
+            result = result + y_recv[layer, k].astype(f32)
+        return result.astype(bf16)
+
+    out_sem = claim("recv", 4)
+    out_loads = []
+
+    def put(src, out, layer, index):
+        push(src, out.at[0, s], out_sem + index, sib, s != layer)
+        copy = pltpu.make_async_copy(src, out.at[0, s], local_sem.at[claim("local", 1)])
+        pl.when(s == layer)(copy.start)
+        out_loads.append((copy, s == layer))
+
+    own_weights = [load_mixer, load_expand, load_reduce]
+    feed_recv = claim("recv", 2)
+    y_base = []
+    out_first = None
+    for layer in range(2):
+        if layer == 0:
+            load_x.wait()
+        norm_one(layer, t)
+        for k in range(1, nt):
+            spread_wait(xs, layer, x_first[layer], k)
+            norm_one(layer, plane(nt - k))
+        if layer == 0:
+            arrived(wq.at[0], wq_first, s == 1)
+        else:
+            arrived(wq.at[1], wq_first, s == 0)
+        q_first = project(layer)
+        if layer == 0:
+            push(expand_in, we.at[s], feed_recv, sib)
+            push(reduce_in, wr.at[s], feed_recv + 1, sib)
+            mix_two(0)
+            mix_one(1)
+        else:
+            load_gy.wait()
+            gy_first[1] = spread(gys.at[1, t], gys, 1)
+        out_first = attend(layer, q_first)
+        if layer == 0:
+            for copy in own_weights:
+                copy.wait()
+            arrived(we.at[1 - s], feed_recv)
+            arrived(wr.at[1 - s], feed_recv + 1)
+            mix_three(0)
+        else:
+            mix_three(1)
+        arrived(wm.at[layer], mix_third[layer], s != layer)
+        mixer_rows(layer, out_first)
+        norm_two(layer)
+        y_base.append(None)
+        feed_first(layer)
+        y_first = feed_second(layer)
+        base = own_rows(resid) + own_rows(total) + row(layer, 5)
+        if layer == 0:
+            mix_two(1)
+            low = output_sum(0, y_first, base)
+            xs[1, t] = low
+            x_first[1] = spread(xs.at[1, t], xs, 1)
+            put(xs.at[1, t], lo_out, 0, 0)
+        else:
+            gi_own[...] = base
+            last_first = y_first
+
+    def grad_hidden(layer):
+        def some(at):
+            upper = gys[layer].reshape(brows, z.width)
+            part = dot_nt(upper, wr[layer, pl.ds(at, tile), :])
+            wide[:, pl.ds(at, tile)] = (part * gelu_grad[layer, :, pl.ds(at, tile)]).astype(bf16)
+
+        tiles(z.hidden, some)
+
+    def grad_mid(layer):
+        def some(at):
+            total[:, pl.ds(at, tile)] = dot_nt(wide[...], we[layer, pl.ds(at, tile), :])
+
+        tiles(z.width, some)
+
+        def pull(i, _):
+            at, part = norm_pull(i, z_two.at[layer], inv_two.at[layer], row(layer, 3))
+            upper = gys[layer, i // (rows // step), pl.ds(lax.rem(i, rows // step) * step, step), :]
+            part = part + upper.astype(f32) * (1.0 / nt)
+            grad_res[pl.ds(at, step), :] = part
+            normed[pl.ds(at, step), :] = part.astype(bf16)
+            return 0
+
+        lax.fori_loop(0, brows // step, pull, 0)
+
+    def grad_to_heads(layer):
+        first = claim("recv", cells)
+        for k in range(1, nt + 1):
+            p = plane(k)
+            here = wm[layer, pl.ds(pl.multiple_of(p * z.local_width, z.local_width), z.local_width), :]
+            part = dot_nt(here, normed[...]).astype(bf16).reshape(nb, HD, brows)
+            gh_send[layer, k - 1] = part
+            for j in range(nb):
+                away = None if k < nt else d != j
+                push(gh_send.at[layer, k - 1, j], gh.at[layer, me], first + me, (s, p, j), away)
+                if k == nt:
+
+                    @pl.when(d == j)
+                    def _():
+                        gh[layer, me] = part[j]
+
+        return first
+
+    def attend_back(layer, first):
+        cells_wait(gh, layer, first)
+        out_first = claim("recv", nb)
+        pre_values = pre[layer, 1, d]
+        pre_keys = pre[layer, 0, d].T
+        dkeys[...] = jnp.zeros_like(dkeys)
+        dvalues[...] = jnp.zeros_like(dvalues)
+        pre_dkeys = jnp.zeros((z.prefix_pad, HD), f32)
+        pre_dvalues = jnp.zeros((z.prefix_pad, HD), f32)
+        for b in reversed(range(nb)):
+            number = b * (b + 1) // 2
+            grad = gh[layer, b].astype(f32)
+            for p in range(1, nt):
+                grad = grad + gh[layer, p * nb + b].astype(f32)
+            grad = grad.astype(bf16)
+            delta = jnp.sum(grad.astype(f32) * out_t[layer, b], axis=0, keepdims=True)
+            grad_n = grad.T
+            queries = (qkv[layer, b, 0:HD, :].astype(f32) * HD ** (-0.5)).astype(bf16).T
+            prob = probs_pre[layer, b]
+            dscore = (prob * (dot_nn(pre_values, grad) - delta)).astype(bf16)
+            dq = dot_nn(pre_keys, dscore)
+            pre_dkeys = pre_dkeys + dot_nn(dscore, queries)
+            pre_dvalues = pre_dvalues + dot_nn(prob.astype(bf16), grad_n)
+            for kb in range(b + 1):
+                prob = probs[layer, number + kb]
+                values = qkv[layer, kb, 2 * HD : 3 * HD, :].T
+                dscore = (prob * (dot_nn(values, grad) - delta)).astype(bf16)
+                dq = dq + dot_nn(qkv[layer, kb, HD : 2 * HD, :], dscore)
+                dkeys[kb] = dkeys[kb] + dot_nn(dscore, queries)
+                dvalues[kb] = dvalues[kb] + dot_nn(prob.astype(bf16), grad_n)
+            joined = jnp.concatenate(
+                [dq * HD ** (-0.5), dkeys[b].T, dvalues[b].T], axis=0
+            ).astype(bf16)
+            dm_send[layer, b] = joined
+            push(dm_send.at[layer, b], dm.at[layer, d], out_first + d, (s, t, b), d != b)
+
+            @pl.when(d == b)
+            def _():
+                dm[layer, d] = joined
+
+        pg[layer, 0] = pre_dkeys
+        pg[layer, 1] = pre_dvalues
+        return out_first
+
+    def grad_rows(layer, first):
+        for j in range(nb):
+            arrived(dm.at[layer, j], first + j, d != j)
+        for j in range(nb):
+            wide[:, j * 3 * HD : (j + 1) * 3 * HD] = dm[layer, j].T
+        depth = nb * 3 * HD
+
+        def some(at):
+            right = wq[layer, :, :, pl.ds(at, tile)].reshape(depth, tile)
+            total[:, pl.ds(at, tile)] = dot_nn(wide[:, :depth], right)
+
+        tiles(z.width, some)
+
+        def pull(i, _):
+            at, part = norm_pull(i, z_one.at[layer], inv_one.at[layer], row(layer, 0))
+            part = part + grad_res[pl.ds(at, step), :]
+            grad_res[pl.ds(at, step), :] = part
+            p = i // (rows // step)
+            gi_send[layer, p, pl.ds(lax.rem(i, rows // step) * step, step), :] = part.astype(bf16)
+            return 0
+
+        lax.fori_loop(0, brows // step, pull, 0)
+        recv = claim("recv", nt)
+        for k in range(1, nt):
+            push(gi_send.at[layer, plane(k)], gi_recv.at[layer, k], recv + k, (s, plane(k), d))
+        return recv
+
+    def grad_sum(layer, first):
+        result = own_rows(grad_res)
+        for k in range(1, nt):
+            arrived(gi_recv.at[layer, k], first + k)
+            result = result + gi_recv[layer, k].astype(f32)
+        return result.astype(bf16)
+
+    for layer in (1, 0):
+        for k in range(1, nt):
+            spread_wait(gys, layer, gy_first[layer], k)
+        grad_hidden(layer)
+        grad_mid(layer)
+        heads_first = grad_to_heads(layer)
+        if layer == 1:
+            y_last[...] = output_sum(1, last_first, gi_own[...])
+            put(y_last, lo_out, 1, 1)
+        rows_first = attend_back(layer, heads_first)
+        grads_first = grad_rows(layer, rows_first)
+        if layer == 1:
+            gys[0, t] = grad_sum(1, grads_first)
+            gy_first[0] = spread(gys.at[0, t], gys, 0)
+            put(gys.at[0, t], ig_out, 1, 2)
+        else:
+            sib_sem = claim("recv", 1)
+            push(pg.at[1 - s], pg_recv, sib_sem, sib)
+            arrived(pg_recv, sib_sem)
+            pg_sum[...] = pg[s] + pg_recv[...]
+            all_first = claim("recv", nb)
+            for k in range(1, nb):
+                push(pg_sum, pg_all.at[d], all_first + k, (s, t, block(k)))
+            pg_all[d] = pg_sum[...]
+            y_last_two = grad_sum(0, grads_first)
+            gi_low = y_last_two
+            for k in range(1, nb):
+                arrived(pg_all.at[block(nb - k)], all_first + k)
+            pg_out[...] = pg_all[...]
+
+    xs[0, t] = gi_low
+    put(xs.at[0, t], ig_out, 0, 3)
+    for index, (out, layer) in enumerate(((lo_out, 0), (lo_out, 1), (ig_out, 1), (ig_out, 0))):
+        arrived(out.at[0, 1 - s], out_sem + index, s == layer)
+    for copy, when in pending:
+        if when is None:
+            copy.wait_send()
+        else:
+            pl.when(when)(copy.wait_send)
+    for copy, when in out_loads:
+        pl.when(when)(copy.wait)
+    z.counts = counts
+
+
+def run_layers(z, valid_len, block_input, output_grad, vec, tbias, triple, mixer, expand, reduce, prefix):
+    nt, nb, rows, brows = z.planes, z.blocks, z.rows, z.block_rows
+    width, hidden = z.width, z.hidden
+    pairs = nb * (nb + 1) // 2
+    V = pltpu.VMEM
+    any_space = pl.BlockSpec(memory_space=pl.ANY)
+    scratch = [
+        V((2, 8, width), f32),
+        V((2, nb, 3 * HD, 128), bf16),
+        V((3, width, z.local_width), bf16),
+        V((2, nb, 3 * HD, width), bf16),
+        V((2, width, width), bf16),
+        V((2, width, hidden), bf16),
+        V((2, hidden, width), bf16),
+        V((2, 2, nb, z.prefix_pad, HD), bf16),
+        V((2, nt, rows, width), bf16),
+        V((2, nt, rows, width), bf16),
+        V((2, nb, 3 * HD, brows), bf16),
+        V((2, nb, 3 * HD, brows), bf16),
+        V((2, nb, HD, brows), bf16),
+        V((2, z.cells, HD, brows), bf16),
+        V((2, nt, rows, width), bf16),
+        V((2, nt, rows, width), bf16),
+        V((2, nt, nb, HD, brows), bf16),
+        V((2, z.cells, HD, brows), bf16),
+        V((2, nb, 3 * HD, brows), bf16),
+        V((2, nb, 3 * HD, brows), bf16),
+        V((2, nt, rows, width), bf16),
+        V((2, nt, rows, width), bf16),
+        V((2, brows, width), f32),
+        V((2, brows, 1), f32),
+        V((2, brows, width), f32),
+        V((2, brows, 1), f32),
+        V((2, brows, hidden), f32),
+        V((2, pairs, brows, brows), f32),
+        V((2, nb, z.prefix_pad, brows), f32),
+        V((2, nb, HD, brows), f32),
+        V((2, nb, brows, HD), bf16),
+        V((brows, width), bf16),
+        V((brows, width), bf16),
+        V((brows, width), f32),
+        V((brows, width), f32),
+        V((brows, width), f32),
+        V((nb, brows, HD), f32),
+        V((nb, brows, HD), f32),
+        V((rows, width), bf16),
+        V((rows, width), f32),
+        V((2, 2, z.prefix_pad, HD), f32),
+        V((2, z.prefix_pad, HD), f32),
+        V((2, z.prefix_pad, HD), f32),
+        V((nb, 2, z.prefix_pad, HD), f32),
+        pltpu.SemaphoreType.DMA((200,)),
+        pltpu.SemaphoreType.DMA((200,)),
+        pltpu.SemaphoreType.DMA((20,)),
+    ]
+    return pl.pallas_call(
+        partial(both_layers, z),
+        out_shape=(
+            jax.ShapeDtypeStruct((1, 2, rows, width), bf16),
+            jax.ShapeDtypeStruct((1, 2, rows, width), bf16),
+            jax.ShapeDtypeStruct((nb, 2, z.prefix_pad, HD), f32),
+        ),
+        in_specs=[pl.BlockSpec(memory_space=pltpu.SMEM)] + [any_space] * 9,
+        out_specs=(any_space, any_space, pl.BlockSpec(memory_space=pltpu.VMEM)),
+        scratch_shapes=scratch,
+        compiler_params=pltpu.CompilerParams(
+            collective_id=0, has_side_effects=True, vmem_limit_bytes=60 * 2**20
+        ),
+        cost_estimate=pl.CostEstimate(
+            flops=7 * 10**9, bytes_accessed=16 * 2**20, transcendentals=4 * 10**6
+        ),
+    )(valid_len, block_input, output_grad, vec, tbias, triple, mixer, expand, reduce, prefix)
+
+
+def head_a_device(
+    block_input,
+    output_grad,
+    valid_len,
+    first_gain,
+    first_bias,
+    triple_weight,
+    triple_bias,
+    mixer_weight,
+    mixer_bias,
+    second_gain,
+    second_bias,
+    expand_weight,
+    expand_bias,
+    reduce_weight,
+    reduce_bias,
+    prefix_table,
+    inner_weight,
+    inner_bias,
+    outer_weight,
+    outer_bias,
+):
+    planes, blocks = lax.axis_size("tensor"), lax.axis_size("dp")
+    local_width = triple_weight.shape[3]
+    prefix_rows = prefix_table.shape[0]
+    z = Sizes(
+        planes,
+        blocks,
+        block_input.shape[1],
+        block_input.shape[2],
+        local_width,
+        expand_weight.shape[2],
+        prefix_rows,
+    )
+    z.prefix_pad = -(-prefix_rows // 16) * 16
+    inner_pre = jnp.dot(prefix_table, inner_weight, preferred_element_type=f32) + inner_bias
+    inner_act = jnp.tanh(inner_pre)
+    inner_low = inner_act.astype(bf16)
+    outer_local = outer_weight[:, 0].reshape(outer_weight.shape[0], 2 * local_width)
+    prefix_full = (
+        jnp.dot(inner_low, outer_local, preferred_element_type=f32)
+        + outer_bias[0].reshape(2 * local_width)
+    ).astype(bf16)
+    prefix_heads = prefix_full.reshape(prefix_rows, 2, blocks, HD).transpose(1, 2, 0, 3)
+    prefix_heads = jnp.pad(prefix_heads, ((0, 0), (0, 0), (0, z.prefix_pad - prefix_rows), (0, 0)))
+    vec = jnp.concatenate(
+        [first_gain, first_bias, mixer_bias, second_gain, second_bias, reduce_bias, expand_bias, expand_bias],
+        axis=0,
+    ).astype(f32)
+    tbias = triple_bias[0].reshape(3, blocks, HD).transpose(1, 0, 2).reshape(blocks, 3 * HD, 1)
+    tbias = jnp.broadcast_to(tbias, (blocks, 3 * HD, 128))
+    layer_outputs, input_grads, prefix_parts = run_layers(
+        z,
+        valid_len,
+        block_input,
+        output_grad,
+        vec,
+        tbias,
+        triple_weight[0].transpose(1, 0, 2),
+        mixer_weight[0],
+        expand_weight[0],
+        reduce_weight[0],
+        prefix_heads,
+    )
+    prefix_total = (
+        prefix_parts[:, :, :prefix_rows].transpose(2, 1, 0, 3).reshape(prefix_rows, 2 * local_width)
+    )
+    return (layer_outputs, input_grads) + prefix_back(
+        prefix_total,
+        prefix_full,
+        inner_act,
+        inner_low,
+        outer_local,
+        prefix_table,
+        inner_weight,
+        local_width,
+    )
+
+
+def prefix_back(
+    prefix_total,
+    prefix_full,
+    inner_act,
+    inner_low,
+    outer_local,
+    prefix_table,
+    inner_weight,
+    local_width,
+):
+    inner_float = inner_low.astype(f32)
+    outer_float = outer_local.astype(f32)
     outer_weight_grad = jnp.dot(inner_float.T, prefix_total, precision=highest).reshape(
         -1, 1, 2, local_width
     )
@@ -371,13 +1178,11 @@
         jnp.dot(prefix_total, outer_float.T, precision=highest), ("section", "tensor")
     )
     inner_grad = hidden_grad * (1.0 - inner_act * inner_act)
-    inner_weight_grad = jnp.dot(prefix_table.astype(jnp.float32).T, inner_grad, precision=highest)
+    inner_weight_grad = jnp.dot(prefix_table.astype(f32).T, inner_grad, precision=highest)
     inner_bias_grad = jnp.sum(inner_grad, axis=0)
-    table_grad = jnp.dot(inner_grad, inner_weight.astype(jnp.float32).T, precision=highest)
+    table_grad = jnp.dot(inner_grad, inner_weight.astype(f32).T, precision=highest)
     prefix_states = prefix_full.reshape(-1, 2, local_width).transpose(1, 0, 2)[None]
     return (
-        layer_outputs,
-        input_grads,
         prefix_states,
         table_grad,
         inner_weight_grad,
@@ -388,8 +1193,22 @@
 
 
 def solution(mesh):
+    def step(*args):
+        triple_weight = args[5]
+        micro_count, share_rows, width = args[0].shape
+        fits = (
+            lax.axis_size("section") == 2
+            and micro_count == 2
+            and triple_weight.shape[3] == HD * lax.axis_size("dp")
+            and share_rows * lax.axis_size("tensor") == 256
+            and triple_weight.shape[3] % 256 == 0
+            and width % 256 == 0
+            and args[11].shape[2] == width
+        )
+        return head_a_device(*args) if fits else shards(*args)
+
     return jax.shard_map(
-        shards,
+        step,
         mesh=mesh,
         in_specs=(
             P(None, ("dp", "tensor"), None),

time: 1160 us -> 253 us (0.22)
  waiting for transfers between devices: 427 us -> 0 us
  blocking collectives: 408 us -> 34.2 us
  Pallas kernels: 0 us -> 200 us
  matrix products: 142 us -> 4.89 us
  other arithmetic: 80.8 us -> 2 us
  local copies, waits for them, and re-layouts: 53.3 us -> 10.7 us
  starting transfers between devices: 25.2 us -> 0 us
  between operations: 16.7 us -> 0.84 us
    reduce_scatter x21 -> x0, waiting for transfers between devices: 423 us -> none  [the longest x6 103 us: layer_forward(): lax.psum_scatter(jnp.dot(attended, mixer_weight, preferred_element_type=j...]
    all_gather x30 -> x0, blocking collectives: 361 us -> none  [the longest x6 91.7 us: layer_forward(): lax.all_gather(normed_two.astype(jnp.bfloat16), 'tensor', axis=0, tiled=T...]
    pallas_call x0 -> x1, Pallas kernels: none -> 200 us  [run_layers(): pl.pallas_call(partial(both_layers, z), out_shape=(jax.ShapeDtypeStruct((...]
    dot_general x81 -> x6, matrix products: 142 us -> 4.89 us  [the longest x1 1.56 us: prefix_back(): jnp.dot(inner_grad, inner_weight.astype(f32).T, precision=highest)]
    reduce_sum x36 -> x2, other arithmetic: 29 us -> 0.62 us  [the longest x1 0.6 us: prefix_back(): inner_bias_grad = jnp.sum(inner_grad, axis=0)]
    ppermute x4 -> x0, starting transfers between devices: 23.9 us -> none  [passed_along(): return lax.ppermute(block, axis, route)]
    all_gather x12 -> x0, local copies, waits for them, and re-layouts: 22.5 us -> none  [the longest x6 11.3 us: layer_forward(): lax.all_gather(mixed_rows[:, 2 * local_width:], 'dp', axis=0, tiled=True)]
    convert_element_type x19 -> x2, other arithmetic: 18.7 us -> 1.37 us  [the longest x1 0.75 us: head_a_device(): jnp.dot(prefix_table, inner_weight, preferred_element_type=f32) + inner_bias]
  transfers between devices with their start and end apart: 25 -> 0, of which waited for: 19 -> 0; matrix products, arithmetic and copies ran while one was open for 9% -> 0% of each run, Pallas kernels for 0% -> 0%
where the time goes in v1:
time: 253 us; the launch traced here: 252 us
  Pallas kernels  200 us (79%)
  blocking collectives  34.2 us (14%)
  local copies, waits for them, and re-layouts  10.7 us (4%)
  matrix products  4.89 us (2%)
    pallas_call x1, Pallas kernels, run_layers(): pl.pallas_call(partial(both_layers, z), out_shape=(jax.ShapeDtypeStruct((...  200 us
    psum x1, blocking collectives, prefix_back(): lax.psum(jnp.dot(prefix_total, outer_float.T, precision=highest), ('secti...  34.2 us
    unnamed x34, local copies, waits for them, and re-layouts  6.56 us

profile of v1, /device:TPU:1, one launch (start us, length us, event | category | flops | bytes accessed | tf_op | source)
XLA Modules:
  0.0 252.3 jit_solution(12632958817038237372)
XLA Ops:
  0.6 0.0 copy-start
  0.7 0.0 copy-start.13
  0.7 0.0 copy-start.12
  0.7 0.0 copy-start.6
  0.7 0.0 copy-start.7
  0.7 0.0 copy-start.8
  0.7 0.0 copy-start.9
  0.7 0.0 copy-start.10
  0.7 0.0 copy-start.5
  0.7 0.0 copy-start.11
  0.7 0.8 convert_element_type.29
  1.5 0.4 copy-done
  1.9 1.0 fusion
  2.9 1.1 copy.50
  4.0 0.0 copy-done.13
  4.1 0.2 fusion.1
  4.2 0.1 reshape.47
  4.3 0.6 pad.4.prefix_in
  5.0 0.0 copy-done.12
  5.0 0.1 reshape_squeeze.7
  5.1 0.1 broadcast_in_dim.12
  5.2 0.8 broadcast_in_dim.13.tbias_in
  6.0 0.0 copy-done.6
  6.0 0.0 copy-done.7
  6.0 0.0 copy-done.8
  6.0 0.0 copy-done.9
  6.0 0.0 copy-done.10
  6.0 0.0 copy-done.5
  6.0 0.0 copy-done.11
  6.1 0.1 concatenate.3
  6.1 0.6 convert_element_type.28.vec_in
  6.7 199.7 %shard_map.251 = (bf16[1,2,64,1024]{3,2,1,0:T(8,128)(2,1)}, bf16[1,2,64,1024]{3,2,1,0:T(8,128)(2,1)}, f32[4,2,16,64]{3,2,1,0:T(8,128)}) custom-call(s32[2]{0:T(128)} %valid_ref.1, bf16[2,64,1024]{2,1,0:T(8,128)(2,1)} %x_in.1, bf16[2,64,1024]{2,1,0:T(8,128)(2,1)} %gy_in.1, f32[8,1024]{1,0:T(8,128)} %convert_element_type.28.vec_in, ...), custom_call_target="tpu_custom_call" | custom-call | flops 7000000000 | bytes 16777216 | tf_op jit(solution)/shard_map/pallas_call | solution.py:1063
  206.4 0.8 slice_bitcast_fusion
  207.3 0.1 reshape.49
  207.4 0.5 fusion.9
  207.9 34.2 %psum.7 = f32[10,512]{1,0:T(8,128)S(1)} all-reduce(f32[10,512]{1,0:T(8,128)S(1)} %fusion.9), channel_id=1, replica_groups=mesh['section'=2,'tensor'=4,'dp'=4] {'section','tensor'}, use_global_device_ids=true, to_apply=%region_0.1 | all-reduce | flops 5120 | bytes 40960 | tf_op jit(solution)/shard_map/psum | solution.py:1177
  242.1 0.0 copy-done.4
  242.1 1.0 convolution_bitcast_fusion
  243.1 1.8 copy.48
  245.0 1.6 fusion.8
  246.5 0.6 fusion.7
  247.1 0.6 convolution_bitcast_fusion.1
  247.8 1.8 copy.49
  249.5 0.0 copy-done.3
  249.6 0.7 reshape.51
  250.2 0.6 reshape.48
  250.8 0.7 copy.60
  251.6 0.7 copy.61
  (14 shorter events, 0.1 us)
Async XLA Ops:
  0.6 1.2 copy-start
  0.7 3.4 %copy-start.13 = (bf16[1,2,256]{2,1,0:T(2,128)(2,1)S(1)}, bf16[1,2,256]{2,1,0:T(2,128)(2,1)}, u32[]{:S(2)}) copy-start(bf16[1,2,256]{2,1,0:T(2,128)(2,1)} %param.39) | copy-start | bytes 3076
  0.7 4.3 %copy-start.12 = (bf16[1,3,256]{2,1,0:T(4,128)(2,1)S(1)}, bf16[1,3,256]{2,1,0:T(4,128)(2,1)}, u32[]{:S(2)}) copy-start(bf16[1,3,256]{2,1,0:T(4,128)(2,1)} %param.26) | copy-start | bytes 4612
  0.7 5.3 %copy-start.6 = (bf16[1,1024]{1,0:T(2,128)(2,1)S(1)}, bf16[1,1024]{1,0:T(2,128)(2,1)}, u32[]{:S(2)}) copy-start(bf16[1,1024]{1,0:T(2,128)(2,1)} %param.23) | copy-start | bytes 6148
  0.7 5.3 %copy-start.7 = (bf16[1,1024]{1,0:T(2,128)(2,1)S(1)}, bf16[1,1024]{1,0:T(2,128)(2,1)}, u32[]{:S(2)}) copy-start(bf16[1,1024]{1,0:T(2,128)(2,1)} %param.24) | copy-start | bytes 6148
  0.7 5.3 %copy-start.8 = (bf16[1,1024]{1,0:T(2,128)(2,1)S(1)}, bf16[1,1024]{1,0:T(2,128)(2,1)}, u32[]{:S(2)}) copy-start(bf16[1,1024]{1,0:T(2,128)(2,1)} %param.28) | copy-start | bytes 6148
  0.7 5.3 %copy-start.9 = (bf16[1,1024]{1,0:T(2,128)(2,1)S(1)}, bf16[1,1024]{1,0:T(2,128)(2,1)}, u32[]{:S(2)}) copy-start(bf16[1,1024]{1,0:T(2,128)(2,1)} %param.29) | copy-start | bytes 6148
  0.7 5.3 %copy-start.10 = (bf16[1,1024]{1,0:T(2,128)(2,1)S(1)}, bf16[1,1024]{1,0:T(2,128)(2,1)}, u32[]{:S(2)}) copy-start(bf16[1,1024]{1,0:T(2,128)(2,1)} %param.30) | copy-start | bytes 6148
  0.7 5.3 %copy-start.5 = (bf16[1,1024]{1,0:T(2,128)(2,1)S(1)}, bf16[1,1024]{1,0:T(2,128)(2,1)}, u32[]{:S(2)}) copy-start(bf16[1,1024]{1,0:T(2,128)(2,1)} %param.32) | copy-start | bytes 6148
  0.7 5.3 %copy-start.11 = (bf16[1,1024]{1,0:T(2,128)(2,1)S(1)}, bf16[1,1024]{1,0:T(2,128)(2,1)}, u32[]{:S(2)}) copy-start(bf16[1,1024]{1,0:T(2,128)(2,1)} %param.34) | copy-start | bytes 6148
  6.7 235.4 %copy-start.4 = (bf16[10,1024]{1,0:T(8,128)(2,1)S(1)}, bf16[10,1024]{1,0:T(8,128)(2,1)}, u32[]{:S(2)}) copy-start(bf16[10,1024]{1,0:T(8,128)(2,1)} %param.35) | copy-start | bytes 61444
  244.9 4.6 %copy-start.3 = (f32[4,2,16,64]{3,2,1,0:T(8,128)S(1)}, f32[4,2,16,64]{3,2,1,0:T(8,128)}, u32[]{:S(2)}) copy-start(f32[4,2,16,64]{3,2,1,0:T(8,128)} %get-tuple-element.13) | copy-start | bytes 98308
  245.0 5.9 %copy-start.2 = (bf16[1,2,64,1024]{3,2,1,0:T(8,128)(2,1)S(1)}, bf16[1,2,64,1024]{3,2,1,0:T(8,128)(2,1)}, u32[]{:S(2)}) copy-start(bf16[1,2,64,1024]{3,2,1,0:T(8,128)(2,1)} %get-tuple-element.54) | copy-start | bytes 786436
  246.5 5.0 %copy-start.1 = (bf16[1,2,64,1024]{3,2,1,0:T(8,128)(2,1)S(1)}, bf16[1,2,64,1024]{3,2,1,0:T(8,128)(2,1)}, u32[]{:S(2)}) copy-start(bf16[1,2,64,1024]{3,2,1,0:T(8,128)(2,1)} %get-tuple-element.55) | copy-start | bytes 786436

commit v2 on v1

--- a/solution.py
+++ b/solution.py
@@ -386,6 +386,12 @@
     return lax.dot_general(left, right, (((1,), (1,)), ((), ())), preferred_element_type=f32)
 
 
+def dot_split(left, right, dot):
+    high = left.astype(bf16)
+    low = (left - high.astype(f32)).astype(bf16)
+    return dot(high, right) + dot(low, right)
+
+
 class Sizes:
     def __init__(self, planes, blocks, rows, width, local_width, hidden, prefix_rows):
         self.planes = planes
@@ -403,18 +409,31 @@
 def both_layers(
     z,
     valid_ref,
+    gain_one_in,
+    bias_one_in,
+    triple_bias_in,
+    mixer_bias_in,
+    gain_two_in,
+    bias_two_in,
+    expand_bias_in,
+    reduce_bias_in,
+    table_in,
+    inner_bias_in,
+    outer_bias_in,
     x_in,
     gy_in,
-    vec_in,
-    tbias_in,
     triple_in,
     mixer_in,
     expand_in,
     reduce_in,
-    prefix_in,
+    inner_in,
+    outer_in,
     lo_out,
     ig_out,
     pg_out,
+    hidden_out,
+    act_out,
+    prefix_out,
     vec,
     tbias,
     triple_own,
@@ -459,6 +478,13 @@
     pg_recv,
     pg_sum,
     pg_all,
+    table_pad,
+    inner_w,
+    outer_w,
+    hid_part,
+    hid_recv,
+    hid_pair,
+    hid_all,
     send_sem,
     recv_sem,
     local_sem,
@@ -524,13 +550,23 @@
 
     load_x = lcopy(x_in.at[s], xs.at[0, t])
     load_triple = lcopy(triple_in, triple_own)
-    load_vec = lcopy(vec_in, vec.at[s])
-    load_tbias = lcopy(tbias_in, tbias.at[s])
-    load_pre = lcopy(prefix_in, pre.at[s])
+    load_inner = lcopy(inner_in, inner_w)
+    load_outer = lcopy(outer_in, outer_w)
     load_mixer = lcopy(mixer_in, wm.at[s, pl.ds(pl.multiple_of(t * z.local_width, 256), z.local_width)])
     load_expand = lcopy(expand_in, we.at[s])
     load_reduce = lcopy(reduce_in, wr.at[s])
     load_gy = lcopy(gy_in.at[s], gys.at[1, t])
+
+    for index, ref in enumerate(
+        (gain_one_in, bias_one_in, mixer_bias_in, gain_two_in, bias_two_in, reduce_bias_in, expand_bias_in)
+    ):
+        vec[s, index : index + 1, :] = ref[...].astype(f32)
+    for c in range(3):
+        shift = jnp.broadcast_to(triple_bias_in[0, c : c + 1, :].astype(f32), (128, z.local_width)).T
+        for j in range(nb):
+            tbias[s, j, c * HD : (c + 1) * HD, :] = shift[j * HD : (j + 1) * HD].astype(bf16)
+    table_pad[...] = jnp.zeros_like(table_pad)
+    table_pad[0 : z.prefix_rows, :] = table_in[...].astype(f32)
 
     pl.semaphore_wait(barrier, cells)
 
@@ -548,9 +584,8 @@
     x_first[0] = spread(x_in.at[s], xs, 0)
 
     small = claim("recv", 3)
-    push(vec_in, vec.at[s], small, sib)
-    push(tbias_in, tbias.at[s], small + 1, sib)
-    push(prefix_in, pre.at[s], small + 2, sib)
+    push(vec.at[s], vec.at[s], small, sib)
+    push(tbias.at[s], tbias.at[s], small + 1, sib)
 
     mix_first = [claim("recv", nt), claim("recv", nt)]
     mix_second = [claim("recv", nt * nb), claim("recv", nt * nb)]
@@ -603,9 +638,19 @@
                 wq[s, j, c * HD : (c + 1) * HD, n * tile : (n + 1) * tile] = turned[j * HD : (j + 1) * HD]
     wq_first = claim("recv", 1)
     push(wq.at[s], wq.at[s], wq_first, sib)
-    load_vec.wait()
-    load_tbias.wait()
-    load_pre.wait()
+    load_inner.wait()
+    inner_act = jnp.tanh(
+        dot_nn(table_pad[...].astype(bf16), inner_w[...]) + inner_bias_in[...].astype(f32)
+    )
+    act_out[...] = inner_act
+    load_outer.wait()
+    prefix = (dot_nn(inner_act.astype(bf16), outer_w[...]) + outer_bias_in[...].astype(f32)).astype(bf16)
+    prefix_out[...] = prefix
+    for c in range(2):
+        for j in range(nb):
+            at = c * z.local_width + j * HD
+            pre[s, c, j] = prefix[:, at : at + HD]
+    push(pre.at[s], pre.at[s], small + 2, sib)
     arrived(vec.at[1 - s], small)
     arrived(tbias.at[1 - s], small + 1)
     arrived(pre.at[1 - s], small + 2)
@@ -628,7 +673,7 @@
             normed[pl.ds(where, step), :] = (unit * row(layer, 0) + row(layer, 1)).astype(bf16)
             return 0
 
-        lax.fori_loop(0, rows // step, some, 0)
+        lax.fori_loop(0, rows // step, some, 0, unroll=True)
 
     def norm_two(layer):
         def some(i, _):
@@ -642,7 +687,7 @@
             normed[pl.ds(at, step), :] = (unit * row(layer, 3) + row(layer, 4)).astype(bf16)
             return 0
 
-        lax.fori_loop(0, brows // step, some, 0)
+        lax.fori_loop(0, brows // step, some, 0, unroll=True)
 
     def norm_pull(i, units, inverses, gain):
         at = pl.multiple_of(i * step, step)
@@ -657,7 +702,7 @@
             body(pl.multiple_of(i * tile, tile))
             return 0
 
-        lax.fori_loop(0, count // tile, some, 0)
+        lax.fori_loop(0, count // tile, some, 0, unroll=True)
 
     def project(layer):
         first = claim("recv", nb)
@@ -863,7 +908,7 @@
             normed[pl.ds(at, step), :] = part.astype(bf16)
             return 0
 
-        lax.fori_loop(0, brows // step, pull, 0)
+        lax.fori_loop(0, brows // step, pull, 0, unroll=True)
 
     def grad_to_heads(layer):
         first = claim("recv", cells)
@@ -948,7 +993,7 @@
             gi_send[layer, p, pl.ds(lax.rem(i, rows // step) * step, step), :] = part.astype(bf16)
             return 0
 
-        lax.fori_loop(0, brows // step, pull, 0)
+        lax.fori_loop(0, brows // step, pull, 0, unroll=True)
         recv = claim("recv", nt)
         for k in range(1, nt):
             push(gi_send.at[layer, plane(k)], gi_recv.at[layer, k], recv + k, (s, plane(k), d))
@@ -971,12 +1016,7 @@
             y_last[...] = output_sum(1, last_first, gi_own[...])
             put(y_last, lo_out, 1, 1)
         rows_first = attend_back(layer, heads_first)
-        grads_first = grad_rows(layer, rows_first)
-        if layer == 1:
-            gys[0, t] = grad_sum(1, grads_first)
-            gy_first[0] = spread(gys.at[0, t], gys, 0)
-            put(gys.at[0, t], ig_out, 1, 2)
-        else:
+        if layer == 0:
             sib_sem = claim("recv", 1)
             push(pg.at[1 - s], pg_recv, sib_sem, sib)
             arrived(pg_recv, sib_sem)
@@ -985,14 +1025,39 @@
             for k in range(1, nb):
                 push(pg_sum, pg_all.at[d], all_first + k, (s, t, block(k)))
             pg_all[d] = pg_sum[...]
-            y_last_two = grad_sum(0, grads_first)
-            gi_low = y_last_two
+        grads_first = grad_rows(layer, rows_first)
+        if layer == 1:
+            gys[0, t] = grad_sum(1, grads_first)
+            gy_first[0] = spread(gys.at[0, t], gys, 0)
+            put(gys.at[0, t], ig_out, 1, 2)
+        else:
             for k in range(1, nb):
                 arrived(pg_all.at[block(nb - k)], all_first + k)
             pg_out[...] = pg_all[...]
-
-    xs[0, t] = gi_low
-    put(xs.at[0, t], ig_out, 0, 3)
+            part = jnp.zeros((z.prefix_pad, z.inner), f32)
+            for j in range(nb):
+                for c in range(2):
+                    at = c * z.local_width + j * HD
+                    part = part + dot_split(pg_all[j, c], outer_w[:, at : at + HD], dot_nt)
+            hid_part[...] = part
+            hid_sem = claim("recv", 1)
+            push(hid_part, hid_recv, hid_sem, sib)
+            arrived(hid_recv, hid_sem)
+            hid_pair[...] = hid_part[...] + hid_recv[...]
+            hid_first = claim("recv", nt)
+            for k in range(1, nt):
+                push(hid_pair, hid_all.at[t], hid_first + k, (s, plane(k), d))
+            hid_all[t] = hid_pair[...]
+            gi_low = grad_sum(0, grads_first)
+            xs[0, t] = gi_low
+            put(xs.at[0, t], ig_out, 0, 3)
+            for k in range(1, nt):
+                arrived(hid_all.at[plane(nt - k)], hid_first + k)
+            part = hid_all[0]
+            for p in range(1, nt):
+                part = part + hid_all[p]
+            hidden_out[...] = part
+
     for index, (out, layer) in enumerate(((lo_out, 0), (lo_out, 1), (ig_out, 1), (ig_out, 0))):
         arrived(out.at[0, 1 - s], out_sem + index, s == layer)
     for copy, when in pending:
@@ -1005,7 +1070,7 @@
     z.counts = counts
 
 
-def run_layers(z, valid_len, block_input, output_grad, vec, tbias, triple, mixer, expand, reduce, prefix):
+def run_layers(z, small, large):
     nt, nb, rows, brows = z.planes, z.blocks, z.rows, z.block_rows
     width, hidden = z.width, z.hidden
     pairs = nb * (nb + 1) // 2
@@ -1056,6 +1121,13 @@
         V((2, z.prefix_pad, HD), f32),
         V((2, z.prefix_pad, HD), f32),
         V((nb, 2, z.prefix_pad, HD), f32),
+        V((z.prefix_pad, width), f32),
+        V((width, z.inner), bf16),
+        V((z.inner, 2 * z.local_width), bf16),
+        V((z.prefix_pad, z.inner), f32),
+        V((z.prefix_pad, z.inner), f32),
+        V((z.prefix_pad, z.inner), f32),
+        V((nt, z.prefix_pad, z.inner), f32),
         pltpu.SemaphoreType.DMA((200,)),
         pltpu.SemaphoreType.DMA((200,)),
         pltpu.SemaphoreType.DMA((20,)),
@@ -1066,9 +1138,14 @@
             jax.ShapeDtypeStruct((1, 2, rows, width), bf16),
             jax.ShapeDtypeStruct((1, 2, rows, width), bf16),
             jax.ShapeDtypeStruct((nb, 2, z.prefix_pad, HD), f32),
+            jax.ShapeDtypeStruct((z.prefix_pad, z.inner), f32),
+            jax.ShapeDtypeStruct((z.prefix_pad, z.inner), f32),
+            jax.ShapeDtypeStruct((z.prefix_pad, 2 * z.local_width), bf16),
         ),
-        in_specs=[pl.BlockSpec(memory_space=pltpu.SMEM)] + [any_space] * 9,
-        out_specs=(any_space, any_space, pl.BlockSpec(memory_space=pltpu.VMEM)),
+        in_specs=[pl.BlockSpec(memory_space=pltpu.SMEM)]
+        + [pl.BlockSpec(memory_space=pltpu.VMEM)] * (len(small) - 1)
+        + [any_space] * len(large),
+        out_specs=(any_space,) * 2 + (pl.BlockSpec(memory_space=pltpu.VMEM),) * 4,
         scratch_shapes=scratch,
         compiler_params=pltpu.CompilerParams(
             collective_id=0, has_side_effects=True, vmem_limit_bytes=60 * 2**20
@@ -1076,7 +1153,64 @@
         cost_estimate=pl.CostEstimate(
             flops=7 * 10**9, bytes_accessed=16 * 2**20, transcendentals=4 * 10**6
         ),
-    )(valid_len, block_input, output_grad, vec, tbias, triple, mixer, expand, reduce, prefix)
+    )(*small, *large)
+
+
+def prefix_end(
+    z, lo_in, ig_in, pg_in, hidden_in, act_in, prefix_in, table_in, inner_in,
+    lo_out, ig_out, states_out, table_out, inner_out, inner_bias_out, outer_out, outer_bias_out,
+    table_pad, sems,
+):
+    copies = [
+        pltpu.make_async_copy(lo_in, lo_out, sems.at[0]),
+        pltpu.make_async_copy(ig_in, ig_out, sems.at[1]),
+    ]
+    for copy in copies:
+        copy.start()
+    count, width = z.prefix_rows, z.local_width
+    act = act_in[...]
+    inner_grad = hidden_in[...] * (1.0 - act * act)
+    inner_bias_out[...] = jnp.sum(inner_grad, axis=0, keepdims=True)
+    table_pad[...] = jnp.zeros_like(table_pad)
+    table_pad[0:count, :] = table_in[...].astype(f32)
+    high = inner_grad.astype(bf16)
+    low = (inner_grad - high.astype(f32)).astype(bf16)
+    table_turned = table_pad[...].T.astype(bf16)
+    inner_out[...] = dot_nn(table_turned, high) + dot_nn(table_turned, low)
+    table_out[...] = (dot_nt(high, inner_in[...]) + dot_nt(low, inner_in[...]))[0:count]
+    act_turned = act.T.astype(bf16)
+    for c in range(2):
+        states_out[0, c] = prefix_in[0:count, c * width : (c + 1) * width]
+        total = jnp.concatenate([pg_in[j, c] for j in range(z.blocks)], axis=1)
+        high = total.astype(bf16)
+        low = (total - high.astype(f32)).astype(bf16)
+        outer_out[:, c, :] = dot_nn(act_turned, high) + dot_nn(act_turned, low)
+        outer_bias_out[0, c : c + 1, :] = jnp.sum(total, axis=0, keepdims=True)
+    for copy in copies:
+        copy.wait()
+
+
+def finish(z, layer_outputs, input_grads, parts, hidden, act, prefix, table, inner_weight):
+    any_space = pl.BlockSpec(memory_space=pl.ANY)
+    whole = pl.BlockSpec(memory_space=pltpu.VMEM)
+    rows = jax.ShapeDtypeStruct(layer_outputs.shape, bf16)
+    return pl.pallas_call(
+        partial(prefix_end, z),
+        out_shape=(
+            rows,
+            rows,
+            jax.ShapeDtypeStruct((1, 2, z.prefix_rows, z.local_width), bf16),
+            jax.ShapeDtypeStruct((z.prefix_rows, z.width), f32),
+            jax.ShapeDtypeStruct((z.width, z.inner), f32),
+            jax.ShapeDtypeStruct((1, z.inner), f32),
+            jax.ShapeDtypeStruct((z.inner, 2, z.local_width), f32),
+            jax.ShapeDtypeStruct((1, 2, z.local_width), f32),
+        ),
+        in_specs=[any_space] * 2 + [whole] * 6,
+        out_specs=(any_space,) * 2 + (whole,) * 6,
+        scratch_shapes=[pltpu.VMEM((z.prefix_pad, z.width), f32), pltpu.SemaphoreType.DMA((2,))],
+        compiler_params=pltpu.CompilerParams(vmem_limit_bytes=32 * 2**20),
+    )(layer_outputs, input_grads, parts, hidden, act, prefix, table, inner_weight)
 
 
 def head_a_device(
@@ -1114,47 +1248,52 @@
         prefix_rows,
     )
     z.prefix_pad = -(-prefix_rows // 16) * 16
-    inner_pre = jnp.dot(prefix_table, inner_weight, preferred_element_type=f32) + inner_bias
-    inner_act = jnp.tanh(inner_pre)
-    inner_low = inner_act.astype(bf16)
+    z.inner = inner_weight.shape[1]
     outer_local = outer_weight[:, 0].reshape(outer_weight.shape[0], 2 * local_width)
-    prefix_full = (
-        jnp.dot(inner_low, outer_local, preferred_element_type=f32)
-        + outer_bias[0].reshape(2 * local_width)
-    ).astype(bf16)
-    prefix_heads = prefix_full.reshape(prefix_rows, 2, blocks, HD).transpose(1, 2, 0, 3)
-    prefix_heads = jnp.pad(prefix_heads, ((0, 0), (0, 0), (0, z.prefix_pad - prefix_rows), (0, 0)))
-    vec = jnp.concatenate(
-        [first_gain, first_bias, mixer_bias, second_gain, second_bias, reduce_bias, expand_bias, expand_bias],
-        axis=0,
-    ).astype(f32)
-    tbias = triple_bias[0].reshape(3, blocks, HD).transpose(1, 0, 2).reshape(blocks, 3 * HD, 1)
-    tbias = jnp.broadcast_to(tbias, (blocks, 3 * HD, 128))
-    layer_outputs, input_grads, prefix_parts = run_layers(
-        z,
+    small = (
         valid_len,
+        first_gain,
+        first_bias,
+        triple_bias,
+        mixer_bias,
+        second_gain,
+        second_bias,
+        expand_bias,
+        reduce_bias,
+        prefix_table,
+        inner_bias.reshape(1, -1),
+        outer_bias.reshape(1, -1),
+    )
+    large = (
         block_input,
         output_grad,
-        vec,
-        tbias,
         triple_weight[0].transpose(1, 0, 2),
         mixer_weight[0],
         expand_weight[0],
         reduce_weight[0],
-        prefix_heads,
-    )
-    prefix_total = (
-        prefix_parts[:, :, :prefix_rows].transpose(2, 1, 0, 3).reshape(prefix_rows, 2 * local_width)
-    )
-    return (layer_outputs, input_grads) + prefix_back(
-        prefix_total,
-        prefix_full,
-        inner_act,
-        inner_low,
+        inner_weight,
         outer_local,
-        prefix_table,
-        inner_weight,
-        local_width,
+    )
+    results = finish(z, *run_layers(z, small, large), prefix_table, inner_weight)
+    (
+        layer_outputs,
+        input_grads,
+        prefix_states,
+        table_grad,
+        inner_weight_grad,
+        inner_bias_grad,
+        outer_weight_grad,
+        outer_bias_grad,
+    ) = results
+    return (
+        layer_outputs,
+        input_grads,
+        prefix_states,
+        table_grad,
+        inner_weight_grad,
+        inner_bias_grad.reshape(-1),
+        outer_weight_grad.reshape(-1, 1, 2, local_width),
+        outer_bias_grad,
     )
 
 

time: 253 us -> 214 us (0.85); the launches traced: 252 us -> 211 us
  blocking collectives: 34.2 us -> 0 us
  matrix products: 4.89 us -> 0 us
    psum x1 -> x0, blocking collectives: 34.2 us -> none  [prefix_back(): lax.psum(jnp.dot(prefix_total, outer_float.T, precision=highest), ('secti...]
    dot_general x6 -> x0, matrix products: 4.89 us -> none  [the longest x1 1.56 us: prefix_back(): jnp.dot(inner_grad, inner_weight.astype(f32).T, precision=highest)]
    pallas_call x0 -> x1, Pallas kernels: none -> 3.42 us  [finish(): pl.pallas_call(partial(prefix_end, z), out_shape=(rows, rows, jax.ShapeDt...]
    pallas_call x1, Pallas kernels: 200 us -> 196 us  [run_layers(): pl.pallas_call(partial(both_layers, z), out_shape=(jax.ShapeDtypeStruct((...]
    unnamed x34 -> x19, local copies, waits for them, and re-layouts: 6.56 us -> 8.76 us
where the time goes in v2:
time: 214 us; the launch traced here: 211 us
  Pallas kernels  200 us (93%)
  local copies, waits for them, and re-layouts  10 us (5%)
    pallas_call x1, Pallas kernels, run_layers(): pl.pallas_call(partial(both_layers, z), out_shape=(jax.ShapeDtypeStruct((...  196 us
    unnamed x19, local copies, waits for them, and re-layouts  8.76 us

profile of v2, /device:TPU:1, one launch (start us, length us, event | category | flops | bytes accessed | tf_op | source)
XLA Modules:
  0.0 210.6 jit_solution(16178593221109892154)
XLA Ops:
  0.6 1.3 reshape.28.inner_bias_in
  1.9 1.3 copy.30
  3.2 1.9 copy.31
  5.1 0.0 copy-start
  5.1 0.0 copy-start.4
  5.1 196.5 %shard_map.251 = (bf16[1,2,64,1024]{3,2,1,0:T(8,128)(2,1)}, bf16[1,2,64,1024]{3,2,1,0:T(8,128)(2,1)}, f32[4,2,16,64]{3,2,1,0:T(8,128)}, f32[16,512]{1,0:T(8,128)...) custom-call(s32[2]{0:T(128)} %valid_ref.1, bf16[1,1024]{1,0:T(2,128)(2,1)} %gain_one_in.1, bf16[1,1024]{1,0:T(2,128)(2,1)} %bias_one_in.1, ...), custom_call_target="tpu_custom_call" | custom-call | flops 7000000000 | bytes 16777216 | tf_op jit(solution)/shard_map/pallas_call | solution.py:1135
  201.6 0.0 copy-done
  201.6 0.0 copy-done.4
  201.6 0.0 copy-start.1
  201.6 0.9 copy-done.1
  202.5 0.0 copy-start.2
  202.5 0.9 copy-done.2
  203.5 0.0 copy-start.3
  203.5 0.8 copy-done.3
  204.3 0.0 copy-start.5
  204.3 0.8 copy-done.5
  205.1 0.0 copy-start.6
  205.1 0.8 copy-done.6
  205.8 0.0 copy-start.7
  205.8 0.7 copy-done.7
  206.6 3.4 %shard_map.252 = (bf16[1,2,64,1024]{3,2,1,0:T(8,128)(2,1)}, bf16[1,2,64,1024]{3,2,1,0:T(8,128)(2,1)}, bf16[1,2,10,256]{3,2,1,0:T(8,128)(2,1)S(1)}, f32[10,1024]{...) custom-call(bf16[1,2,64,1024]{3,2,1,0:T(8,128)(2,1)S(1)} %copy-done.1, ...), custom_call_target="tpu_custom_call" | custom-call | tf_op jit(solution)/shard_map/pallas_call | solution.py:1197
  210.0 0.6 copy.28
Async XLA Ops:
  5.1 196.5 %copy-start = (bf16[1024,512]{1,0:T(8,128)(2,1)S(1)}, bf16[1024,512]{1,0:T(8,128)(2,1)}, u32[]{:S(2)}) copy-start(bf16[1024,512]{1,0:T(8,128)(2,1)} %inner_in.3) | copy-start | bytes 3145732
  5.1 196.5 %copy-start.4 = (bf16[10,1024]{1,0:T(8,128)(2,1)S(1)}, bf16[10,1024]{1,0:T(8,128)(2,1)}, u32[]{:S(2)}) copy-start(bf16[10,1024]{1,0:T(8,128)(2,1)} %table_in.3) | copy-start | bytes 61444
  201.6 1.0 copy-start.1
  202.5 0.9 copy-start.2
  203.5 0.8 copy-start.3
  204.3 0.8 copy-start.5
  205.1 0.8 copy-start.6
  205.8 0.7 copy-start.7

commit v3 on v2

--- a/solution.py
+++ b/solution.py
@@ -428,12 +428,8 @@
     reduce_in,
     inner_in,
     outer_in,
-    lo_out,
-    ig_out,
-    pg_out,
-    hidden_out,
-    act_out,
-    prefix_out,
+    rows_out,
+    parts_out,
     vec,
     tbias,
     triple_own,
@@ -456,6 +452,9 @@
     dm,
     gi_send,
     gi_recv,
+    y_relay,
+    gi_relay,
+    gh_relay,
     z_one,
     inv_one,
     z_two,
@@ -480,6 +479,7 @@
     pg_all,
     table_pad,
     inner_w,
+    outer_raw,
     outer_w,
     hid_part,
     hid_recv,
@@ -488,7 +488,9 @@
     send_sem,
     recv_sem,
     local_sem,
+    phase_sem,
 ):
+    lo_out, ig_out = rows_out.at[0], rows_out.at[1]
     s = lax.axis_index("section")
     t = lax.axis_index("tensor")
     d = lax.axis_index("dp")
@@ -535,6 +537,20 @@
         copy.start()
         return copy
 
+    outer = (t == 0) | (t == nt - 1)
+    inner = jnp.logical_not(outer)
+    across = lax.rem(t + 2, nt)
+    beside = t + 1 - 2 * lax.rem(t, 2)
+
+    def far(k):
+        return ((t == 0) & (k == nt - 1)) | ((t == nt - 1) & (k == 1))
+
+    def unheard(k):
+        return ((t == 0) & (k == 1)) | ((t == nt - 1) & (k == nt - 1))
+
+    def near(k):
+        return jnp.logical_not(far(k))
+
     def plane(k):
         return lax.rem(t + k, nt)
 
@@ -551,7 +567,7 @@
     load_x = lcopy(x_in.at[s], xs.at[0, t])
     load_triple = lcopy(triple_in, triple_own)
     load_inner = lcopy(inner_in, inner_w)
-    load_outer = lcopy(outer_in, outer_w)
+    load_outer = lcopy(outer_in, outer_raw)
     load_mixer = lcopy(mixer_in, wm.at[s, pl.ds(pl.multiple_of(t * z.local_width, 256), z.local_width)])
     load_expand = lcopy(expand_in, we.at[s])
     load_reduce = lcopy(reduce_in, wr.at[s])
@@ -568,16 +584,36 @@
     table_pad[...] = jnp.zeros_like(table_pad)
     table_pad[0 : z.prefix_rows, :] = table_in[...].astype(f32)
 
+    for layer in range(2):
+        for k in (1, nt - 1):
+
+            @pl.when(unheard(k))
+            def _():
+                y_recv[layer, k] = jnp.zeros((rows, z.width), bf16)
+                gi_recv[layer, k] = jnp.zeros((rows, z.width), bf16)
+
+        @pl.when(outer)
+        def _():
+            for j in range(nb):
+                gh[layer, (nt - 1 - t) * nb + j] = jnp.zeros((HD, brows), bf16)
+            gh_relay[layer] = jnp.zeros((nb, HD, brows), bf16)
+
     pl.semaphore_wait(barrier, cells)
 
-    def spread(src, buf, layer):
-        first = claim("recv", nt)
-        for k in range(1, nt):
-            push(src, buf.at[layer, t], first + k, (s, plane(k), d))
+    def spread(src, buf, layer, first=None, when=None):
+        if first is None:
+            first = claim("recv", nt)
+        for k in (2, 1, 3):
+            go = near(k) if when is None else near(k) & when
+            push(src, buf.at[layer, t], first + k, (s, plane(k), d), go)
         return first
 
+    def spread_relay(buf, layer, first):
+        arrived(buf.at[layer, across], first + 2, inner)
+        push(buf.at[layer, across], buf.at[layer, across], first + 2 * t - 1, (s, beside, d), inner)
+
     def spread_wait(buf, layer, first, k):
-        arrived(buf.at[layer, plane(nt - k)], first + k)
+        arrived(buf.at[layer, plane(nt - k)], first + k, outer if k == 2 else None)
 
     x_first = [None, None]
     gy_first = [None, None]
@@ -640,12 +676,15 @@
     push(wq.at[s], wq.at[s], wq_first, sib)
     load_inner.wait()
     inner_act = jnp.tanh(
-        dot_nn(table_pad[...].astype(bf16), inner_w[...]) + inner_bias_in[...].astype(f32)
-    )
-    act_out[...] = inner_act
+        dot_nn(table_pad[...].astype(bf16), inner_w[...]) + inner_bias_in[...].reshape(1, z.inner).astype(f32)
+    )
+    parts_out[0] = inner_act
     load_outer.wait()
-    prefix = (dot_nn(inner_act.astype(bf16), outer_w[...]) + outer_bias_in[...].astype(f32)).astype(bf16)
-    prefix_out[...] = prefix
+    for c in range(2):
+        outer_w[:, c * z.local_width : (c + 1) * z.local_width] = outer_raw[:, c, :]
+    outer_shift = jnp.concatenate([outer_bias_in[0, 0:1, :], outer_bias_in[0, 1:2, :]], axis=1)
+    prefix = (dot_nn(inner_act.astype(bf16), outer_w[...]) + outer_shift.astype(f32)).astype(bf16)
+    parts_out[1] = prefix.astype(f32)
     for c in range(2):
         for j in range(nb):
             at = c * z.local_width + j * HD
@@ -763,7 +802,7 @@
             out_t[layer, b] = result
             low = result.astype(bf16)
             ot_send[layer, b] = low
-            for k in range(nt):
+            for k in (2, 1, 3, 0):
                 if k == 0:
                     push(ot_send.at[layer, b], att.at[layer, me], out_first + me, (s, t, b), d != b)
 
@@ -771,15 +810,22 @@
                     def _():
                         att[layer, me] = low
                 else:
-                    push(ot_send.at[layer, b], att.at[layer, me], out_first + me, (s, plane(k), b))
+                    push(
+                        ot_send.at[layer, b], att.at[layer, me], out_first + me, (s, plane(k), b), near(k)
+                    )
         return out_first
 
-    def cells_wait(buf, layer, first):
+    def att_relay(layer, first):
+        for j in range(nb):
+            cell = across * nb + j
+            arrived(att.at[layer, cell], first + cell, inner)
+            push(att.at[layer, cell], att.at[layer, cell], first + cell, (s, beside, d), inner)
+
+    def mixer_rows(layer, first):
+        att_relay(layer, first)
         for cell in range(cells):
-            arrived(buf.at[layer, cell], first + cell, me != cell)
-
-    def mixer_rows(layer, first):
-        cells_wait(att, layer, first)
+            seen = inner & (across == cell // nb)
+            arrived(att.at[layer, cell], first + cell, (me != cell) & jnp.logical_not(seen))
         for p in range(nt):
             joined = att[layer, p * nb : (p + 1) * nb].reshape(nb * HD, brows)
             wide[:, p * nb * HD : (p + 1) * nb * HD] = joined.T
@@ -812,20 +858,35 @@
             y_send[layer, :, :, pl.ds(at, tile)] = part.astype(bf16).reshape(nt, rows, tile)
 
         tiles(z.width, some)
-        first = claim("recv", nt)
-        for k in range(1, nt):
-            push(y_send.at[layer, plane(k)], y_recv.at[layer, k], first + k, (s, plane(k), d))
+        return scatter(layer, y_send, y_recv, y_relay, total)
+
+    def scatter(layer, out, back, relay, full):
+        first = claim("recv", nt + 1)
+        push(out.at[layer, nt - 1 - t], relay.at[layer], first + nt, (s, beside, d), outer)
+        for k in (2, 1, 3):
+            go = near(k) if k != 2 else outer
+            push(out.at[layer, plane(k)], back.at[layer, k], first + k, (s, plane(k), d), go)
+        arrived(relay.at[layer], first + nt, inner)
+
+        @pl.when(inner)
+        def _():
+            where = pl.ds(pl.multiple_of(across * rows, rows), rows)
+            out[layer, across] = (full[where, :] + relay[layer].astype(f32)).astype(bf16)
+
+        push(out.at[layer, across], back.at[layer, 2], first + 2, (s, across, d), inner)
         return first
+
+    def scatter_wait(layer, back, first, result):
+        for k in (1, 3, 2):
+            arrived(back.at[layer, k], first + k, jnp.logical_not(unheard(k)))
+            result = result + back[layer, k].astype(f32)
+        return result
 
     def own_rows(ref):
         return ref[pl.ds(pl.multiple_of(t * rows, rows), rows), :]
 
     def output_sum(layer, first, base):
-        result = base
-        for k in range(1, nt):
-            arrived(y_recv.at[layer, k], first + k)
-            result = result + y_recv[layer, k].astype(f32)
-        return result.astype(bf16)
+        return scatter_wait(layer, y_recv, first, base).astype(bf16)
 
     out_sem = claim("recv", 4)
     out_loads = []
@@ -843,8 +904,10 @@
     for layer in range(2):
         if layer == 0:
             load_x.wait()
+
         norm_one(layer, t)
-        for k in range(1, nt):
+        spread_relay(xs, layer, x_first[layer])
+        for k in (2, 1, 3):
             spread_wait(xs, layer, x_first[layer], k)
             norm_one(layer, plane(nt - k))
         if layer == 0:
@@ -912,13 +975,20 @@
 
     def grad_to_heads(layer):
         first = claim("recv", cells)
-        for k in range(1, nt + 1):
+        relay_sem = claim("recv", 1)
+        for k in (3, 1, 2, 4):
             p = plane(k)
             here = wm[layer, pl.ds(pl.multiple_of(p * z.local_width, z.local_width), z.local_width), :]
             part = dot_nt(here, normed[...]).astype(bf16).reshape(nb, HD, brows)
+            if k == 2:
+                arrived(gh_relay.at[layer], relay_sem, inner)
+                met = jnp.where(inner, gh_relay[layer].astype(f32), 0.0)
+                part = (part.astype(f32) + met).astype(bf16)
             gh_send[layer, k - 1] = part
+            if k != 2 and k < nt:
+                push(gh_send.at[layer, k - 1], gh_relay.at[layer], relay_sem, (s, beside, d), far(k))
             for j in range(nb):
-                away = None if k < nt else d != j
+                away = near(k) if k < nt else d != j
                 push(gh_send.at[layer, k - 1, j], gh.at[layer, me], first + me, (s, p, j), away)
                 if k == nt:
 
@@ -929,7 +999,9 @@
         return first
 
     def attend_back(layer, first):
-        cells_wait(gh, layer, first)
+        for cell in range(cells):
+            seen = outer & (t + cell // nb == nt - 1)
+            arrived(gh.at[layer, cell], first + cell, (me != cell) & jnp.logical_not(seen))
         out_first = claim("recv", nb)
         pre_values = pre[layer, 1, d]
         pre_keys = pre[layer, 0, d].T
@@ -994,19 +1066,13 @@
             return 0
 
         lax.fori_loop(0, brows // step, pull, 0, unroll=True)
-        recv = claim("recv", nt)
-        for k in range(1, nt):
-            push(gi_send.at[layer, plane(k)], gi_recv.at[layer, k], recv + k, (s, plane(k), d))
-        return recv
+        return scatter(layer, gi_send, gi_recv, gi_relay, grad_res)
 
     def grad_sum(layer, first):
-        result = own_rows(grad_res)
-        for k in range(1, nt):
-            arrived(gi_recv.at[layer, k], first + k)
-            result = result + gi_recv[layer, k].astype(f32)
-        return result.astype(bf16)
+        return scatter_wait(layer, gi_recv, first, own_rows(grad_res)).astype(bf16)
 
     for layer in (1, 0):
+        spread_relay(gys, layer, gy_first[layer])
         for k in range(1, nt):
             spread_wait(gys, layer, gy_first[layer], k)
         grad_hidden(layer)
@@ -1033,7 +1099,9 @@
         else:
             for k in range(1, nb):
                 arrived(pg_all.at[block(nb - k)], all_first + k)
-            pg_out[...] = pg_all[...]
+            for c in range(2):
+                joined = jnp.concatenate([pg_all[j, c] for j in range(nb)], axis=1)
+                parts_out[2, :, c * z.local_width : (c + 1) * z.local_width] = joined
             part = jnp.zeros((z.prefix_pad, z.inner), f32)
             for j in range(nb):
                 for c in range(2):
@@ -1056,7 +1124,7 @@
             part = hid_all[0]
             for p in range(1, nt):
                 part = part + hid_all[p]
-            hidden_out[...] = part
+            parts_out[3] = part
 
     for index, (out, layer) in enumerate(((lo_out, 0), (lo_out, 1), (ig_out, 1), (ig_out, 0))):
         arrived(out.at[0, 1 - s], out_sem + index, s == layer)
@@ -1099,6 +1167,9 @@
         V((2, nb, 3 * HD, brows), bf16),
         V((2, nt, rows, width), bf16),
         V((2, nt, rows, width), bf16),
+        V((2, rows, width), bf16),
+        V((2, rows, width), bf16),
+        V((2, nb, HD, brows), bf16),
         V((2, brows, width), f32),
         V((2, brows, 1), f32),
         V((2, brows, width), f32),
@@ -1123,6 +1194,7 @@
         V((nb, 2, z.prefix_pad, HD), f32),
         V((z.prefix_pad, width), f32),
         V((width, z.inner), bf16),
+        V((z.inner, 2, z.local_width), bf16),
         V((z.inner, 2 * z.local_width), bf16),
         V((z.prefix_pad, z.inner), f32),
         V((z.prefix_pad, z.inner), f32),
@@ -1131,21 +1203,18 @@
         pltpu.SemaphoreType.DMA((200,)),
         pltpu.SemaphoreType.DMA((200,)),
         pltpu.SemaphoreType.DMA((20,)),
+        pltpu.SemaphoreType.REGULAR,
     ]
     return pl.pallas_call(
         partial(both_layers, z),
         out_shape=(
-            jax.ShapeDtypeStruct((1, 2, rows, width), bf16),
-            jax.ShapeDtypeStruct((1, 2, rows, width), bf16),
-            jax.ShapeDtypeStruct((nb, 2, z.prefix_pad, HD), f32),
-            jax.ShapeDtypeStruct((z.prefix_pad, z.inner), f32),
-            jax.ShapeDtypeStruct((z.prefix_pad, z.inner), f32),
-            jax.ShapeDtypeStruct((z.prefix_pad, 2 * z.local_width), bf16),
+            jax.ShapeDtypeStruct((2, 1, 2, rows, width), bf16),
+            jax.ShapeDtypeStruct((4, z.prefix_pad, z.inner), f32),
         ),
         in_specs=[pl.BlockSpec(memory_space=pltpu.SMEM)]
         + [pl.BlockSpec(memory_space=pltpu.VMEM)] * (len(small) - 1)
         + [any_space] * len(large),
-        out_specs=(any_space,) * 2 + (pl.BlockSpec(memory_space=pltpu.VMEM),) * 4,
+        out_specs=(any_space, pl.BlockSpec(memory_space=pltpu.VMEM)),
         scratch_shapes=scratch,
         compiler_params=pltpu.CompilerParams(
             collective_id=0, has_side_effects=True, vmem_limit_bytes=60 * 2**20
@@ -1157,19 +1226,19 @@
 
 
 def prefix_end(
-    z, lo_in, ig_in, pg_in, hidden_in, act_in, prefix_in, table_in, inner_in,
+    z, rows_in, parts_in, table_in, inner_in,
     lo_out, ig_out, states_out, table_out, inner_out, inner_bias_out, outer_out, outer_bias_out,
     table_pad, sems,
 ):
     copies = [
-        pltpu.make_async_copy(lo_in, lo_out, sems.at[0]),
-        pltpu.make_async_copy(ig_in, ig_out, sems.at[1]),
+        pltpu.make_async_copy(rows_in.at[0], lo_out, sems.at[0]),
+        pltpu.make_async_copy(rows_in.at[1], ig_out, sems.at[1]),
     ]
     for copy in copies:
         copy.start()
     count, width = z.prefix_rows, z.local_width
-    act = act_in[...]
-    inner_grad = hidden_in[...] * (1.0 - act * act)
+    act = parts_in[0]
+    inner_grad = parts_in[3] * (1.0 - act * act)
     inner_bias_out[...] = jnp.sum(inner_grad, axis=0, keepdims=True)
     table_pad[...] = jnp.zeros_like(table_pad)
     table_pad[0:count, :] = table_in[...].astype(f32)
@@ -1180,8 +1249,9 @@
     table_out[...] = (dot_nt(high, inner_in[...]) + dot_nt(low, inner_in[...]))[0:count]
     act_turned = act.T.astype(bf16)
     for c in range(2):
-        states_out[0, c] = prefix_in[0:count, c * width : (c + 1) * width]
-        total = jnp.concatenate([pg_in[j, c] for j in range(z.blocks)], axis=1)
+        at = slice(c * width, (c + 1) * width)
+        states_out[:, c, :] = parts_in[1, 0:count, at].astype(bf16)
+        total = parts_in[2, :, at]
         high = total.astype(bf16)
         low = (total - high.astype(f32)).astype(bf16)
         outer_out[:, c, :] = dot_nn(act_turned, high) + dot_nn(act_turned, low)
@@ -1190,27 +1260,27 @@
         copy.wait()
 
 
-def finish(z, layer_outputs, input_grads, parts, hidden, act, prefix, table, inner_weight):
+def finish(z, both_rows, parts, table, inner_weight):
     any_space = pl.BlockSpec(memory_space=pl.ANY)
     whole = pl.BlockSpec(memory_space=pltpu.VMEM)
-    rows = jax.ShapeDtypeStruct(layer_outputs.shape, bf16)
+    rows = jax.ShapeDtypeStruct(both_rows.shape[1:], bf16)
     return pl.pallas_call(
         partial(prefix_end, z),
         out_shape=(
             rows,
             rows,
-            jax.ShapeDtypeStruct((1, 2, z.prefix_rows, z.local_width), bf16),
+            jax.ShapeDtypeStruct((z.prefix_rows, 2, z.local_width), bf16),
             jax.ShapeDtypeStruct((z.prefix_rows, z.width), f32),
             jax.ShapeDtypeStruct((z.width, z.inner), f32),
             jax.ShapeDtypeStruct((1, z.inner), f32),
             jax.ShapeDtypeStruct((z.inner, 2, z.local_width), f32),
             jax.ShapeDtypeStruct((1, 2, z.local_width), f32),
         ),
-        in_specs=[any_space] * 2 + [whole] * 6,
+        in_specs=[any_space] + [whole] * 3,
         out_specs=(any_space,) * 2 + (whole,) * 6,
         scratch_shapes=[pltpu.VMEM((z.prefix_pad, z.width), f32), pltpu.SemaphoreType.DMA((2,))],
         compiler_params=pltpu.CompilerParams(vmem_limit_bytes=32 * 2**20),
-    )(layer_outputs, input_grads, parts, hidden, act, prefix, table, inner_weight)
+    )(both_rows, parts, table, inner_weight)
 
 
 def head_a_device(
@@ -1249,7 +1319,6 @@
     )
     z.prefix_pad = -(-prefix_rows // 16) * 16
     z.inner = inner_weight.shape[1]
-    outer_local = outer_weight[:, 0].reshape(outer_weight.shape[0], 2 * local_width)
     small = (
         valid_len,
         first_gain,
@@ -1261,8 +1330,8 @@
         expand_bias,
         reduce_bias,
         prefix_table,
-        inner_bias.reshape(1, -1),
-        outer_bias.reshape(1, -1),
+        inner_bias,
+        outer_bias,
     )
     large = (
         block_input,
@@ -1272,7 +1341,7 @@
         expand_weight[0],
         reduce_weight[0],
         inner_weight,
-        outer_local,
+        outer_weight[:, 0],
     )
     results = finish(z, *run_layers(z, small, large), prefix_table, inner_weight)
     (
@@ -1288,7 +1357,7 @@
     return (
         layer_outputs,
         input_grads,
-        prefix_states,
+        prefix_states.transpose(1, 0, 2)[None],
         table_grad,
         inner_weight_grad,
         inner_bias_grad.reshape(-1),

time: 214 us -> 190 us (0.89); the launches traced: 211 us -> 189 us
  Pallas kernels: 200 us -> 186 us
  local copies, waits for them, and re-layouts: 10 us -> 1.95 us
    pallas_call x1, Pallas kernels: 196 us -> 183 us  [run_layers(): pl.pallas_call(partial(both_layers, z), out_shape=(jax.ShapeDtypeStruct((...]
    unnamed x19 -> x8, local copies, waits for them, and re-layouts: 8.76 us -> 1.95 us
where the time goes in v3:
time: 190 us; the launch traced here: 189 us
  Pallas kernels  186 us (98%)
  local copies, waits for them, and re-layouts  1.95 us (1%)
    pallas_call x1, Pallas kernels, run_layers(): pl.pallas_call(partial(both_layers, z), out_shape=(jax.ShapeDtypeStruct((...  183 us

profile of v3, /device:TPU:1, one launch (start us, length us, event | category | flops | bytes accessed | tf_op | source)
XLA Modules:
  0.0 189.3 jit_solution(7132091524208050811)
XLA Ops:
  0.6 0.0 copy-start
  0.7 0.0 copy-start.3
  0.7 183.0 %shard_map.251 = (bf16[2,1,2,64,1024]{4,3,2,1,0:T(8,128)(2,1)}, f32[4,16,512]{2,1,0:T(8,128)}) custom-call(s32[2]{0:T(128)} %valid_ref.1, bf16[1,1024]{1,0:T(2,128)(2,1)} %gain_one_in.1, bf16[1,1024]{1,0:T(2,128)(2,1)} %bias_one_in.1, bf16[1,3,256]{2,1,0:T(4,128)(2,1)} %triple_bias_in.1, bf16[1,1024]{1,0:T(2,128)(2,1)} %mixer_bias_in.1, ...), custom_call_target="tpu_custom_call" | custom-call | flops 7000000000 | bytes 16777216 | tf_op jit(solution)/shard_map/pallas_call | solution.py:1208
  183.7 0.0 copy-done
  183.7 0.0 copy-done.3
  183.7 0.0 copy-start.1
  183.7 1.0 copy-done.1
  184.7 0.0 copy-start.2
  184.7 0.9 copy-done.2
  185.6 3.4 %shard_map.252 = (bf16[1,2,64,1024]{3,2,1,0:T(8,128)(2,1)}, bf16[1,2,64,1024]{3,2,1,0:T(8,128)(2,1)}, bf16[10,2,256]{2,1,0:T(2,128)(2,1)}, f32[10,1024]{1,0:T(8,...) custom-call(bf16[2,1,2,64,1024]{4,3,2,1,0:T(8,128)(2,1)S(1)} %copy-done.1, ...), custom_call_target="tpu_custom_call" | custom-call | tf_op jit(solution)/shard_map/pallas_call | solution.py:1267
Async XLA Ops:
  0.6 183.0 %copy-start = (bf16[1024,512]{1,0:T(8,128)(2,1)S(1)}, bf16[1024,512]{1,0:T(8,128)(2,1)}, u32[]{:S(2)}) copy-start(bf16[1024,512]{1,0:T(8,128)(2,1)} %inner_in.3) | copy-start | bytes 3145732
  0.7 183.0 %copy-start.3 = (bf16[10,1024]{1,0:T(8,128)(2,1)S(1)}, bf16[10,1024]{1,0:T(8,128)(2,1)}, u32[]{:S(2)}) copy-start(bf16[10,1024]{1,0:T(8,128)(2,1)} %table_in.3) | copy-start | bytes 61444
  183.7 1.0 copy-start.1
  184.7 0.9 copy-start.2

commit v4 on v3

--- a/solution.py
+++ b/solution.py
@@ -460,8 +460,15 @@
     z_two,
     inv_two,
     gelu_grad,
-    probs,
-    probs_pre,
+    upper,
+    expons_low,
+    expons_pre,
+    scales,
+    dscores,
+    dscores_pre,
+    values_n,
+    queries_n,
+    grads_n,
     out_t,
     keys_n,
     normed,
@@ -469,9 +476,8 @@
     total,
     grad_res,
     resid,
-    dkeys,
-    dvalues,
     y_last,
+    active_last,
     gi_own,
     pg,
     pg_recv,
@@ -573,6 +579,53 @@
     load_reduce = lcopy(reduce_in, wr.at[s])
     load_gy = lcopy(gy_in.at[s], gys.at[1, t])
 
+    for layer in range(2):
+        for k in (1, nt - 1):
+
+            @pl.when(unheard(k))
+            def _():
+                y_recv[layer, k] = jnp.zeros((rows, z.width), bf16)
+                gi_recv[layer, k] = jnp.zeros((rows, z.width), bf16)
+
+        @pl.when(outer)
+        def _():
+            for j in range(nb):
+                gh[layer, (nt - 1 - t) * nb + j] = jnp.zeros((HD, brows), bf16)
+
+    pl.semaphore_wait(barrier, cells)
+
+    half = rows // 2
+
+    def parts_of(ref):
+        return ref.at[pl.ds(0, half)], ref.at[pl.ds(half, half)]
+
+    def spread(src, buf, layer):
+        first = claim("recv", nt + 2)
+        for i, (one, goal) in enumerate(zip(parts_of(src), parts_of(buf.at[layer, t]))):
+            push(one, goal, first + (2, nt)[i], (s, across, d), outer)
+        push(src, buf.at[layer, t], first + 2, (s, across, d), inner)
+        for k in (1, 3):
+            push(src, buf.at[layer, t], first + k, (s, plane(k), d), near(k))
+        return first
+
+    def spread_relay(buf, layer, first):
+        for i, one in enumerate(parts_of(buf.at[layer, across])):
+            arrived(one, first + (2, nt)[i], inner)
+            push(one, one, first + (2 * t - 1, nt + 1)[i], (s, beside, d), inner)
+
+    def spread_wait(buf, layer, first, k):
+        unit = buf.at[layer, plane(nt - k)]
+        if k == 2:
+            arrived(unit, first + k, outer)
+        else:
+            arrived(unit, first + k, jnp.logical_not(unheard(k)))
+            for i, one in enumerate(parts_of(unit)):
+                arrived(one, first + (k, nt + 1)[i], unheard(k))
+
+    x_first = [None, None]
+    gy_first = [None, None]
+    x_first[0] = spread(x_in.at[s], xs, 0)
+
     for index, ref in enumerate(
         (gain_one_in, bias_one_in, mixer_bias_in, gain_two_in, bias_two_in, reduce_bias_in, expand_bias_in)
     ):
@@ -584,40 +637,6 @@
     table_pad[...] = jnp.zeros_like(table_pad)
     table_pad[0 : z.prefix_rows, :] = table_in[...].astype(f32)
 
-    for layer in range(2):
-        for k in (1, nt - 1):
-
-            @pl.when(unheard(k))
-            def _():
-                y_recv[layer, k] = jnp.zeros((rows, z.width), bf16)
-                gi_recv[layer, k] = jnp.zeros((rows, z.width), bf16)
-
-        @pl.when(outer)
-        def _():
-            for j in range(nb):
-                gh[layer, (nt - 1 - t) * nb + j] = jnp.zeros((HD, brows), bf16)
-            gh_relay[layer] = jnp.zeros((nb, HD, brows), bf16)
-
-    pl.semaphore_wait(barrier, cells)
-
-    def spread(src, buf, layer, first=None, when=None):
-        if first is None:
-            first = claim("recv", nt)
-        for k in (2, 1, 3):
-            go = near(k) if when is None else near(k) & when
-            push(src, buf.at[layer, t], first + k, (s, plane(k), d), go)
-        return first
-
-    def spread_relay(buf, layer, first):
-        arrived(buf.at[layer, across], first + 2, inner)
-        push(buf.at[layer, across], buf.at[layer, across], first + 2 * t - 1, (s, beside, d), inner)
-
-    def spread_wait(buf, layer, first, k):
-        arrived(buf.at[layer, plane(nt - k)], first + k, outer if k == 2 else None)
-
-    x_first = [None, None]
-    gy_first = [None, None]
-    x_first[0] = spread(x_in.at[s], xs, 0)
 
     small = claim("recv", 3)
     push(vec.at[s], vec.at[s], small, sib)
@@ -743,6 +762,9 @@
 
         lax.fori_loop(0, count // tile, some, 0, unroll=True)
 
+    def positions(ref, b):
+        return ref.at[:, pl.ds(pl.multiple_of(b * brows, brows), brows)]
+
     def project(layer):
         first = claim("recv", nb)
         for k in range(1, nb + 1):
@@ -752,9 +774,9 @@
             part = (part + jnp.concatenate([shift, shift], axis=1)).astype(bf16)
             if k < nb:
                 qkv_send[layer, k] = part
-                push(qkv_send.at[layer, k], qkv.at[layer, d], first + k, (s, t, head))
+                push(qkv_send.at[layer, k], positions(qkv.at[layer], d), first + k, (s, t, head))
             else:
-                qkv[layer, d] = part
+                qkv[layer, :, pl.ds(pl.multiple_of(d * brows, brows), brows)] = part
         return first
 
     def attend(layer, first):
@@ -765,40 +787,41 @@
         key_at = lax.broadcasted_iota(jnp.int32, (brows, brows), 0)
         query_at = lax.broadcasted_iota(jnp.int32, (brows, brows), 1)
         valid = valid_ref[s]
-        number = 0
         for b in range(nb):
-            arrived(qkv.at[layer, b], first + lax.rem(d + nb - b, nb), d != b)
-            keys_n[layer, b] = qkv[layer, b, HD : 2 * HD, :].T
-            queries = (qkv[layer, b, 0:HD, :].astype(f32) * HD ** (-0.5)).astype(bf16)
-            scores = dot_nn(pre_keys, queries)
-            scores = jnp.where(prefix_row < z.prefix_rows, scores, masked_score)
-            probs_pre[layer, b] = scores
-            peak = jnp.max(scores, axis=0, keepdims=True)
-            for kb in range(b + 1):
-                scores = dot_nn(keys_n[layer, kb], queries)
+            here = slice(b * brows, (b + 1) * brows)
+            arrived(positions(qkv.at[layer], b), first + lax.rem(d + nb - b, nb), d != b)
+            keys_n[layer, here] = qkv[layer, HD : 2 * HD, here].T
+            queries = (qkv[layer, 0:HD, here].astype(f32) * HD ** (-0.5)).astype(bf16)
+
+            def scores_of(kb):
+                scores = dot_nn(keys_n[layer, kb * brows : (kb + 1) * brows], queries)
                 if kb == b:
                     seen = key_at <= query_at
                     if b == nb - 1:
                         seen = seen & (key_at + b * brows < valid)
                     scores = jnp.where(seen, scores, masked_score)
-                probs[layer, number + kb] = scores
-                peak = jnp.maximum(peak, jnp.max(scores, axis=0, keepdims=True))
-            expons = jnp.exp(probs_pre[layer, b] - peak)
-            probs_pre[layer, b] = expons
+                return scores
+
+            pre_scores = dot_nn(pre_keys, queries)
+            pre_scores = jnp.where(prefix_row < z.prefix_rows, pre_scores, masked_score)
+            peak = jnp.max(pre_scores, axis=0, keepdims=True)
+            for kb in range(b + 1):
+                peak = jnp.maximum(peak, jnp.max(scores_of(kb), axis=0, keepdims=True))
+            expons = jnp.exp(pre_scores - peak)
+            expons_pre[layer, :, here] = expons
             denominator = jnp.sum(expons, axis=0, keepdims=True)
             for kb in range(b + 1):
-                expons = jnp.exp(probs[layer, number + kb] - peak)
-                probs[layer, number + kb] = expons
+                expons = jnp.exp(scores_of(kb) - peak)
                 denominator = denominator + jnp.sum(expons, axis=0, keepdims=True)
+                expons_low[layer, kb * brows : (kb + 1) * brows, here] = expons.astype(bf16)
             scale = 1.0 / denominator
-            prob = probs_pre[layer, b] * scale
-            probs_pre[layer, b] = prob
-            result = dot_nn(pre_values, prob.astype(bf16))
-            for kb in range(b + 1):
-                prob = probs[layer, number + kb] * scale
-                probs[layer, number + kb] = prob
-                result = result + dot_nn(qkv[layer, kb, 2 * HD : 3 * HD, :], prob.astype(bf16))
-            number += b + 1
+            scales[layer, b] = scale
+            seen_keys = (b + 1) * brows
+            result = dot_nn(
+                qkv[layer, 2 * HD : 3 * HD, :seen_keys], expons_low[layer, :seen_keys, here]
+            )
+            result = result + dot_nn(pre_values, expons_pre[layer, :, here].astype(bf16))
+            result = result * scale
             out_t[layer, b] = result
             low = result.astype(bf16)
             ot_send[layer, b] = low
@@ -826,6 +849,9 @@
         for cell in range(cells):
             seen = inner & (across == cell // nb)
             arrived(att.at[layer, cell], first + cell, (me != cell) & jnp.logical_not(seen))
+        if layer == 0:
+            mix_three(0)
+        arrived(wm.at[layer], mix_third[layer], s != layer)
         for p in range(nt):
             joined = att[layer, p * nb : (p + 1) * nb].reshape(nb * HD, brows)
             wide[:, p * nb * HD : (p + 1) * nb * HD] = joined.T
@@ -837,48 +863,68 @@
 
         tiles(z.width, some)
 
-    def feed_first(layer):
+    def grad_active():
+        def some(at):
+            last = gys[1].reshape(brows, z.width)
+            upper[:, pl.ds(at, tile)] = dot_nt(last, wr[1, pl.ds(at, tile), :])
+
+        tiles(z.hidden, some)
+
+    def feed_first(layer, active):
         def some(at):
             v = dot_nn(normed[...], we[layer, :, pl.ds(at, tile)]) + vec[layer, 6:7, pl.ds(at, tile)]
             root = 0.7978845608028654
             square = v * v
             th = jnp.tanh(root * v * (1.0 + 0.044715 * square))
             half = 0.5 * (1.0 + th)
-            wide[:, pl.ds(at, tile)] = (v * half).astype(bf16)
-            gelu_grad[layer, :, pl.ds(at, tile)] = half + (0.5 * root) * v * (1.0 - th * th) * (
-                1.0 + 3.0 * 0.044715 * square
-            )
+            active[:, pl.ds(at, tile)] = (v * half).astype(bf16)
+            slope = half + (0.5 * root) * v * (1.0 - th * th) * (1.0 + 3.0 * 0.044715 * square)
+            if layer == 0:
+                gelu_grad[:, pl.ds(at, tile)] = slope
+            else:
+                wide[:, pl.ds(at, tile)] = (upper[:, pl.ds(at, tile)] * slope).astype(bf16)
 
         tiles(z.hidden, some)
 
-    def feed_second(layer):
+    def feed_second(layer, active):
         def some(at):
-            part = dot_nn(wide[...], wr[layer, :, pl.ds(at, tile)])
+            part = dot_nn(active[...], wr[layer, :, pl.ds(at, tile)])
             total[:, pl.ds(at, tile)] = part
             y_send[layer, :, :, pl.ds(at, tile)] = part.astype(bf16).reshape(nt, rows, tile)
 
         tiles(z.width, some)
-        return scatter(layer, y_send, y_recv, y_relay, total)
-
-    def scatter(layer, out, back, relay, full):
-        first = claim("recv", nt + 1)
-        push(out.at[layer, nt - 1 - t], relay.at[layer], first + nt, (s, beside, d), outer)
+        return scatter(layer, y_send, y_recv, y_relay)
+
+    def scatter(layer, out, back, relay):
+        first = claim("recv", nt + 3)
+        for i, (one, goal) in enumerate(zip(parts_of(out.at[layer, nt - 1 - t]), parts_of(relay.at[layer]))):
+            push(one, goal, first + nt + i, (s, beside, d), outer)
         for k in (2, 1, 3):
             go = near(k) if k != 2 else outer
             push(out.at[layer, plane(k)], back.at[layer, k], first + k, (s, plane(k), d), go)
-        arrived(relay.at[layer], first + nt, inner)
-
-        @pl.when(inner)
-        def _():
-            where = pl.ds(pl.multiple_of(across * rows, rows), rows)
-            out[layer, across] = (full[where, :] + relay[layer].astype(f32)).astype(bf16)
-
-        push(out.at[layer, across], back.at[layer, 2], first + 2, (s, across, d), inner)
         return first
+
+    def scatter_relay(layer, out, back, relay, full, first):
+        for i in range(2):
+            arrived(parts_of(relay.at[layer])[i], first + nt + i, inner)
+
+            @pl.when(inner)
+            def _():
+                at = pl.ds(i * half, half)
+                where = pl.ds(pl.multiple_of(across * rows + i * half, half), half)
+                out[layer, across, at] = (full[where, :] + relay[layer, at].astype(f32)).astype(bf16)
+
+            one, goal = parts_of(out.at[layer, across])[i], parts_of(back.at[layer, 2])[i]
+            push(one, goal, first + (2, nt + 2)[i], (s, across, d), inner)
 
     def scatter_wait(layer, back, first, result):
         for k in (1, 3, 2):
-            arrived(back.at[layer, k], first + k, jnp.logical_not(unheard(k)))
+            if k == 2:
+                arrived(back.at[layer, k], first + k, inner)
+                for i, one in enumerate(parts_of(back.at[layer, k])):
+                    arrived(one, first + (2, nt + 2)[i], outer)
+            else:
+                arrived(back.at[layer, k], first + k, jnp.logical_not(unheard(k)))
             result = result + back[layer, k].astype(f32)
         return result
 
@@ -921,6 +967,7 @@
             mix_two(0)
             mix_one(1)
         else:
+            mix_three(1)
             load_gy.wait()
             gy_first[1] = spread(gys.at[1, t], gys, 1)
         out_first = attend(layer, q_first)
@@ -929,31 +976,29 @@
                 copy.wait()
             arrived(we.at[1 - s], feed_recv)
             arrived(wr.at[1 - s], feed_recv + 1)
-            mix_three(0)
-        else:
-            mix_three(1)
-        arrived(wm.at[layer], mix_third[layer], s != layer)
+        if layer == 1:
+            spread_relay(gys, 1, gy_first[1])
+            for k in range(1, nt):
+                spread_wait(gys, 1, gy_first[1], k)
+            grad_active()
         mixer_rows(layer, out_first)
         norm_two(layer)
         y_base.append(None)
-        feed_first(layer)
-        y_first = feed_second(layer)
-        base = own_rows(resid) + own_rows(total) + row(layer, 5)
+        feed_first(layer, wide if layer == 0 else active_last)
         if layer == 0:
+            y_first = feed_second(layer, wide)
+            scatter_relay(0, y_send, y_recv, y_relay, total, y_first)
+            base = own_rows(resid) + own_rows(total) + row(layer, 5)
             mix_two(1)
             low = output_sum(0, y_first, base)
             xs[1, t] = low
             x_first[1] = spread(xs.at[1, t], xs, 1)
             put(xs.at[1, t], lo_out, 0, 0)
-        else:
-            gi_own[...] = base
-            last_first = y_first
 
     def grad_hidden(layer):
         def some(at):
-            upper = gys[layer].reshape(brows, z.width)
-            part = dot_nt(upper, wr[layer, pl.ds(at, tile), :])
-            wide[:, pl.ds(at, tile)] = (part * gelu_grad[layer, :, pl.ds(at, tile)]).astype(bf16)
+            part = dot_nt(gys[layer].reshape(brows, z.width), wr[layer, pl.ds(at, tile), :])
+            wide[:, pl.ds(at, tile)] = (part * gelu_grad[:, pl.ds(at, tile)]).astype(bf16)
 
         tiles(z.hidden, some)
 
@@ -965,8 +1010,8 @@
 
         def pull(i, _):
             at, part = norm_pull(i, z_two.at[layer], inv_two.at[layer], row(layer, 3))
-            upper = gys[layer, i // (rows // step), pl.ds(lax.rem(i, rows // step) * step, step), :]
-            part = part + upper.astype(f32) * (1.0 / nt)
+            above = gys[layer, i // (rows // step), pl.ds(lax.rem(i, rows // step) * step, step), :]
+            part = part + above.astype(f32) * (1.0 / nt)
             grad_res[pl.ds(at, step), :] = part
             normed[pl.ds(at, step), :] = part.astype(bf16)
             return 0
@@ -975,63 +1020,84 @@
 
     def grad_to_heads(layer):
         first = claim("recv", cells)
-        relay_sem = claim("recv", 1)
-        for k in (3, 1, 2, 4):
-            p = plane(k)
+        relay_sem = claim("recv", 2)
+        pairs = [pl.ds(0, nb // 2), pl.ds(nb // 2, nb - nb // 2)]
+
+        def share(p, index):
             here = wm[layer, pl.ds(pl.multiple_of(p * z.local_width, z.local_width), z.local_width), :]
             part = dot_nt(here, normed[...]).astype(bf16).reshape(nb, HD, brows)
-            if k == 2:
-                arrived(gh_relay.at[layer], relay_sem, inner)
-                met = jnp.where(inner, gh_relay[layer].astype(f32), 0.0)
-                part = (part.astype(f32) + met).astype(bf16)
-            gh_send[layer, k - 1] = part
-            if k != 2 and k < nt:
-                push(gh_send.at[layer, k - 1], gh_relay.at[layer], relay_sem, (s, beside, d), far(k))
+            gh_send[layer, index] = part
+            return part
+
+        def pass_on(p, index, when):
             for j in range(nb):
-                away = near(k) if k < nt else d != j
-                push(gh_send.at[layer, k - 1, j], gh.at[layer, me], first + me, (s, p, j), away)
-                if k == nt:
-
-                    @pl.when(d == j)
-                    def _():
-                        gh[layer, me] = part[j]
+                push(gh_send.at[layer, index, j], gh.at[layer, me], first + me, (s, p, j), when)
+
+        share(nt - 1 - t, 0)
+        for i, two in enumerate(pairs):
+            push(gh_send.at[layer, 0, two], gh_relay.at[layer, two], relay_sem + i, (s, beside, d), outer)
+        pass_on(nt - 1 - t, 0, inner)
+        share(across, 1)
+        pass_on(across, 1, outer)
+        share(beside, 2)
+        pass_on(beside, 2, None)
+        part = share(t, 3)
+        for j in range(nb):
+            push(gh_send.at[layer, 3, j], gh.at[layer, me], first + me, (s, t, j), d != j)
+
+            @pl.when(d == j)
+            def _():
+                gh[layer, me] = part[j]
+
+        for i, two in enumerate(pairs):
+            arrived(gh_relay.at[layer, two], relay_sem + i, inner)
+
+            @pl.when(inner)
+            def _():
+                met = gh_send[layer, 1, two].astype(f32) + gh_relay[layer, two].astype(f32)
+                gh_send[layer, 1, two] = met.astype(bf16)
+
+            for j in range(two.start, two.start + two.size):
+                push(gh_send.at[layer, 1, j], gh.at[layer, me], first + me, (s, across, j), inner)
 
         return first
 
     def attend_back(layer, first):
+        for b in range(nb):
+            here = slice(b * brows, (b + 1) * brows)
+            values_n[here] = qkv[layer, 2 * HD : 3 * HD, here].T
+            queries = (qkv[layer, 0:HD, here].astype(f32) * HD ** (-0.5)).astype(bf16)
+            queries_n[here] = queries.T
         for cell in range(cells):
             seen = outer & (t + cell // nb == nt - 1)
             arrived(gh.at[layer, cell], first + cell, (me != cell) & jnp.logical_not(seen))
         out_first = claim("recv", nb)
         pre_values = pre[layer, 1, d]
         pre_keys = pre[layer, 0, d].T
-        dkeys[...] = jnp.zeros_like(dkeys)
-        dvalues[...] = jnp.zeros_like(dvalues)
-        pre_dkeys = jnp.zeros((z.prefix_pad, HD), f32)
-        pre_dvalues = jnp.zeros((z.prefix_pad, HD), f32)
         for b in reversed(range(nb)):
-            number = b * (b + 1) // 2
+            here = slice(b * brows, (b + 1) * brows)
             grad = gh[layer, b].astype(f32)
             for p in range(1, nt):
                 grad = grad + gh[layer, p * nb + b].astype(f32)
             grad = grad.astype(bf16)
-            delta = jnp.sum(grad.astype(f32) * out_t[layer, b], axis=0, keepdims=True)
-            grad_n = grad.T
-            queries = (qkv[layer, b, 0:HD, :].astype(f32) * HD ** (-0.5)).astype(bf16).T
-            prob = probs_pre[layer, b]
-            dscore = (prob * (dot_nn(pre_values, grad) - delta)).astype(bf16)
-            dq = dot_nn(pre_keys, dscore)
-            pre_dkeys = pre_dkeys + dot_nn(dscore, queries)
-            pre_dvalues = pre_dvalues + dot_nn(prob.astype(bf16), grad_n)
+            scale = scales[layer, b]
+            wide_grad = grad.astype(f32)
+            delta = jnp.sum(wide_grad * out_t[layer, b], axis=0, keepdims=True)
+            grads_n[here] = (wide_grad * scale).astype(bf16).T
+            prob = expons_pre[layer, :, here] * scale
+            dscores_pre[:, here] = (prob * (dot_nn(pre_values, grad) - delta)).astype(bf16)
             for kb in range(b + 1):
-                prob = probs[layer, number + kb]
-                values = qkv[layer, kb, 2 * HD : 3 * HD, :].T
-                dscore = (prob * (dot_nn(values, grad) - delta)).astype(bf16)
-                dq = dq + dot_nn(qkv[layer, kb, HD : 2 * HD, :], dscore)
-                dkeys[kb] = dkeys[kb] + dot_nn(dscore, queries)
-                dvalues[kb] = dvalues[kb] + dot_nn(prob.astype(bf16), grad_n)
+                rows_k = slice(kb * brows, (kb + 1) * brows)
+                prob = expons_low[layer, rows_k, here].astype(f32) * scale
+                dprob = dot_nn(values_n[rows_k], grad)
+                dscores[rows_k, here] = (prob * (dprob - delta)).astype(bf16)
+            seen_keys = (b + 1) * brows
+            dq = dot_nn(qkv[layer, HD : 2 * HD, :seen_keys], dscores[:seen_keys, here])
+            dq = dq + dot_nn(pre_keys, dscores_pre[:, here])
+            dkey = dot_nn(dscores[here, b * brows :], queries_n[b * brows :])
+            dvalue = dot_nn(expons_low[layer, here, b * brows :], grads_n[b * brows :])
             joined = jnp.concatenate(
-                [dq * HD ** (-0.5), dkeys[b].T, dvalues[b].T], axis=0
+                [dq * HD ** (-0.5), dkey.T, dvalue.T], axis=0
             ).astype(bf16)
             dm_send[layer, b] = joined
             push(dm_send.at[layer, b], dm.at[layer, d], out_first + d, (s, t, b), d != b)
@@ -1040,8 +1106,8 @@
             def _():
                 dm[layer, d] = joined
 
-        pg[layer, 0] = pre_dkeys
-        pg[layer, 1] = pre_dvalues
+        pg[layer, 0] = dot_nn(dscores_pre[...], queries_n[...])
+        pg[layer, 1] = dot_nn(expons_pre[layer].astype(bf16), grads_n[...])
         return out_first
 
     def grad_rows(layer, first):
@@ -1066,22 +1132,25 @@
             return 0
 
         lax.fori_loop(0, brows // step, pull, 0, unroll=True)
-        return scatter(layer, gi_send, gi_recv, gi_relay, grad_res)
+        return scatter(layer, gi_send, gi_recv, gi_relay)
 
     def grad_sum(layer, first):
         return scatter_wait(layer, gi_recv, first, own_rows(grad_res)).astype(bf16)
 
     for layer in (1, 0):
-        spread_relay(gys, layer, gy_first[layer])
-        for k in range(1, nt):
-            spread_wait(gys, layer, gy_first[layer], k)
-        grad_hidden(layer)
+        if layer == 0:
+            spread_relay(gys, 0, gy_first[0])
+            for k in range(1, nt):
+                spread_wait(gys, 0, gy_first[0], k)
+            grad_hidden(0)
         grad_mid(layer)
         heads_first = grad_to_heads(layer)
         if layer == 1:
-            y_last[...] = output_sum(1, last_first, gi_own[...])
-            put(y_last, lo_out, 1, 1)
+            y_first = feed_second(1, active_last)
+            gi_own[...] = own_rows(resid) + own_rows(total) + row(1, 5)
         rows_first = attend_back(layer, heads_first)
+        if layer == 1:
+            scatter_relay(1, y_send, y_recv, y_relay, total, y_first)
         if layer == 0:
             sib_sem = claim("recv", 1)
             push(pg.at[1 - s], pg_recv, sib_sem, sib)
@@ -1093,6 +1162,9 @@
             pg_all[d] = pg_sum[...]
         grads_first = grad_rows(layer, rows_first)
         if layer == 1:
+            scatter_relay(1, gi_send, gi_recv, gi_relay, grad_res, grads_first)
+            y_last[...] = output_sum(1, y_first, gi_own[...])
+            put(y_last, lo_out, 1, 1)
             gys[0, t] = grad_sum(1, grads_first)
             gy_first[0] = spread(gys.at[0, t], gys, 0)
             put(gys.at[0, t], ig_out, 1, 2)
@@ -1116,6 +1188,7 @@
             for k in range(1, nt):
                 push(hid_pair, hid_all.at[t], hid_first + k, (s, plane(k), d))
             hid_all[t] = hid_pair[...]
+            scatter_relay(0, gi_send, gi_recv, gi_relay, grad_res, grads_first)
             gi_low = grad_sum(0, grads_first)
             xs[0, t] = gi_low
             put(xs.at[0, t], ig_out, 0, 3)
@@ -1141,7 +1214,7 @@
 def run_layers(z, small, large):
     nt, nb, rows, brows = z.planes, z.blocks, z.rows, z.block_rows
     width, hidden = z.width, z.hidden
-    pairs = nb * (nb + 1) // 2
+    length = nb * brows
     V = pltpu.VMEM
     any_space = pl.BlockSpec(memory_space=pl.ANY)
     scratch = [
@@ -1156,7 +1229,7 @@
         V((2, nt, rows, width), bf16),
         V((2, nt, rows, width), bf16),
         V((2, nb, 3 * HD, brows), bf16),
-        V((2, nb, 3 * HD, brows), bf16),
+        V((2, 3 * HD, length), bf16),
         V((2, nb, HD, brows), bf16),
         V((2, z.cells, HD, brows), bf16),
         V((2, nt, rows, width), bf16),
@@ -1174,19 +1247,25 @@
         V((2, brows, 1), f32),
         V((2, brows, width), f32),
         V((2, brows, 1), f32),
-        V((2, brows, hidden), f32),
-        V((2, pairs, brows, brows), f32),
-        V((2, nb, z.prefix_pad, brows), f32),
+        V((brows, hidden), f32),
+        V((brows, hidden), f32),
+        V((2, length, length), bf16),
+        V((2, z.prefix_pad, length), f32),
+        V((2, nb, 1, brows), f32),
+        V((length, length), bf16),
+        V((z.prefix_pad, length), bf16),
+        V((length, HD), bf16),
+        V((length, HD), bf16),
+        V((length, HD), bf16),
         V((2, nb, HD, brows), f32),
-        V((2, nb, brows, HD), bf16),
+        V((2, length, HD), bf16),
         V((brows, width), bf16),
         V((brows, width), bf16),
         V((brows, width), f32),
         V((brows, width), f32),
         V((brows, width), f32),
-        V((nb, brows, HD), f32),
-        V((nb, brows, HD), f32),
         V((rows, width), bf16),
+        V((brows, width), bf16),
         V((rows, width), f32),
         V((2, 2, z.prefix_pad, HD), f32),
         V((2, z.prefix_pad, HD), f32),
@@ -1200,8 +1279,8 @@
         V((z.prefix_pad, z.inner), f32),
         V((z.prefix_pad, z.inner), f32),
         V((nt, z.prefix_pad, z.inner), f32),
-        pltpu.SemaphoreType.DMA((200,)),
-        pltpu.SemaphoreType.DMA((200,)),
+        pltpu.SemaphoreType.DMA((256,)),
+        pltpu.SemaphoreType.DMA((256,)),
         pltpu.SemaphoreType.DMA((20,)),
         pltpu.SemaphoreType.REGULAR,
     ]

time: 190 us -> 172 us (0.905)
  Pallas kernels: 186 us -> 168 us
    pallas_call x1, Pallas kernels: 183 us -> 164 us  [run_layers(): pl.pallas_call(partial(both_layers, z), out_shape=(jax.ShapeDtypeStruct((...]
where the time goes in v4:
time: 172 us; the launch traced here: 171 us
  Pallas kernels  168 us (98%)
  local copies, waits for them, and re-layouts  1.95 us (1%)
    pallas_call x1, Pallas kernels, run_layers(): pl.pallas_call(partial(both_layers, z), out_shape=(jax.ShapeDtypeStruct((...  164 us

profile of v4, /device:TPU:1, one launch (start us, length us, event | category | flops | bytes accessed | tf_op | source)
XLA Modules:
  0.0 170.6 jit_solution(7313466703125952099)
XLA Ops:
  0.6 0.0 copy-start
  0.7 0.0 copy-start.3
  0.7 164.3 %shard_map.251 = (bf16[2,1,2,64,1024]{4,3,2,1,0:T(8,128)(2,1)}, f32[4,16,512]{2,1,0:T(8,128)}) custom-call(s32[2]{0:T(128)} %valid_ref.1, bf16[1,1024]{1,0:T(2,128)(2,1)} %gain_one_in.1, bf16[1,1024]{1,0:T(2,128)(2,1)} %bias_one_in.1, bf16[1,3,256]{2,1,0:T(4,128)(2,1)} %triple_bias_in.1, bf16[1,1024]{1,0:T(2,128)(2,1)} %mixer_bias_in.1, ...), custom_call_target="tpu_custom_call" | custom-call | flops 7000000000 | bytes 16777216 | tf_op jit(solution)/shard_map/pallas_call | solution.py:1287
  165.0 0.0 copy-done
  165.0 0.0 copy-done.3
  165.0 0.0 copy-start.1
  165.0 1.0 copy-done.1
  166.1 0.0 copy-start.2
  166.1 0.9 copy-done.2
  167.0 3.4 %shard_map.252 = (bf16[1,2,64,1024]{3,2,1,0:T(8,128)(2,1)}, bf16[1,2,64,1024]{3,2,1,0:T(8,128)(2,1)}, bf16[10,2,256]{2,1,0:T(2,128)(2,1)}, f32[10,1024]{1,0:T(8,...) custom-call(bf16[2,1,2,64,1024]{4,3,2,1,0:T(8,128)(2,1)S(1)} %copy-done.1, ...), custom_call_target="tpu_custom_call" | custom-call | tf_op jit(solution)/shard_map/pallas_call | solution.py:1346
Async XLA Ops:
  0.6 164.4 %copy-start = (bf16[1024,512]{1,0:T(8,128)(2,1)S(1)}, bf16[1024,512]{1,0:T(8,128)(2,1)}, u32[]{:S(2)}) copy-start(bf16[1024,512]{1,0:T(8,128)(2,1)} %inner_in.3) | copy-start | bytes 3145732
  0.7 164.4 %copy-start.3 = (bf16[10,1024]{1,0:T(8,128)(2,1)S(1)}, bf16[10,1024]{1,0:T(8,128)(2,1)}, u32[]{:S(2)}) copy-start(bf16[10,1024]{1,0:T(8,128)(2,1)} %table_in.3) | copy-start | bytes 61444
  165.0 1.0 copy-start.1
  166.1 0.9 copy-start.2

commit v5 on v4

--- a/solution.py
+++ b/solution.py
@@ -404,6 +404,7 @@
         self.prefix_rows = prefix_rows
         self.cells = planes * blocks
         self.tile = 256
+        self.sends = 48
 
 
 def both_layers(
@@ -429,7 +430,6 @@
     inner_in,
     outer_in,
     rows_out,
-    parts_out,
     vec,
     tbias,
     triple_own,
@@ -489,7 +489,7 @@
     outer_w,
     hid_part,
     hid_recv,
-    hid_pair,
+    parts_low,
     hid_all,
     send_sem,
     recv_sem,
@@ -506,10 +506,15 @@
     sib = (1 - s, t, d)
     counts = dict(send=0, recv=0, local=0)
     pending = []
-
-    def claim(kind, number):
+    shared = {}
+
+    def claim(kind, number, name=None):
+        if name in shared:
+            return shared[name]
         first = counts[kind]
         counts[kind] += number
+        if name is not None:
+            shared[name] = first
         return first
 
     def rcopy(src, dst, ss, rs, device):
@@ -523,13 +528,20 @@
         )
 
     def push(src, dst, rs, device, when=None):
-        copy = rcopy(src, dst, claim("send", 1), rs, device)
+        if len(pending) >= z.sends:
+            sent(*pending[len(pending) - z.sends])
+        copy = rcopy(src, dst, len(pending) % z.sends, rs, device)
         if when is None:
             copy.start()
-            pending.append((copy, None))
         else:
             pl.when(when)(copy.start)
-            pending.append((copy, when))
+        pending.append((copy, when))
+
+    def sent(copy, when):
+        if when is None:
+            copy.wait_send()
+        else:
+            pl.when(when)(copy.wait_send)
 
     def arrived(dst, rs, when=None):
         copy = rcopy(dst, dst, 0, rs, sib)
@@ -556,6 +568,14 @@
 
     def near(k):
         return jnp.logical_not(far(k))
+
+    def keep(index, value):
+        high = value.astype(bf16)
+        low = (value - high.astype(f32)).astype(bf16)
+        at, columns = index // 2 * z.prefix_pad, slice(index % 2 * z.inner, (index % 2 + 1) * z.inner)
+        parts_low[at : at + z.prefix_pad, columns] = high
+        at += 2 * z.prefix_pad
+        parts_low[at : at + z.prefix_pad, columns] = low
 
     def plane(k):
         return lax.rem(t + k, nt)
@@ -599,13 +619,13 @@
     def parts_of(ref):
         return ref.at[pl.ds(0, half)], ref.at[pl.ds(half, half)]
 
-    def spread(src, buf, layer):
-        first = claim("recv", nt + 2)
+    def spread(src, buf, layer, when=True):
+        first = claim("recv", nt + 2, "rows" if buf is xs else "grads")
         for i, (one, goal) in enumerate(zip(parts_of(src), parts_of(buf.at[layer, t]))):
-            push(one, goal, first + (2, nt)[i], (s, across, d), outer)
-        push(src, buf.at[layer, t], first + 2, (s, across, d), inner)
+            push(one, goal, first + (2, nt)[i], (s, across, d), outer & when)
+        push(src, buf.at[layer, t], first + 2, (s, across, d), inner & when)
         for k in (1, 3):
-            push(src, buf.at[layer, t], first + k, (s, plane(k), d), near(k))
+            push(src, buf.at[layer, t], first + k, (s, plane(k), d), near(k) & when)
         return first
 
     def spread_relay(buf, layer, first):
@@ -624,7 +644,7 @@
 
     x_first = [None, None]
     gy_first = [None, None]
-    x_first[0] = spread(x_in.at[s], xs, 0)
+    x_first[0] = spread(x_in.at[s], xs, 0, s == 0)
 
     for index, ref in enumerate(
         (gain_one_in, bias_one_in, mixer_bias_in, gain_two_in, bias_two_in, reduce_bias_in, expand_bias_in)
@@ -642,9 +662,9 @@
     push(vec.at[s], vec.at[s], small, sib)
     push(tbias.at[s], tbias.at[s], small + 1, sib)
 
-    mix_first = [claim("recv", nt), claim("recv", nt)]
-    mix_second = [claim("recv", nt * nb), claim("recv", nt * nb)]
-    mix_third = [claim("recv", 1), claim("recv", 1)]
+    mix_first = claim("recv", nt)
+    mix_second = claim("recv", nt * nb)
+    mix_third = claim("recv", 1)
 
     def piece(layer, p, q):
         return wm.at[layer, pl.ds(pl.multiple_of((p * nb + q) * (z.local_width // nb), 64), z.local_width // nb)]
@@ -655,7 +675,7 @@
             push(
                 mixer_in.at[pl.ds(pl.multiple_of(d * part, 64), part)],
                 piece(layer, t, d),
-                mix_first[layer] + k,
+                mix_first + k,
                 (s, plane(k), d),
                 s == layer,
             )
@@ -663,12 +683,12 @@
     def mix_two(layer):
         for k in range(1, nt):
             source = plane(nt - k)
-            arrived(piece(layer, source, d), mix_first[layer] + k, s == layer)
+            arrived(piece(layer, source, d), mix_first + k, s == layer)
             for q in range(1, nb):
                 push(
                     piece(layer, source, d),
                     piece(layer, source, d),
-                    mix_second[layer] + k * nb + q,
+                    mix_second + k * nb + q,
                     (s, t, block(q)),
                     s == layer,
                 )
@@ -678,10 +698,10 @@
             for q in range(1, nb):
                 arrived(
                     piece(layer, plane(nt - k), block(nb - q)),
-                    mix_second[layer] + k * nb + q,
+                    mix_second + k * nb + q,
                     s == layer,
                 )
-        push(wm.at[layer], wm.at[layer], mix_third[layer], sib, s == layer)
+        push(wm.at[layer], wm.at[layer], mix_third, sib, s == layer)
 
     mix_one(0)
 
@@ -697,13 +717,13 @@
     inner_act = jnp.tanh(
         dot_nn(table_pad[...].astype(bf16), inner_w[...]) + inner_bias_in[...].reshape(1, z.inner).astype(f32)
     )
-    parts_out[0] = inner_act
+    keep(0, inner_act)
     load_outer.wait()
     for c in range(2):
         outer_w[:, c * z.local_width : (c + 1) * z.local_width] = outer_raw[:, c, :]
     outer_shift = jnp.concatenate([outer_bias_in[0, 0:1, :], outer_bias_in[0, 1:2, :]], axis=1)
     prefix = (dot_nn(inner_act.astype(bf16), outer_w[...]) + outer_shift.astype(f32)).astype(bf16)
-    parts_out[1] = prefix.astype(f32)
+    keep(1, prefix.astype(f32))
     for c in range(2):
         for j in range(nb):
             at = c * z.local_width + j * HD
@@ -766,7 +786,7 @@
         return ref.at[:, pl.ds(pl.multiple_of(b * brows, brows), brows)]
 
     def project(layer):
-        first = claim("recv", nb)
+        first = claim("recv", nb, "project")
         for k in range(1, nb + 1):
             head = block(k)
             part = dot_nt(wq[layer, head], normed[...])
@@ -780,7 +800,7 @@
         return first
 
     def attend(layer, first):
-        out_first = claim("recv", cells)
+        out_first = claim("recv", cells, "attend")
         pre_keys = pre[layer, 0, d]
         pre_values = pre[layer, 1, d].T
         prefix_row = lax.broadcasted_iota(jnp.int32, (z.prefix_pad, brows), 0)
@@ -846,22 +866,24 @@
 
     def mixer_rows(layer, first):
         att_relay(layer, first)
-        for cell in range(cells):
-            seen = inner & (across == cell // nb)
-            arrived(att.at[layer, cell], first + cell, (me != cell) & jnp.logical_not(seen))
         if layer == 0:
             mix_three(0)
-        arrived(wm.at[layer], mix_third[layer], s != layer)
-        for p in range(nt):
-            joined = att[layer, p * nb : (p + 1) * nb].reshape(nb * HD, brows)
-            wide[:, p * nb * HD : (p + 1) * nb * HD] = joined.T
-
-        def some(at):
-            x = xs[layer, :, :, pl.ds(at, tile)].reshape(brows, tile).astype(f32)
-            shift = vec[layer, 2:3, pl.ds(at, tile)]
-            resid[:, pl.ds(at, tile)] = dot_nn(wide[...], wm[layer, :, pl.ds(at, tile)]) + x + shift
-
-        tiles(z.width, some)
+        for at in range(0, z.width, tile):
+            at = slice(at, at + tile)
+            resid[:, at] = xs[layer, :, :, at].reshape(brows, tile).astype(f32) + vec[layer, 2:3, at]
+        arrived(wm.at[layer], mix_third, s != layer)
+        for p, seen in ((t, None), (beside, None), (across, inner), (nt - 1 - t, None)):
+            for j in range(nb):
+                cell = p * nb + j
+                if seen is None:
+                    arrived(att.at[layer, cell], first + cell, me != cell)
+                else:
+                    arrived(att.at[layer, cell], first + cell, jnp.logical_not(seen))
+            joined = att[layer, pl.ds(p * nb, nb)].reshape(nb * HD, brows).T
+            some_rows = pl.ds(pl.multiple_of(p * z.local_width, z.local_width), z.local_width)
+            for at in range(0, z.width, tile):
+                at = slice(at, at + tile)
+                resid[:, at] += dot_nn(joined, wm[layer, some_rows, at])
 
     def grad_active():
         def some(at):
@@ -896,7 +918,7 @@
         return scatter(layer, y_send, y_recv, y_relay)
 
     def scatter(layer, out, back, relay):
-        first = claim("recv", nt + 3)
+        first = claim("recv", nt + 3, "output" if out is y_send else "input")
         for i, (one, goal) in enumerate(zip(parts_of(out.at[layer, nt - 1 - t]), parts_of(relay.at[layer]))):
             push(one, goal, first + nt + i, (s, beside, d), outer)
         for k in (2, 1, 3):
@@ -945,17 +967,28 @@
 
     own_weights = [load_mixer, load_expand, load_reduce]
     feed_recv = claim("recv", 2)
-    y_base = []
     out_first = None
     for layer in range(2):
         if layer == 0:
             load_x.wait()
+
+            @pl.when(s == 1)
+            def _():
+                pl.semaphore_wait(phase_sem, 1)
+
+            spread(x_in.at[s], xs, 0, s == 1)
 
         norm_one(layer, t)
         spread_relay(xs, layer, x_first[layer])
         for k in (2, 1, 3):
             spread_wait(xs, layer, x_first[layer], k)
             norm_one(layer, plane(nt - k))
+            if layer == 0 and k == 3:
+
+                @pl.when(s == 0)
+                def _():
+                    pl.semaphore_signal(phase_sem, inc=1, device_id=sib, device_id_type=MESH)
+
         if layer == 0:
             arrived(wq.at[0], wq_first, s == 1)
         else:
@@ -974,16 +1007,18 @@
         if layer == 0:
             for copy in own_weights:
                 copy.wait()
-            arrived(we.at[1 - s], feed_recv)
-            arrived(wr.at[1 - s], feed_recv + 1)
         if layer == 1:
+            arrived(we.at[1], feed_recv, s == 0)
+            arrived(wr.at[1], feed_recv + 1, s == 0)
             spread_relay(gys, 1, gy_first[1])
             for k in range(1, nt):
                 spread_wait(gys, 1, gy_first[1], k)
             grad_active()
         mixer_rows(layer, out_first)
         norm_two(layer)
-        y_base.append(None)
+        if layer == 0:
+            arrived(we.at[0], feed_recv, s == 1)
+            arrived(wr.at[0], feed_recv + 1, s == 1)
         feed_first(layer, wide if layer == 0 else active_last)
         if layer == 0:
             y_first = feed_second(layer, wide)
@@ -1019,8 +1054,8 @@
         lax.fori_loop(0, brows // step, pull, 0, unroll=True)
 
     def grad_to_heads(layer):
-        first = claim("recv", cells)
-        relay_sem = claim("recv", 2)
+        first = claim("recv", cells, "heads")
+        relay_sem = claim("recv", 2, "heads beside")
         pairs = [pl.ds(0, nb // 2), pl.ds(nb // 2, nb - nb // 2)]
 
         def share(p, index):
@@ -1071,7 +1106,7 @@
         for cell in range(cells):
             seen = outer & (t + cell // nb == nt - 1)
             arrived(gh.at[layer, cell], first + cell, (me != cell) & jnp.logical_not(seen))
-        out_first = claim("recv", nb)
+        out_first = claim("recv", nb, "mixed")
         pre_values = pre[layer, 1, d]
         pre_keys = pre[layer, 0, d].T
         for b in reversed(range(nb)):
@@ -1154,13 +1189,14 @@
         if layer == 0:
             sib_sem = claim("recv", 1)
             push(pg.at[1 - s], pg_recv, sib_sem, sib)
+        grads_first = grad_rows(layer, rows_first)
+        if layer == 0:
             arrived(pg_recv, sib_sem)
             pg_sum[...] = pg[s] + pg_recv[...]
             all_first = claim("recv", nb)
             for k in range(1, nb):
                 push(pg_sum, pg_all.at[d], all_first + k, (s, t, block(k)))
             pg_all[d] = pg_sum[...]
-        grads_first = grad_rows(layer, rows_first)
         if layer == 1:
             scatter_relay(1, gi_send, gi_recv, gi_relay, grad_res, grads_first)
             y_last[...] = output_sum(1, y_first, gi_own[...])
@@ -1169,46 +1205,40 @@
             gy_first[0] = spread(gys.at[0, t], gys, 0)
             put(gys.at[0, t], ig_out, 1, 2)
         else:
+            scatter_relay(0, gi_send, gi_recv, gi_relay, grad_res, grads_first)
             for k in range(1, nb):
                 arrived(pg_all.at[block(nb - k)], all_first + k)
-            for c in range(2):
-                joined = jnp.concatenate([pg_all[j, c] for j in range(nb)], axis=1)
-                parts_out[2, :, c * z.local_width : (c + 1) * z.local_width] = joined
+            keep(2, jnp.concatenate([pg_all[j, c] for c in range(2) for j in range(nb)], axis=1))
             part = jnp.zeros((z.prefix_pad, z.inner), f32)
             for j in range(nb):
                 for c in range(2):
                     at = c * z.local_width + j * HD
                     part = part + dot_split(pg_all[j, c], outer_w[:, at : at + HD], dot_nt)
-            hid_part[...] = part
-            hid_sem = claim("recv", 1)
-            push(hid_part, hid_recv, hid_sem, sib)
-            arrived(hid_recv, hid_sem)
-            hid_pair[...] = hid_part[...] + hid_recv[...]
+            hid_all[t] = part
             hid_first = claim("recv", nt)
             for k in range(1, nt):
-                push(hid_pair, hid_all.at[t], hid_first + k, (s, plane(k), d))
-            hid_all[t] = hid_pair[...]
-            scatter_relay(0, gi_send, gi_recv, gi_relay, grad_res, grads_first)
-            gi_low = grad_sum(0, grads_first)
-            xs[0, t] = gi_low
+                push(hid_all.at[t], hid_all.at[t], hid_first + k, (s, plane(k), d))
+            xs[0, t] = grad_sum(0, grads_first)
             put(xs.at[0, t], ig_out, 0, 3)
             for k in range(1, nt):
                 arrived(hid_all.at[plane(nt - k)], hid_first + k)
             part = hid_all[0]
             for p in range(1, nt):
                 part = part + hid_all[p]
-            parts_out[3] = part
+            hid_part[...] = part
+            hid_sem = claim("recv", 1)
+            push(hid_part, hid_recv, hid_sem, sib)
+            arrived(hid_recv, hid_sem)
+            keep(3, hid_part[...] + hid_recv[...])
+            load_parts = lcopy(parts_low, rows_out.at[2, 0, 0])
 
     for index, (out, layer) in enumerate(((lo_out, 0), (lo_out, 1), (ig_out, 1), (ig_out, 0))):
         arrived(out.at[0, 1 - s], out_sem + index, s == layer)
-    for copy, when in pending:
-        if when is None:
-            copy.wait_send()
-        else:
-            pl.when(when)(copy.wait_send)
+    for copy, when in pending[-z.sends :]:
+        sent(copy, when)
     for copy, when in out_loads:
         pl.when(when)(copy.wait)
-    z.counts = counts
+    load_parts.wait()
 
 
 def run_layers(z, small, large):
@@ -1277,23 +1307,22 @@
         V((z.inner, 2 * z.local_width), bf16),
         V((z.prefix_pad, z.inner), f32),
         V((z.prefix_pad, z.inner), f32),
-        V((z.prefix_pad, z.inner), f32),
+        V((rows, width), bf16),
         V((nt, z.prefix_pad, z.inner), f32),
-        pltpu.SemaphoreType.DMA((256,)),
-        pltpu.SemaphoreType.DMA((256,)),
-        pltpu.SemaphoreType.DMA((20,)),
+        pltpu.SemaphoreType.DMA((z.sends,)),
+        pltpu.SemaphoreType.DMA((109,)),
+        pltpu.SemaphoreType.DMA((13,)),
         pltpu.SemaphoreType.REGULAR,
     ]
     return pl.pallas_call(
         partial(both_layers, z),
         out_shape=(
-            jax.ShapeDtypeStruct((2, 1, 2, rows, width), bf16),
-            jax.ShapeDtypeStruct((4, z.prefix_pad, z.inner), f32),
+            jax.ShapeDtypeStruct((3, 1, 2, rows, width), bf16),
         ),
         in_specs=[pl.BlockSpec(memory_space=pltpu.SMEM)]
         + [pl.BlockSpec(memory_space=pltpu.VMEM)] * (len(small) - 1)
         + [any_space] * len(large),
-        out_specs=(any_space, pl.BlockSpec(memory_space=pltpu.VMEM)),
+        out_specs=(any_space,),
         scratch_shapes=scratch,
         compiler_params=pltpu.CompilerParams(
             collective_id=0, has_side_effects=True, vmem_limit_bytes=60 * 2**20
@@ -1305,41 +1334,59 @@
 
 
 def prefix_end(
-    z, rows_in, parts_in, table_in, inner_in,
+    z, rows_in, table_in, inner_in,
     lo_out, ig_out, states_out, table_out, inner_out, inner_bias_out, outer_out, outer_bias_out,
-    table_pad, sems,
+    table_pad, parts, inner_full, outer_full, sems,
 ):
-    copies = [
-        pltpu.make_async_copy(rows_in.at[0], lo_out, sems.at[0]),
-        pltpu.make_async_copy(rows_in.at[1], ig_out, sems.at[1]),
-    ]
-    for copy in copies:
-        copy.start()
+    copies = []
+
+    def start(src, dst):
+        copies.append(pltpu.make_async_copy(src, dst, sems.at[len(copies)]))
+        copies[-1].start()
+
+    start(rows_in.at[2, 0, 0], parts)
+    start(rows_in.at[0], lo_out)
+    start(rows_in.at[1], ig_out)
     count, width = z.prefix_rows, z.local_width
-    act = parts_in[0]
-    inner_grad = parts_in[3] * (1.0 - act * act)
-    inner_bias_out[...] = jnp.sum(inner_grad, axis=0, keepdims=True)
     table_pad[...] = jnp.zeros_like(table_pad)
     table_pad[0:count, :] = table_in[...].astype(f32)
+    table_turned = table_pad[...].T.astype(bf16)
+    copies[0].wait()
+
+    def halves(index):
+        at, columns = index // 2 * z.prefix_pad, slice(index % 2 * z.inner, (index % 2 + 1) * z.inner)
+        high = parts[at : at + z.prefix_pad, columns]
+        at += 2 * z.prefix_pad
+        return high, parts[at : at + z.prefix_pad, columns]
+
+    act = halves(0)[0].astype(f32) + halves(0)[1].astype(f32)
+    hidden = halves(3)[0].astype(f32) + halves(3)[1].astype(f32)
+    inner_grad = hidden * (1.0 - act * act)
     high = inner_grad.astype(bf16)
     low = (inner_grad - high.astype(f32)).astype(bf16)
-    table_turned = table_pad[...].T.astype(bf16)
-    inner_out[...] = dot_nn(table_turned, high) + dot_nn(table_turned, low)
-    table_out[...] = (dot_nt(high, inner_in[...]) + dot_nt(low, inner_in[...]))[0:count]
+    some = z.width // 2
+    for i in range(2):
+        at = slice(i * some, (i + 1) * some)
+        inner_full[at] = dot_nn(table_turned[at], high) + dot_nn(table_turned[at], low)
+        start(inner_full.at[at], inner_out.at[at])
     act_turned = act.T.astype(bf16)
+    total = halves(2)
     for c in range(2):
         at = slice(c * width, (c + 1) * width)
-        states_out[:, c, :] = parts_in[1, 0:count, at].astype(bf16)
-        total = parts_in[2, :, at]
-        high = total.astype(bf16)
-        low = (total - high.astype(f32)).astype(bf16)
-        outer_out[:, c, :] = dot_nn(act_turned, high) + dot_nn(act_turned, low)
-        outer_bias_out[0, c : c + 1, :] = jnp.sum(total, axis=0, keepdims=True)
-    for copy in copies:
+        outer_full[:, c, :] = dot_nn(act_turned, total[0][:, at]) + dot_nn(act_turned, total[1][:, at])
+    start(outer_full, outer_out)
+    whole = total[0].astype(f32) + total[1].astype(f32)
+    for c in range(2):
+        at = slice(c * width, (c + 1) * width)
+        states_out[:, c, :] = halves(1)[0][0:count, at]
+        outer_bias_out[0, c : c + 1, :] = jnp.sum(whole[:, at], axis=0, keepdims=True)
+    inner_bias_out[...] = jnp.sum(inner_grad, axis=0, keepdims=True)
+    table_out[...] = (dot_nt(high, inner_in[...]) + dot_nt(low, inner_in[...]))[0:count]
+    for copy in copies[1:]:
         copy.wait()
 
 
-def finish(z, both_rows, parts, table, inner_weight):
+def finish(z, both_rows, table, inner_weight):
     any_space = pl.BlockSpec(memory_space=pl.ANY)
     whole = pl.BlockSpec(memory_space=pltpu.VMEM)
     rows = jax.ShapeDtypeStruct(both_rows.shape[1:], bf16)
@@ -1355,11 +1402,17 @@
             jax.ShapeDtypeStruct((z.inner, 2, z.local_width), f32),
             jax.ShapeDtypeStruct((1, 2, z.local_width), f32),
         ),
-        in_specs=[any_space] + [whole] * 3,
-        out_specs=(any_space,) * 2 + (whole,) * 6,
-        scratch_shapes=[pltpu.VMEM((z.prefix_pad, z.width), f32), pltpu.SemaphoreType.DMA((2,))],
+        in_specs=[any_space] + [whole] * 2,
+        out_specs=(any_space,) * 2 + (whole,) * 2 + (any_space, whole, any_space, whole),
+        scratch_shapes=[
+            pltpu.VMEM((z.prefix_pad, z.width), f32),
+            pltpu.VMEM(both_rows.shape[3:], bf16),
+            pltpu.VMEM((z.width, z.inner), f32),
+            pltpu.VMEM((z.inner, 2, z.local_width), f32),
+            pltpu.SemaphoreType.DMA((6,)),
+        ],
         compiler_params=pltpu.CompilerParams(vmem_limit_bytes=32 * 2**20),
-    )(both_rows, parts, table, inner_weight)
+    )(both_rows, table, inner_weight)
 
 
 def head_a_device(
@@ -1491,6 +1544,9 @@
             and triple_weight.shape[3] % 256 == 0
             and width % 256 == 0
             and args[11].shape[2] == width
+            and args[16].shape[1] * 2 == width
+            and args[15].shape[0] <= 16
+            and share_rows == 64
         )
         return head_a_device(*args) if fits else shards(*args)
 

time: 172 us -> 164 us (0.953)
  Pallas kernels: 168 us -> 162 us
    pallas_call x1, Pallas kernels: 164 us -> 158 us  [run_layers(): pl.pallas_call(partial(both_layers, z), out_shape=(jax.ShapeDtypeStruct((...]
where the time goes in v5:
time: 164 us
  Pallas kernels  162 us (99%)
    pallas_call x1, Pallas kernels, run_layers(): pl.pallas_call(partial(both_layers, z), out_shape=(jax.ShapeDtypeStruct((...  158 us

profile of v5, /device:TPU:1, one launch (start us, length us, event | category | flops | bytes accessed | tf_op | source)
XLA Modules:
  0.0 163.6 jit_solution(15575623866322764305)
XLA Ops:
  0.6 0.0 copy-start
  0.7 0.0 copy-start.2
  0.7 158.5 %shard_map.251.rows_in = bf16[3,1,2,64,1024]{4,3,2,1,0:T(8,128)(2,1)} custom-call(s32[2]{0:T(128)} %valid_ref.1, bf16[1,1024]{1,0:T(2,128)(2,1)} %gain_one_in.1, bf16[1,1024]{1,0:T(2,128)(2,1)} %bias_one_in.1, bf16[1,3,256]{2,1,0:T(4,128)(2,1)} %triple_bias_in.1, bf16[1,1024]{1,0:T(2,128)(2,1)} %mixer_bias_in.1, bf16[1,1024]{1,0:T(2,128)(2,1)} %gain_two_in.1, ...), custom_call_target="tpu_custom_call" | custom-call | flops 7000000000 | bytes 16777216 | tf_op jit(solution)/shard_map/pallas_call | solution.py:1317
  159.2 0.0 copy-done
  159.2 0.0 copy-done.2
  159.2 0.0 copy-start.1
  159.2 1.1 copy-done.1
  160.3 3.1 %shard_map.252 = (bf16[1,2,64,1024]{3,2,1,0:T(8,128)(2,1)}, bf16[1,2,64,1024]{3,2,1,0:T(8,128)(2,1)}, bf16[10,2,256]{2,1,0:T(2,128)(2,1)}, f32[10,1024]{1,0:T(8,...) custom-call(bf16[3,1,2,64,1024]{4,3,2,1,0:T(8,128)(2,1)S(1)} %copy-done.1, ...), custom_call_target="tpu_custom_call" | custom-call | tf_op jit(solution)/shard_map/pallas_call | solution.py:1393
Async XLA Ops:
  0.6 158.5 %copy-start = (bf16[1024,512]{1,0:T(8,128)(2,1)S(1)}, bf16[1024,512]{1,0:T(8,128)(2,1)}, u32[]{:S(2)}) copy-start(bf16[1024,512]{1,0:T(8,128)(2,1)} %inner_in.3) | copy-start | bytes 3145732
  0.7 158.5 %copy-start.2 = (bf16[10,1024]{1,0:T(8,128)(2,1)S(1)}, bf16[10,1024]{1,0:T(8,128)(2,1)}, u32[]{:S(2)}) copy-start(bf16[10,1024]{1,0:T(8,128)(2,1)} %table_in.3) | copy-start | bytes 61444
  159.2 1.1 copy-start.1

commit v6 on v5

--- a/solution.py
+++ b/solution.py
@@ -494,7 +494,6 @@
     send_sem,
     recv_sem,
     local_sem,
-    phase_sem,
 ):
     lo_out, ig_out = rows_out.at[0], rows_out.at[1]
     s = lax.axis_index("section")
@@ -644,24 +643,6 @@
 
     x_first = [None, None]
     gy_first = [None, None]
-    x_first[0] = spread(x_in.at[s], xs, 0, s == 0)
-
-    for index, ref in enumerate(
-        (gain_one_in, bias_one_in, mixer_bias_in, gain_two_in, bias_two_in, reduce_bias_in, expand_bias_in)
-    ):
-        vec[s, index : index + 1, :] = ref[...].astype(f32)
-    for c in range(3):
-        shift = jnp.broadcast_to(triple_bias_in[0, c : c + 1, :].astype(f32), (128, z.local_width)).T
-        for j in range(nb):
-            tbias[s, j, c * HD : (c + 1) * HD, :] = shift[j * HD : (j + 1) * HD].astype(bf16)
-    table_pad[...] = jnp.zeros_like(table_pad)
-    table_pad[0 : z.prefix_rows, :] = table_in[...].astype(f32)
-
-
-    small = claim("recv", 3)
-    push(vec.at[s], vec.at[s], small, sib)
-    push(tbias.at[s], tbias.at[s], small + 1, sib)
-
     mix_first = claim("recv", nt)
     mix_second = claim("recv", nt * nb)
     mix_third = claim("recv", 1)
@@ -704,6 +685,24 @@
         push(wm.at[layer], wm.at[layer], mix_third, sib, s == layer)
 
     mix_one(0)
+
+    x_first[0] = spread(x_in.at[s], xs, 0, s == 1)
+
+    for index, ref in enumerate(
+        (gain_one_in, bias_one_in, mixer_bias_in, gain_two_in, bias_two_in, reduce_bias_in, expand_bias_in)
+    ):
+        vec[s, index : index + 1, :] = ref[...].astype(f32)
+    for c in range(3):
+        shift = jnp.broadcast_to(triple_bias_in[0, c : c + 1, :].astype(f32), (128, z.local_width)).T
+        for j in range(nb):
+            tbias[s, j, c * HD : (c + 1) * HD, :] = shift[j * HD : (j + 1) * HD].astype(bf16)
+    table_pad[...] = jnp.zeros_like(table_pad)
+    table_pad[0 : z.prefix_rows, :] = table_in[...].astype(f32)
+
+
+    small = claim("recv", 3)
+    push(vec.at[s], vec.at[s], small, sib)
+    push(tbias.at[s], tbias.at[s], small + 1, sib)
 
     load_triple.wait()
     for c in range(3):
@@ -866,8 +865,6 @@
 
     def mixer_rows(layer, first):
         att_relay(layer, first)
-        if layer == 0:
-            mix_three(0)
         for at in range(0, z.width, tile):
             at = slice(at, at + tile)
             resid[:, at] = xs[layer, :, :, at].reshape(brows, tile).astype(f32) + vec[layer, 2:3, at]
@@ -972,23 +969,14 @@
         if layer == 0:
             load_x.wait()
 
-            @pl.when(s == 1)
-            def _():
-                pl.semaphore_wait(phase_sem, 1)
-
-            spread(x_in.at[s], xs, 0, s == 1)
+            spread(x_in.at[s], xs, 0, s == 0)
+            mix_two(0)
 
         norm_one(layer, t)
         spread_relay(xs, layer, x_first[layer])
         for k in (2, 1, 3):
             spread_wait(xs, layer, x_first[layer], k)
             norm_one(layer, plane(nt - k))
-            if layer == 0 and k == 3:
-
-                @pl.when(s == 0)
-                def _():
-                    pl.semaphore_signal(phase_sem, inc=1, device_id=sib, device_id_type=MESH)
-
         if layer == 0:
             arrived(wq.at[0], wq_first, s == 1)
         else:
@@ -997,7 +985,6 @@
         if layer == 0:
             push(expand_in, we.at[s], feed_recv, sib)
             push(reduce_in, wr.at[s], feed_recv + 1, sib)
-            mix_two(0)
             mix_one(1)
         else:
             mix_three(1)
@@ -1007,6 +994,7 @@
         if layer == 0:
             for copy in own_weights:
                 copy.wait()
+            mix_three(0)
         if layer == 1:
             arrived(we.at[1], feed_recv, s == 0)
             arrived(wr.at[1], feed_recv + 1, s == 0)
@@ -1103,14 +1091,15 @@
             values_n[here] = qkv[layer, 2 * HD : 3 * HD, here].T
             queries = (qkv[layer, 0:HD, here].astype(f32) * HD ** (-0.5)).astype(bf16)
             queries_n[here] = queries.T
-        for cell in range(cells):
-            seen = outer & (t + cell // nb == nt - 1)
-            arrived(gh.at[layer, cell], first + cell, (me != cell) & jnp.logical_not(seen))
         out_first = claim("recv", nb, "mixed")
         pre_values = pre[layer, 1, d]
         pre_keys = pre[layer, 0, d].T
         for b in reversed(range(nb)):
             here = slice(b * brows, (b + 1) * brows)
+            for p in range(nt):
+                cell = p * nb + b
+                heard = (me != cell) & jnp.logical_not(outer & (t + p == nt - 1))
+                arrived(gh.at[layer, cell], first + cell, heard)
             grad = gh[layer, b].astype(f32)
             for p in range(1, nt):
                 grad = grad + gh[layer, p * nb + b].astype(f32)
@@ -1312,7 +1301,6 @@
         pltpu.SemaphoreType.DMA((z.sends,)),
         pltpu.SemaphoreType.DMA((109,)),
         pltpu.SemaphoreType.DMA((13,)),
-        pltpu.SemaphoreType.REGULAR,
     ]
     return pl.pallas_call(
         partial(both_layers, z),

time: 164 us -> 162 us (0.988)
  Pallas kernels: 162 us -> 160 us
where the time goes in v6:
time: 162 us
  Pallas kernels  160 us (99%)
    pallas_call x1, Pallas kernels, run_layers(): pl.pallas_call(partial(both_layers, z), out_shape=(jax.ShapeDtypeStruct((...  157 us

profile of v6, /device:TPU:1, one launch (start us, length us, event | category | flops | bytes accessed | tf_op | source)
XLA Modules:
  0.0 162.1 jit_solution(2058491886529122350)
XLA Ops:
  0.6 0.0 copy-start
  0.7 0.0 copy-start.2
  0.7 157.0 %shard_map.251.rows_in = bf16[3,1,2,64,1024]{4,3,2,1,0:T(8,128)(2,1)} custom-call(s32[2]{0:T(128)} %valid_ref.1, bf16[1,1024]{1,0:T(2,128)(2,1)} %gain_one_in.1, bf16[1,1024]{1,0:T(2,128)(2,1)} %bias_one_in.1, bf16[1,3,256]{2,1,0:T(4,128)(2,1)} %triple_bias_in.1, bf16[1,1024]{1,0:T(2,128)(2,1)} %mixer_bias_in.1, bf16[1,1024]{1,0:T(2,128)(2,1)} %gain_two_in.1, ...), custom_call_target="tpu_custom_call" | custom-call | flops 7000000000 | bytes 16777216 | tf_op jit(solution)/shard_map/pallas_call | solution.py:1305
  157.7 0.0 copy-done
  157.7 0.0 copy-done.2
  157.7 0.0 copy-start.1
  157.7 1.1 copy-done.1
  158.8 3.1 %shard_map.252 = (bf16[1,2,64,1024]{3,2,1,0:T(8,128)(2,1)}, bf16[1,2,64,1024]{3,2,1,0:T(8,128)(2,1)}, bf16[10,2,256]{2,1,0:T(2,128)(2,1)}, f32[10,1024]{1,0:T(8,...) custom-call(bf16[3,1,2,64,1024]{4,3,2,1,0:T(8,128)(2,1)S(1)} %copy-done.1, ...), custom_call_target="tpu_custom_call" | custom-call | tf_op jit(solution)/shard_map/pallas_call | solution.py:1381
Async XLA Ops:
  0.6 157.0 %copy-start = (bf16[1024,512]{1,0:T(8,128)(2,1)S(1)}, bf16[1024,512]{1,0:T(8,128)(2,1)}, u32[]{:S(2)}) copy-start(bf16[1024,512]{1,0:T(8,128)(2,1)} %inner_in.3) | copy-start | bytes 3145732
  0.7 157.0 %copy-start.2 = (bf16[10,1024]{1,0:T(8,128)(2,1)S(1)}, bf16[10,1024]{1,0:T(8,128)(2,1)}, u32[]{:S(2)}) copy-start(bf16[10,1024]{1,0:T(8,128)(2,1)} %table_in.3) | copy-start | bytes 61444
  157.7 1.1 copy-start.1

commit v7 on v6

--- a/solution.py
+++ b/solution.py
@@ -985,7 +985,6 @@
         if layer == 0:
             push(expand_in, we.at[s], feed_recv, sib)
             push(reduce_in, wr.at[s], feed_recv + 1, sib)
-            mix_one(1)
         else:
             mix_three(1)
             load_gy.wait()
@@ -995,6 +994,7 @@
             for copy in own_weights:
                 copy.wait()
             mix_three(0)
+            mix_one(1)
         if layer == 1:
             arrived(we.at[1], feed_recv, s == 0)
             arrived(wr.at[1], feed_recv + 1, s == 0)

time: 162 us -> 160 us (0.988)
  Pallas kernels: 160 us -> 158 us
    pallas_call x1, Pallas kernels: 157 us -> 155 us  [run_layers(): pl.pallas_call(partial(both_layers, z), out_shape=(jax.ShapeDtypeStruct((...]
where the time goes in v7:
time: 160 us
  Pallas kernels  158 us (99%)
    pallas_call x1, Pallas kernels, run_layers(): pl.pallas_call(partial(both_layers, z), out_shape=(jax.ShapeDtypeStruct((...  155 us

profile of v7, /device:TPU:1, one launch (start us, length us, event | category | flops | bytes accessed | tf_op | source)
XLA Modules:
  0.0 159.8 jit_solution(17859044426496136692)
XLA Ops:
  0.6 0.0 copy-start
  0.7 0.0 copy-start.2
  0.7 154.7 %shard_map.251.rows_in = bf16[3,1,2,64,1024]{4,3,2,1,0:T(8,128)(2,1)} custom-call(s32[2]{0:T(128)} %valid_ref.1, bf16[1,1024]{1,0:T(2,128)(2,1)} %gain_one_in.1, bf16[1,1024]{1,0:T(2,128)(2,1)} %bias_one_in.1, bf16[1,3,256]{2,1,0:T(4,128)(2,1)} %triple_bias_in.1, bf16[1,1024]{1,0:T(2,128)(2,1)} %mixer_bias_in.1, bf16[1,1024]{1,0:T(2,128)(2,1)} %gain_two_in.1, ...), custom_call_target="tpu_custom_call" | custom-call | flops 7000000000 | bytes 16777216 | tf_op jit(solution)/shard_map/pallas_call | solution.py:1305
  155.4 0.0 copy-done
  155.4 0.0 copy-done.2
  155.4 0.0 copy-start.1
  155.4 1.1 copy-done.1
  156.5 3.1 %shard_map.252 = (bf16[1,2,64,1024]{3,2,1,0:T(8,128)(2,1)}, bf16[1,2,64,1024]{3,2,1,0:T(8,128)(2,1)}, bf16[10,2,256]{2,1,0:T(2,128)(2,1)}, f32[10,1024]{1,0:T(8,...) custom-call(bf16[3,1,2,64,1024]{4,3,2,1,0:T(8,128)(2,1)S(1)} %copy-done.1, ...), custom_call_target="tpu_custom_call" | custom-call | tf_op jit(solution)/shard_map/pallas_call | solution.py:1381
Async XLA Ops:
  0.6 154.7 %copy-start = (bf16[1024,512]{1,0:T(8,128)(2,1)S(1)}, bf16[1024,512]{1,0:T(8,128)(2,1)}, u32[]{:S(2)}) copy-start(bf16[1024,512]{1,0:T(8,128)(2,1)} %inner_in.3) | copy-start | bytes 3145732
  0.7 154.7 %copy-start.2 = (bf16[10,1024]{1,0:T(8,128)(2,1)S(1)}, bf16[10,1024]{1,0:T(8,128)(2,1)}, u32[]{:S(2)}) copy-start(bf16[10,1024]{1,0:T(8,128)(2,1)} %table_in.3) | copy-start | bytes 61444
  155.4 1.1 copy-start.1
